TPU v7x, 128 devices: a whole 4x4x4 slice. The times are simulated.
128 devices in a mesh: ax: 16 (over z, y_lo, core), rad: 8 (over x, y_hi).
Axes of the slice: x: 4, y: 4 (y_hi: 2, y_lo: 2; y = y_hi * 2 + y_lo), z: 4, core: 2. Of those that a mesh axis runs over, the one named last changes fastest.
Arguments:
- velocity: float32 [3, 128, 512, 1024], P(None, 'ax', 'rad'), may hold values from -6 to 6
- viscosity: float32 [128, 512, 1024], P('ax', 'rad'), may hold values from 0.05 to 0.5
- inv_dx: float32 [128], P('ax'), may hold values from 0.5 to 2
- inv_dr: float32 [512], P('rad'), may hold values from 0.5 to 2
- inv_rt: float32 [512], P('rad'), may hold values from 0.5 to 2
- az_inverse: float32 [1024, 1024], replicated, may hold values from -0.5 to 2.5
- rad_inverse: float32 [512, 512], replicated, may hold values from -0.5 to 2.5
Outputs:
- velocity_next: float32 [3, 128, 512, 1024], P(None, 'ax', 'rad')
All inputs are finite; a program needn't handle non-finite values.
Results may differ from a plain program's by a relative error of at most 0.0003.
Values sent between devices are 32-bit elements; how exact they have to be, the bound alone decides.
No kernel may reach another device: no remote copies, remote signals or barrier semaphores. Data moves between devices by JAX's collectives and lax.ppermute only.
A program may use at most 256 MiB of HBM per device.

v0:
```python
import jax
import jax.numpy as jnp
from jax import lax
from jax.sharding import PartitionSpec as P

COEF = 0.25


def padded_2(block, sides, width):
    for axis, dim in sides:
        count = lax.axis_size(axis)
        forward = [(i, i + 1) for i in range(count - 1)]
        backward = [(target, source) for source, target in forward]
        low = lax.ppermute(
            lax.slice_in_dim(block, block.shape[dim] - width, None, axis=dim), axis, forward
        )
        high = lax.ppermute(lax.slice_in_dim(block, 0, width, axis=dim), axis, backward)
        block = jnp.concatenate([low, block, high], axis=dim)
    return block


def tendency(padded, inv_dx, inv_dr, inv_rt):
    planes = padded.shape[1] - 4
    radial = padded.shape[2] - 4

    def shifted(step_a, step_r):
        return padded[:, 2 + step_a : 2 + step_a + planes, 2 + step_r : 2 + step_r + radial, :]

    centre = shifted(0, 0)
    vel = centre[:3]
    visc = centre[3]
    metric_x = inv_dx[:, None, None]
    metric_r = inv_dr[None, :, None]
    metric_t = inv_rt[None, :, None]

    def parts(metric, plus_one, minus_one, plus_two, minus_two):
        deriv = (
            metric * (8.0 * (plus_one[:3] - minus_one[:3]) - (plus_two[:3] - minus_two[:3])) / 12.0
        )
        upper = 0.5 * (visc + plus_one[3]) * (plus_one[:3] - vel)
        lower = 0.5 * (visc + minus_one[3]) * (vel - minus_one[:3])
        return (deriv, metric * metric * (upper - lower))

    deriv_x, diff_x = parts(metric_x, shifted(1, 0), shifted(-1, 0), shifted(2, 0), shifted(-2, 0))
    deriv_r, diff_r = parts(metric_r, shifted(0, 1), shifted(0, -1), shifted(0, 2), shifted(0, -2))
    deriv_t, diff_t = parts(
        metric_t,
        jnp.roll(centre, -1, axis=3),
        jnp.roll(centre, 1, axis=3),
        jnp.roll(centre, -2, axis=3),
        jnp.roll(centre, 2, axis=3),
    )
    advect = vel[0] * deriv_x + vel[1] * deriv_t + vel[2] * deriv_r
    return vel + COEF * (diff_x + diff_t + diff_r - advect)


def local(velocity, viscosity, inv_dx, inv_dr, inv_rt, az_inverse, rad_inverse):
    fields = jnp.concatenate([velocity, viscosity[None]], axis=0)
    padded = padded_2(fields, (("ax", 1), ("rad", 2)), 2)
    rhs = tendency(padded, inv_dx, inv_dr, inv_rt)

    def radial(field):
        return jnp.einsum("rk,cakt->cart", rad_inverse, field, precision=lax.Precision.HIGHEST)

    solved = jnp.einsum("cars,ts->cart", rhs, az_inverse, precision=lax.Precision.HIGHEST)
    return lax.all_to_all(
        radial(lax.all_to_all(solved, "rad", split_axis=3, concat_axis=2, tiled=True)),
        "rad",
        split_axis=2,
        concat_axis=3,
        tiled=True,
    )


def solution(mesh):
    placed = (
        P(None, "ax", "rad", None),
        P("ax", "rad", None),
        P("ax"),
        P("rad"),
        P("rad"),
        P(),
        P(),
    )
    return jax.shard_map(
        local, mesh=mesh, in_specs=placed, out_specs=P(None, "ax", "rad", None), check_vma=False
    )
```

profile of v0, /device:TPU:96, one launch (start us, length us, event | category | flops | bytes accessed | tf_op | source)
XLA Modules:
  0.0 418.2 jit_solution(3006121644179621851)
XLA Ops:
  0.0 0.0 copy-start
  0.0 0.0 copy-start.7
  0.0 0.0 copy-start.1
  0.0 0.0 copy-start.2
  0.0 5.0 %fusion.75 = (f32[4,2,64,1024]{3,2,1,0:T(8,128)}, f32[4,2,64,1024]{3,2,1,0:T(8,128)}) fusion(f32[3,8,64,1024]{3,2,1,0:T(8,128)} %param.7, f32[1,8,64,1024]{3,2,1,0:T(8,128)} %bitcast.69), kind=kLoop, calls=%fused_computation.109 | loop fusion | flops 1048576 | bytes 12582912 | tf_op jit(solution)/shard_map/concatenate | solution.py:58
  5.1 2.9 collective-permute-start
  8.0 1.9 collective-permute-start.1
  9.9 0.0 copy-done.9
  9.9 0.0 copy-done.8
  9.9 0.6 mul.188
  10.5 0.0 copy-done.7
  10.5 0.6 mul.197
  11.1 0.0 copy-done.1
  11.1 0.0 copy-done.2
  11.1 0.4 fusion.89
  11.5 0.0 copy-start.6
  11.5 2.0 fusion.91
  13.5 5.1 %fusion.2 = f32[4,8,64,1022]{3,2,1,0:T(8,128)} fusion(f32[3,8,64,1024]{3,2,1,0:T(8,128)S(1)} %copy-done.1, f32[1,8,64,1024]{3,2,1,0:T(8,128)S(1)} %bitcast.72), kind=kLoop, calls=%fused_computation.22 | loop fusion | flops 2093056 | bytes 16760832 | tf_op jit(solution)/shard_map/concatenate | solution.py:58
  18.7 5.8 %fusion = (f32[4,8,64,1023]{3,2,1,0:T(8,128)S(1)}, f32[4,8,64,1023]{3,2,1,0:T(8,128)}) fusion(f32[3,8,64,1024]{3,2,1,0:T(8,128)S(1)} %copy-done.1, f32[1,8,64,1024]{3,2,1,0:T(8,128)S(1)} %bitcast.73), kind=kLoop, calls=%fused_computation.20 | loop fusion | flops 4190208 | bytes 25149440 | tf_op jit(solution)/shard_map/concatenate | solution.py:58
  24.4 0.0 copy-done.6
  24.4 2.1 fusion.83
  26.6 1.7 copy-done.3
  28.3 2.9 multiply_bitcast_fusion.2
  31.2 21.0 %collective-permute-done = f32[4,2,64,1024]{3,2,1,0:T(8,128)S(1)} collective-permute-done((f32[4,2,64,1024]{3,2,1,0:T(8,128)}, f32[4,2,64,1024]{3,2,1,0:T(8,128)S(1)}, u32[]{:S(2)}, u32[]{:S(2)}) %collective-permute-start) | collective-permute-done | bytes 2097184 | tf_op jit(solution)/shard_map/ppermute | solution.py:17
  52.1 3.2 collective-permute-done.1
  55.3 1.4 pad_maximum_fusion.32
  56.7 1.3 collective-permute-start.2
  58.0 0.0 slice-start
  58.0 0.0 slice-start.1
  58.0 7.1 %collective-permute-start.3 = (f32[4,12,2,1024]{3,2,1,0:T(2,128)S(1)}, f32[4,12,2,1024]{3,2,1,0:T(2,128)}, u32[]{:S(2)}, u32[]{:S(2)}) collective-permute-start(f32[4,12,2,1024]{3,2,1,0:T(2,128)S(1)} %get-tuple-element.10), channel_id=1, source_target_pairs={{0,1},{1,2},{2,3},{3,4},{4,5},{5,6},{6,7},{8,9},{9,10},{10,11},{11... | collective-permute-start | bytes 1179656 | tf_op jit(solution)/shard_map/ppermute | solution.py:14
  65.1 8.6 %pad_maximum_fusion = (f32[4,10,64,1024]{3,2,1,0:T(8,128)}, f32[4,10,64,1024]{3,2,1,0:T(8,128)}) fusion(f32[4,2,64,1024]{3,2,1,0:T(8,128)S(1)} %collective-permute-done, f32[1,8,64,1024]{3,2,1,0:T(8,128)S(1)} %bitcast.75, f32[3,8,64,1024]{3,2,1,0:T(8,128)S(1)} %copy-done.1, f32[4,2,64,1024]{3,2,1,0:T(8,128)} %collective-permute-done.1), kind=kLoop, calls=%fused_computation.18 | loop fusion | flops 10485760 | bytes 33554432 | tf_op jit(solution)/shard_map/concatenate | solution.py:18
  73.6 0.0 collective-permute-done.2
  73.6 4.8 %collective-permute-done.3 = f32[4,12,2,1024]{3,2,1,0:T(2,128)} collective-permute-done((f32[4,12,2,1024]{3,2,1,0:T(2,128)S(1)}, f32[4,12,2,1024]{3,2,1,0:T(2,128)}, u32[]{:S(2)}, u32[]{:S(2)}) %collective-permute-start.3) | collective-permute-done | bytes 393248 | tf_op jit(solution)/shard_map/ppermute | solution.py:14
  78.4 0.0 slice-done
  78.5 6.2 %fusion.79 = (f32[8,64,1024]{2,1,0:T(8,128)}, f32[8,64,1024]{2,1,0:T(8,128)}, f32[8,64,1024]{2,1,0:T(8,128)}, f32[8,64,1024]{2,1,0:T(8,128)}, f32[8,64,1024]{2,1,0:T(8,128)}) fusion(f32[8,64,1024]{2,1,0:T(8,128)S(1)} %copy-done.2, f32[4,12,2,1024]{3,2,1,0:T(2,128)S(1)} %collective-permute-done.2, f32[4,2,64,1024]{3,2,1,0:T(8,128)} %copy-done.4, ...), kind=kLoop, calls=%fused_computation.115 | loop fusion | flops 12058624 | bytes 34340864 | tf_op jit(solution)/shard_map/mul | solution.py:40
  84.6 68.5 %fusion.11 = f32[3,8,64,1024]{3,2,1,0:T(8,128)} fusion(f32[3,8,64,1024]{3,2,1,0:T(8,128)} %param.7, f32[4,12,2,1024]{3,2,1,0:T(2,128)} %collective-permute-done.3, f32[4,2,64,1024]{3,2,1,0:T(8,128)} %copy-done.4, f32[4,2,64,1024]{3,2,1,0:T(8,128)} %collective-permute-done.1, f32[1,8,64,1024]{3,2,1,0:T(8,128)S(1)} %bitcast.77, ...), kind=kOutput, calls=%fused_computation.32 | convolution fusion | flops 19428016128 | bytes 97257024 | tf_op jit(solution)/shard_map/cars,ts->cart/dot_general | solution.py:65
  153.1 9.8 %copy.22 = f32[3,8,64,1024]{2,1,0,3:T(8,128)} copy(f32[3,8,64,1024]{3,2,1,0:T(8,128)} %fusion.11) | data formatting | bytes 12582912 | tf_op jit(solution)/shard_map/cars,ts->cart/dot_general | solution.py:65
  162.9 12.6 %reshape.26 = f32[8,1,196608]{2,1,0:T(1,128)} reshape(f32[1024,3,8,64]{3,2,1,0:T(8,128)} %bitcast.78) | data formatting | bytes 12582912
  175.5 81.7 %all_to_all.36 = f32[8,1,196608]{2,1,0:T(1,128)} all-to-all(f32[8,1,196608]{2,1,0:T(1,128)} %reshape.26), channel_id=1, replica_groups=mesh['ax'=16,'rad'=8] {'rad'}, dimensions={0} | all-to-all | bytes 12582912 | tf_op jit(solution)/shard_map/all_to_all | solution.py:67
  257.2 0.6 broadcast.46
  257.8 19.5 %reduce = f32[8,196608]{1,0:T(8,128)} reduce(f32[8,1,196608]{2,1,0:T(1,128)} %all_to_all.36, f32[]{:T(128)} %broadcast.46), dimensions={1}, to_apply=%all_to_all.26.reduce_sub_computation | reduce | bytes 12582916 | tf_op jit(solution)/shard_map/all_to_all | solution.py:67
  277.4 12.2 %reshape.27 = f32[1024,3,8,64]{3,2,1,0:T(8,128)} reshape(f32[8,196608]{1,0:T(8,128)} %reduce) | data formatting | bytes 12582912
  289.6 9.8 %copy.24 = f32[3,8,8,64,128]{4,3,2,1,0:T(8,128)} copy(f32[3,8,8,64,128]{3,1,0,4,2:T(8,128)} %bitcast.79) | data formatting | bytes 12582912 | tf_op jit(solution)/shard_map/all_to_all | solution.py:67
  299.3 23.0 %convolution_bitcast_fusion = f32[3,8,512,128]{2,3,1,0:T(8,128)} fusion(f32[3,8,512,128]{3,2,1,0:T(8,128)} %bitcast.83, f32[512,512]{1,0:T(8,128)S(1)} %copy-done), kind=kOutput, calls=%fused_computation.107 | convolution fusion | flops 9663676416 | bytes 13631488 | tf_op jit(solution)/shard_map/rk,cakt->cart/dot_general | solution.py:63
  322.3 6.6 %copy.26 = f32[3,8,512,128]{3,1,0,2:T(8,128)} copy(f32[3,8,512,128]{2,3,1,0:T(8,128)} %convolution_bitcast_fusion) | data formatting | bytes 12582912 | tf_op jit(solution)/shard_map/rk,cakt->cart/transpose | solution.py:63
  328.8 76.0 %all_to_all.37 = f32[3,8,512,128]{3,1,0,2:T(8,128)S(1)} all-to-all(f32[3,8,512,128]{3,1,0,2:T(8,128)} %copy.26), channel_id=1, replica_groups=mesh['ax'=16,'rad'=8] {'rad'}, dimensions={2} | all-to-all | bytes 12582912 | tf_op jit(solution)/shard_map/all_to_all | solution.py:66
  404.9 6.3 %copy.28 = f32[3,8,64,8,128]{4,3,2,1,0:T(8,128)} copy(f32[3,8,64,8,128]{4,1,0,2,3:T(8,128)S(1)} %bitcast.82) | data formatting | bytes 12582912 | tf_op jit(solution)/shard_map/all_to_all | solution.py:66
  411.2 7.1 %all_to_all.33 = f32[3,8,64,1024]{3,2,1,0:T(8,128)} reshape(f32[3,8,64,8,128]{4,3,2,1,0:T(8,128)} %copy.28) | data formatting | bytes 12582912 | tf_op jit(solution)/shard_map/all_to_all | solution.py:66
  (11 shorter events, 0.0 us)
Async XLA Ops:
  0.0 299.3 %copy-start = (f32[512,512]{1,0:T(8,128)S(1)}, f32[512,512]{1,0:T(8,128)}, u32[]{:S(2)}) copy-start(f32[512,512]{1,0:T(8,128)} %param.13) | copy-start | bytes 3145732
  0.0 9.9 %copy-start.9 = (f32[8]{0:T(128)S(1)}, f32[8]{0:T(128)}, u32[]{:S(2)}) copy-start(f32[8]{0:T(128)} %param.9) | copy-start | bytes 100
  0.0 9.9 %copy-start.8 = (f32[64]{0:T(128)S(1)}, f32[64]{0:T(128)}, u32[]{:S(2)}) copy-start(f32[64]{0:T(128)} %param.11) | copy-start | bytes 772
  0.0 10.5 %copy-start.7 = (f32[64]{0:T(128)S(1)}, f32[64]{0:T(128)}, u32[]{:S(2)}) copy-start(f32[64]{0:T(128)} %param.10) | copy-start | bytes 772
  0.0 11.1 %copy-start.1 = (f32[3,8,64,1024]{3,2,1,0:T(8,128)S(1)}, f32[3,8,64,1024]{3,2,1,0:T(8,128)}, u32[]{:S(2)}) copy-start(f32[3,8,64,1024]{3,2,1,0:T(8,128)} %param.7) | copy-start | bytes 18874372
  0.0 11.1 %copy-start.2 = (f32[8,64,1024]{2,1,0:T(8,128)S(1)}, f32[8,64,1024]{2,1,0:T(8,128)}, u32[]{:S(2)}) copy-start(f32[8,64,1024]{2,1,0:T(8,128)} %param.8) | copy-start | bytes 6291460
  5.1 47.1 %collective-permute-start = (f32[4,2,64,1024]{3,2,1,0:T(8,128)}, f32[4,2,64,1024]{3,2,1,0:T(8,128)S(1)}, u32[]{:S(2)}, u32[]{:S(2)}) collective-permute-start(f32[4,2,64,1024]{3,2,1,0:T(8,128)} %get-tuple-element.20), channel_id=1, source_target_pairs={{8,0},{16,8},{24,16},{32,24},{40,32},{48,40},{56,48},{64,56},{72,6... | collective-permute-start | bytes 6291464 | tf_op jit(solution)/shard_map/ppermute | solution.py:17
  8.0 47.3 %collective-permute-start.1 = (f32[4,2,64,1024]{3,2,1,0:T(8,128)}, f32[4,2,64,1024]{3,2,1,0:T(8,128)}, u32[]{:S(2)}, u32[]{:S(2)}) collective-permute-start(f32[4,2,64,1024]{3,2,1,0:T(8,128)} %get-tuple-element.19), channel_id=1, source_target_pairs={{0,8},{8,16},{16,24},{24,32},{32,40},{40,48},{48,56},{56,64},{64,7... | collective-permute-start | bytes 6291464 | tf_op jit(solution)/shard_map/ppermute | solution.py:14
  11.5 12.9 %copy-start.6 = (f32[4,8,64,1]{3,2,1,0:T(8,128)}, f32[4,8,64,1]{3,2,1,0:T(8,128)S(1)}, u32[]{:S(2)}) copy-start(f32[4,8,64,1]{3,2,1,0:T(8,128)S(1)} %get-tuple-element.13) | copy-start | bytes 24580
  11.5 66.9 %copy-start.5 = (f32[4,8,64,1]{3,2,1,0:T(8,128)}, f32[4,8,64,1]{3,2,1,0:T(8,128)S(1)}, u32[]{:S(2)}) copy-start(f32[4,8,64,1]{3,2,1,0:T(8,128)S(1)} %get-tuple-element.14) | copy-start | bytes 24580
  24.4 3.9 copy-start.3
  52.1 13.0 %copy-start.4 = (f32[4,2,64,1024]{3,2,1,0:T(8,128)}, f32[4,2,64,1024]{3,2,1,0:T(8,128)S(1)}, u32[]{:S(2)}) copy-start(f32[4,2,64,1024]{3,2,1,0:T(8,128)S(1)} %collective-permute-done) | copy-start | bytes 6291460
  56.7 16.9 %collective-permute-start.2 = (f32[4,12,2,1024]{3,2,1,0:T(2,128)S(1)}, f32[4,12,2,1024]{3,2,1,0:T(2,128)S(1)}, u32[]{:S(2)}, u32[]{:S(2)}) collective-permute-start(f32[4,12,2,1024]{3,2,1,0:T(2,128)S(1)} %get-tuple-element.9), channel_id=1, source_target_pairs={{1,0},{2,1},{3,2},{4,3},{5,4},{6,5},{7,6},{9,8},{10,9},{11,10},{12... | collective-permute-start | bytes 1179656 | tf_op jit(solution)/shard_map/ppermute | solution.py:17
  58.0 20.5 %slice-start = ((s8[8388608]{0:T(1024)(128)(4,1)}), s8[4194304]{0:T(1024)(128)(4,1)S(1)}, s32[]{:S(2)}) async-start(s8[8388608]{0:T(1024)(128)(4,1)} %bitcast.80), calls=%async_computation.2 | async-start | bytes 8388608
  58.0 20.4 %slice-start.1 = ((s8[8388608]{0:T(1024)(128)(4,1)}), s8[4194304]{0:T(1024)(128)(4,1)S(1)}, s32[]{:S(2)}) async-start(s8[8388608]{0:T(1024)(128)(4,1)} %bitcast.80), calls=%async_computation.3 | async-start | bytes 8388608
  58.0 20.4 %collective-permute-start.3 = (f32[4,12,2,1024]{3,2,1,0:T(2,128)S(1)}, f32[4,12,2,1024]{3,2,1,0:T(2,128)}, u32[]{:S(2)}, u32[]{:S(2)}) collective-permute-start(f32[4,12,2,1024]{3,2,1,0:T(2,128)S(1)} %get-tuple-element.10), channel_id=1, source_target_pairs={{0,1},{1,2},{2,3},{3,4},{4,5},{5,6},{6,7},{8,9},{9,10},{10,11},{11... | collective-permute-start | bytes 1179656 | tf_op jit(solution)/shard_map/ppermute | solution.py:14
where the time goes:
time: 419 us; the launch traced here: 418 us
  blocking collectives  158 us (38%)
  matrix products  91.4 us (22%)
  local copies, waits for them, and re-layouts  66.6 us (16%)
  other arithmetic  60.2 us (14%)
  waiting for transfers between devices  28.9 us (7%)
  starting transfers between devices  13.2 us (3%)
    all_to_all x1, blocking collectives, local(): lax.all_to_all(solved, 'rad', split_axis=3, concat_axis=2, tiled=True)  81.7 us
    all_to_all x1, blocking collectives, local(): lax.all_to_all(radial(lax.all_to_all(solved, 'rad', split_axis=3, concat_...  76 us
    dot_general x1, matrix products, local(): jnp.einsum('cars,ts->cart', rhs, az_inverse, precision=lax.Precision.HIGH...  68.5 us
    unnamed x26, local copies, waits for them, and re-layouts  26.6 us
    dot_general x1, matrix products, radial(): jnp.einsum('rk,cakt->cart', rad_inverse, field, precision=lax.Precision.H...  23 us
    ppermute x2, waiting for transfers between devices, padded_2(): lax.ppermute(lax.slice_in_dim(block, 0, width, axis=dim), axis, backward)  21 us
    all_to_all x1, other arithmetic, local(): lax.all_to_all(solved, 'rad', split_axis=3, concat_axis=2, tiled=True)  19.5 us
    concatenate x5, other arithmetic, local(): fields = jnp.concatenate([velocity, viscosity[None]], axis=0)  18.3 us
  transfers between devices with their start and end apart: 4, of which 3 were waited for; matrix products, arithmetic and copies ran while one was open for 7% of the time, Pallas kernels for 0%

commit v1 on v0

v1 whole, which is shorter than its diff:
```python
import functools

import jax
import jax.numpy as jnp
from jax import lax
from jax.experimental import pallas as pl
from jax.experimental.pallas import tpu as pltpu
from jax.sharding import PartitionSpec as P

COEF = 0.25
F32 = jnp.float32
BF16 = jnp.bfloat16
CHUNKS = ((2, 3), (4, 5), (0, 1), (6, 7))
HALF_BYTES = 200 * 1024 * 1024
VMEM_LIMIT = 56 * 1024 * 1024


def split(x):
    hi = x.astype(BF16)
    return hi, (x - hi.astype(F32)).astype(BF16)


def dot3(a_hi, a_lo, b_hi, b_lo, dims):
    dot = functools.partial(
        lax.dot_general, dimension_numbers=(dims, ((), ())), preferred_element_type=F32
    )
    return dot(a_hi, b_hi) + (dot(a_hi, b_lo) + dot(a_lo, b_hi))


def split_kernel(x_ref, hi_ref, lo_ref):
    hi_ref[...], lo_ref[...] = split(x_ref[...])


def split_call(x):
    rows, cols = x.shape
    spec = pl.BlockSpec((256, cols), lambda i: (i, 0))
    return pl.pallas_call(
        split_kernel,
        name=f"split_{rows}",
        grid=(rows // 256,),
        in_specs=[spec],
        out_specs=[spec, spec],
        out_shape=[jax.ShapeDtypeStruct(x.shape, BF16)] * 2,
    )(x)


def rhs_kernel(
    planes, edge, inv_dx, inv_dr, inv_rt, velocity, viscosity, rad_lo, rad_hi, *rest
):
    if edge:
        ax_lo, ax_hi, az_hi, az_lo, out, vbuf, nbuf, rhs, sems = rest
    else:
        az_hi, az_lo, out, vbuf, nbuf, rhs, sems = rest
    rows, nt = velocity.shape[2], velocity.shape[3]
    width = out.shape[3]
    copies = []

    def bring(source, target):
        copy = pltpu.make_async_copy(source, target, sems.at[len(copies)])
        copy.start()
        copies.append(copy)

    for c in range(3):
        bring(velocity.at[c], vbuf.at[c, pl.ds(2, 8), pl.ds(8, rows)])
    bring(viscosity, nbuf.at[pl.ds(2, 8), pl.ds(8, rows)])
    if edge:
        for halo, at, thin in ((ax_lo, 0, 1), (ax_hi, 10, 10)):
            for c in range(3):
                bring(halo.at[pl.ds(2 * c, 2)], vbuf.at[c, pl.ds(at, 2), pl.ds(8, rows)])
            bring(halo.at[6], nbuf.at[thin, pl.ds(8, rows)])
    for copy in copies:
        copy.wait()

    def plane(j, carry):
        p = planes[0] + j
        at = p + 2
        low, high = rad_lo[p], rad_hi[p]
        for c in range(3):
            vbuf[c, at, 0:8, :] = pltpu.roll(low, 6 - 2 * c, 0)
            vbuf[c, at, rows + 8 : rows + 16, :] = pltpu.roll(high, (8 - 2 * c) % 8, 0)
        nbuf[at, 0:8, :] = pltpu.roll(low, 1, 0)
        nbuf[at, rows + 8 : rows + 16, :] = pltpu.roll(high, 2, 0)
        gx = inv_dx[p]

        def strip(i, carry):
            r0 = pl.multiple_of(i * 8, 8)
            mid = pl.ds(pl.multiple_of(r0 + 8, 8), 8)
            wide = pl.ds(r0, 24)
            gr = inv_dr[pl.ds(r0, 8), :]
            gt = inv_rt[pl.ds(r0, 8), :]
            nu = nbuf[at, mid, :]
            nu24 = nbuf[at, wide, :]
            nus = (
                (nbuf[at + 1, mid, :], nbuf[at - 1, mid, :], gx),
                (pltpu.roll(nu, nt - 1, 1), pltpu.roll(nu, 1, 1), gt),
                (nu24[9:17], nu24[7:15], gr),
            )
            coefs = []
            centre = None
            for d, (up, down, g) in enumerate(nus):
                gg = (0.5 * COEF) * g * g
                a_up = gg * (nu + up)
                a_down = gg * (nu + down)
                b = ((COEF / 12.0) * g) * vbuf[d, at, mid, :]
                b8 = 8.0 * b
                total = a_up + a_down
                centre = total if centre is None else centre + total
                coefs.append((a_up - b8, a_down + b8, b))
            centre = 1.0 - centre
            for c in range(3):
                q24 = vbuf[c, at, wide, :]
                q = q24[8:16]
                near = (
                    (
                        vbuf[c, at + 1, mid, :],
                        vbuf[c, at - 1, mid, :],
                        vbuf[c, at + 2, mid, :],
                        vbuf[c, at - 2, mid, :],
                    ),
                    (
                        pltpu.roll(q, nt - 1, 1),
                        pltpu.roll(q, 1, 1),
                        pltpu.roll(q, nt - 2, 1),
                        pltpu.roll(q, 2, 1),
                    ),
                    (q24[9:17], q24[7:15], q24[10:18], q24[6:14]),
                )
                total = centre * q
                for (up, down, up2, down2), (c_up, c_down, b) in zip(near, coefs):
                    total = total + c_up * up + c_down * down + b * (up2 - down2)
                rhs[c, pl.ds(r0, 8), :] = total
            return carry

        lax.fori_loop(0, rows // 8, strip, 0)
        hi, lo = split(rhs[...].reshape(3 * rows, nt))
        solved = dot3(hi, lo, az_hi[...], az_lo[...], ((1,), (1,)))
        for c in range(3):
            for d in range(nt // width):
                out[d, 3 * j + c] = solved[
                    c * rows : (c + 1) * rows, d * width : (d + 1) * width
                ]
        return carry

    lax.fori_loop(0, len(planes), plane, 0)


def rhs_call(planes, parts, inv_dx, inv_dr, inv_rt, velocity, viscosity, rad_lo, rad_hi, ax, az):
    rows, nt = velocity.shape[2], velocity.shape[3]
    anywhere = pl.BlockSpec(memory_space=pl.ANY)
    vmem = pl.BlockSpec(memory_space=pltpu.VMEM)
    slabs = 3 * len(planes)
    return pl.pallas_call(
        functools.partial(rhs_kernel, planes, bool(ax)),
        name=f"rhs_{planes[0]}",
        in_specs=[pl.BlockSpec(memory_space=pltpu.SMEM), vmem, vmem, anywhere, anywhere, vmem, vmem]
        + [anywhere] * len(ax)
        + [vmem, vmem],
        out_specs=vmem,
        out_shape=jax.ShapeDtypeStruct((parts, slabs, rows, nt // parts), F32),
        scratch_shapes=[
            pltpu.VMEM((3, 12, rows + 16, nt), F32),
            pltpu.VMEM((12, rows + 16, nt), F32),
            pltpu.VMEM((3, rows, nt), F32),
            pltpu.SemaphoreType.DMA((12,)),
        ],
        compiler_params=pltpu.CompilerParams(vmem_limit_bytes=VMEM_LIMIT),
        cost_estimate=pl.CostEstimate(
            flops=1024,
            bytes_accessed=1024,
            transcendentals=0,
        ),
    )(inv_dx, inv_dr[:, None], inv_rt[:, None], velocity, viscosity, rad_lo, rad_hi, *ax, *az)


def half_kernel(side_ref, x_ref, hi_ref, lo_ref):
    rows = x_ref.shape[0] // 8
    side = side_ref[0]
    for part in range(4):
        x = x_ref[pl.ds(pl.multiple_of(part * 2 * rows + side * rows, rows), rows), :]
        swapped = jnp.concatenate(
            [
                pltpu.roll(x[:, at : at + 2 * rows], rows, 1)
                for at in range(0, x.shape[1], 2 * rows)
            ],
            axis=1,
        )
        at = slice(part * rows, (part + 1) * rows)
        hi_ref[at, :], lo_ref[at, :] = split(jnp.where(side == 0, x, swapped))


def half_call(side, x):
    rows, cols = x.shape
    vmem = pl.BlockSpec(memory_space=pltpu.VMEM)
    return pl.pallas_call(
        half_kernel,
        name="half",
        in_specs=[pl.BlockSpec(memory_space=pltpu.SMEM), vmem],
        out_specs=[vmem, vmem],
        out_shape=[jax.ShapeDtypeStruct((rows // 2, cols), BF16)] * 2,
        cost_estimate=pl.CostEstimate(
            flops=0, bytes_accessed=HALF_BYTES, transcendentals=0
        ),
    )(side, x)


def radial_kernel(r_hi, r_lo, own_ref, other_ref, out_ref):
    parts, slabs, rows, width = own_ref.shape
    x = jnp.concatenate(
        [
            jnp.concatenate(
                [ref[part, s] for part in range(parts) for ref in (own_ref, other_ref)], axis=0
            )
            for s in range(slabs)
        ],
        axis=1,
    )
    hi, lo = split(x)
    y = dot3(r_hi[...], r_lo[...], hi, lo, ((1,), (0,)))
    for s in range(slabs):
        out_ref[:, s] = y[:, s * width : (s + 1) * width].reshape(parts, rows, width)


def radial_call(rad, own, other):
    parts, slabs, rows, width = own.shape
    step = 3
    block = pl.BlockSpec((parts, step, rows, width), lambda i: (0, i, 0, 0))
    full = pl.BlockSpec(rad[0].shape, lambda i: (0, 0))
    return pl.pallas_call(
        radial_kernel,
        name="radial",
        grid=(slabs // step,),
        in_specs=[full, full, block, block],
        out_specs=block,
        out_shape=jax.ShapeDtypeStruct(own.shape, F32),
        compiler_params=pltpu.CompilerParams(vmem_limit_bytes=VMEM_LIMIT),
        cost_estimate=pl.CostEstimate(
            flops=12 * slabs * parts * rows * parts * rows * width,
            bytes_accessed=12 * own.size,
            transcendentals=0,
        ),
    )(*rad, own, other)


def place_kernel(x_ref, *rest):
    out_ref = rest[-1]
    for d in range(x_ref.shape[0]):
        width = x_ref.shape[3]
        for c in range(x_ref.shape[1]):
            out_ref[c, 0, :, d * width : (d + 1) * width] = x_ref[d, c]


def place_call(planes, x, whole, shape):
    parts, slabs, rows, width = x.shape
    first = planes[0]
    aliased = () if whole is None else (whole,)

    return pl.pallas_call(
        place_kernel,
        name="place",
        grid=(len(planes),),
        in_specs=[pl.BlockSpec((parts, 3, rows, width), lambda j: (0, j, 0, 0))]
        + [pl.BlockSpec(memory_space=pl.ANY)] * len(aliased),
        out_specs=pl.BlockSpec((3, 1, rows, parts * width), lambda j: (0, first + j, 0, 0)),
        out_shape=jax.ShapeDtypeStruct(shape, F32),
        input_output_aliases={1: 0} if aliased else {},
        cost_estimate=pl.CostEstimate(flops=0, bytes_accessed=8 * x.size, transcendentals=0),
    )(x, *aliased)


def pack_kernel(velocity, viscosity, rad_top, rad_bottom, ax_top, ax_bottom, edges, sems):
    planes, rows = viscosity.shape[0], viscosity.shape[1]
    copies = []

    def move(source, target):
        copy = pltpu.make_async_copy(source, target, sems.at[len(copies)])
        copy.start()
        copies.append(copy)

    for side, at in enumerate((rows - 8, 0)):
        for c in range(3):
            move(velocity.at[c, :, pl.ds(at, 8)], edges.at[side, c])
        move(viscosity.at[:, pl.ds(at, 8)], edges.at[side, 3])
    near = len(copies)
    for out, at, thin in ((ax_top, planes - 2, planes - 1), (ax_bottom, 0, 0)):
        for c in range(3):
            move(velocity.at[c, pl.ds(at, 2)], out.at[pl.ds(2 * c, 2)])
        move(viscosity.at[thin], out.at[6])
    for copy in copies[:near]:
        copy.wait()
    row = lax.broadcasted_iota(jnp.int32, edges.shape[3:], 0)
    for p in range(planes):
        for side, out, turns in ((0, rad_top, (2, 4, 6, 7)), (1, rad_bottom, (0, 2, 4, 6))):
            strips = [
                pltpu.roll(edges[side, f, p], turn, 0) if turn else edges[side, f, p]
                for f, turn in enumerate(turns)
            ]
            out[p] = jnp.where(
                row < 4,
                jnp.where(row < 2, strips[0], strips[1]),
                jnp.where(row < 6, strips[2], strips[3]),
            )
    for copy in copies[near:]:
        copy.wait()


def pack_call(velocity, viscosity):
    planes, rows, nt = viscosity.shape
    anywhere = pl.BlockSpec(memory_space=pl.ANY)
    vmem = pl.BlockSpec(memory_space=pltpu.VMEM)
    line = jax.ShapeDtypeStruct((planes, 8, nt), F32)
    face = jax.ShapeDtypeStruct((7, rows, nt), F32)
    return pl.pallas_call(
        pack_kernel,
        name="pack",
        in_specs=[anywhere, anywhere],
        out_specs=[vmem, vmem, vmem, vmem],
        out_shape=[line, line, face, face],
        scratch_shapes=[pltpu.VMEM((2, 4, planes, 8, nt), F32), pltpu.SemaphoreType.DMA((16,))],
        compiler_params=pltpu.CompilerParams(vmem_limit_bytes=VMEM_LIMIT),
    )(velocity, viscosity)


def after(x, *events):
    return lax.optimization_barrier((x, *events))[0]


def local(velocity, viscosity, inv_dx, inv_dr, inv_rt, az_inverse, rad_inverse):
    planes = velocity.shape[1]
    lines = lax.axis_size("rad")
    parts = lines // 2
    side = (lax.axis_index("rad") % 2).astype(jnp.int32).reshape(1)

    def shifts(axis):
        count = lax.axis_size(axis)
        forward = [(i, i + 1) for i in range(count - 1)]
        return forward, [(b, a) for a, b in forward]

    rad_top, rad_bottom, ax_top, ax_bottom = pack_call(velocity, viscosity)
    forward, backward = shifts("rad")
    rad_lo = lax.ppermute(rad_top, "rad", forward)
    rad_hi = lax.ppermute(rad_bottom, "rad", backward)
    forward, backward = shifts("ax")
    ax_top, ax_bottom, rad_lo, rad_hi = lax.optimization_barrier(
        (ax_top, ax_bottom, rad_lo, rad_hi)
    )
    ax_lo = lax.ppermute(ax_top, "ax", forward)
    ax_hi = lax.ppermute(ax_bottom, "ax", backward)

    az = split_call(az_inverse)
    groups = [list(range(0, lines, 2)), list(range(1, lines, 2))]

    def exchange(x):
        return lax.all_to_all(
            x, "rad", split_axis=0, concat_axis=0, tiled=True, axis_index_groups=groups
        )

    def partner(x):
        return lax.ppermute(x, "rad", [(i, i ^ 1) for i in range(lines)])

    count = len(CHUNKS)
    out, own, other, back = [], [], [], []
    for k, chunk in enumerate(CHUNKS):
        edge = min(chunk) < 2 or max(chunk) >= planes - 2
        dx = inv_dx if k == 0 else after(inv_dx, out[-1])
        if k == 2:
            rad = half_call(after(side, ax_lo, ax_hi, out[-1]), rad_inverse)
            dx = after(dx, rad[0])
        if k > 2:
            dx = after(dx, other[k - 3])
        out.append(
            rhs_call(
                chunk, parts, dx, inv_dr, inv_rt, velocity, viscosity, rad_lo, rad_hi,
                (ax_lo, ax_hi) if edge else (), az,
            )
        )
        if k == 1:
            continue
        for j in {0: (0,), 2: (1, 2)}.get(k, (k,)):
            own.append(exchange(after(out[j], own[-1], *((rad[0],) if j == 1 else ())) if j else out[j]))
            if k == 2 and j == 1:
                other.append(partner(after(own[0], rad[0])))
        if k >= 2:
            other.append(partner(after(own[k - 1], rad[0], *((other[k - 3],) if k > 2 else ()))))
    other.append(partner(after(own[count - 1], other[count - 3])))
    whole = None
    for k, chunk in enumerate(CHUNKS):
        solved = radial_call(rad, own[k], other[k])
        back.append(exchange(after(solved, back[-1] if k else own[-1])))
        whole = place_call(chunk, back[k], whole, velocity.shape)
    return whole


def solution(mesh):
    placed = (
        P(None, "ax", "rad", None),
        P("ax", "rad", None),
        P("ax"),
        P("rad"),
        P("rad"),
        P(),
        P(),
    )
    return jax.shard_map(
        local, mesh=mesh, in_specs=placed, out_specs=P(None, "ax", "rad", None), check_vma=False
    )
```

time: 419 us -> 276 us (0.66)
  the two profiles are of different devices: /device:TPU:96 before, /device:TPU:0 now
where the time goes in v1:
time: 276 us; the launch traced here: 275 us
  waiting for transfers between devices  116 us (42%)
  Pallas kernels  99.7 us (36%)
  starting transfers between devices  52.1 us (19%)
  local copies, waits for them, and re-layouts  7.33 us (3%)
    ppermute x4, waiting for transfers between devices, partner(): return lax.ppermute(x, 'rad', [(i, i ^ 1) for i in range(lines)])  67.7 us
    pallas_call x4, Pallas kernels, rhs_call(): pl.pallas_call(functools.partial(rhs_kernel, planes, bool(ax)), name=f'rh...  61.9 us
    all_to_all x8, waiting for transfers between devices, exchange(): lax.all_to_all(x, 'rad', split_axis=0, concat_axis=0, tiled=True, axis_in...  37.8 us
    all_to_all x8, starting transfers between devices, exchange(): lax.all_to_all(x, 'rad', split_axis=0, concat_axis=0, tiled=True, axis_in...  35.9 us
    pallas_call x4, Pallas kernels, radial_call(): pl.pallas_call(radial_kernel, name='radial', grid=(slabs // step,), in_sp...  16 us
    ppermute x1, waiting for transfers between devices, local(): rad_lo = lax.ppermute(rad_top, 'rad', forward)  10.2 us
    pallas_call x4, Pallas kernels, place_call(): pl.pallas_call(place_kernel, name='place', grid=(len(planes),), in_specs=...  9.3 us
    ppermute x4, starting transfers between devices, partner(): return lax.ppermute(x, 'rad', [(i, i ^ 1) for i in range(lines)])  7.06 us
  transfers between devices with their start and end apart: 16, of which 10 were waited for; matrix products, arithmetic and copies ran while one was open for 1% of the time, Pallas kernels for 34%

profile of v1, /device:TPU:0, one launch (start us, length us, event | category | flops | bytes accessed | tf_op | source)
XLA Modules:
  0.0 275.0 jit_solution(14979937412382096088)
XLA Ops:
  0.0 4.8 %pack.1 = (f32[8,8,1024]{2,1,0:T(8,128)}, f32[8,8,1024]{2,1,0:T(8,128)}, f32[7,64,1024]{2,1,0:T(8,128)}, f32[7,64,1024]{2,1,0:T(8,128)}) custom-call(f32[3,8,64,1024]{3,2,1,0:T(8,128)} %velocity.9, f32[8,64,1024]{2,1,0:T(8,128)} %viscosity.9), custom_call_target="tpu_custom_call" | custom-call | tf_op jit(solution)/shard_map/pack/pallas_call | solution.py:312
  4.8 5.2 %collective-permute-start = (f32[8,8,1024]{2,1,0:T(8,128)}, f32[8,8,1024]{2,1,0:T(8,128)S(1)}, u32[]{:S(2)}, u32[]{:S(2)}) collective-permute-start(f32[8,8,1024]{2,1,0:T(8,128)} %get-tuple-element.36), channel_id=1, source_target_pairs={{0,1},{1,2},{2,3},{3,4},{4,5},{5,6},{6,7},{8,9},{9,10},{10,11},{11... | collective-permute-start | bytes 786440 | tf_op jit(solution)/shard_map/ppermute | solution.py:340
  10.0 1.3 collective-permute-start.1
  11.3 10.2 %collective-permute-done.rad_lo = f32[8,8,1024]{2,1,0:T(8,128)S(1)} collective-permute-done((f32[8,8,1024]{2,1,0:T(8,128)}, f32[8,8,1024]{2,1,0:T(8,128)S(1)}, u32[]{:S(2)}, u32[]{:S(2)}) %collective-permute-start) | collective-permute-done | bytes 262176 | tf_op jit(solution)/shard_map/ppermute | solution.py:340
  21.5 1.4 collective-permute-start.2
  22.9 1.3 collective-permute-start.3
  24.2 0.7 copy.11.inv_dr
  24.9 0.7 copy.12.inv_rt
  25.6 4.7 %split_1024.1 = (bf16[1024,1024]{1,0:T(8,128)(2,1)}, bf16[1024,1024]{1,0:T(8,128)(2,1)}) custom-call(f32[1024,1024]{1,0:T(8,128)} %x_ref.2), custom_call_target="tpu_custom_call" | custom-call | tf_op jit(solution)/shard_map/split_1024/pallas_call | solution.py:37
  30.4 14.9 %rhs_2.1 = f32[4,6,64,256]{3,2,1,0:T(8,128)} custom-call(f32[8]{0:T(128)} %inv_dx.4, f32[64,1]{1,0:T(8,128)} %copy.11.inv_dr, f32[64,1]{1,0:T(8,128)} %copy.12.inv_rt, f32[3,8,64,1024]{3,2,1,0:T(8,128)} %velocity.9, f32[8,64,1024]{2,1,0:T(8,128)} %viscosity.9, f32[8,8,1024]{2,1,0:T(8,128)} %copy-done.6, f32[8,8,1024]{2,1,0:T(8,128)} %copy-done.7, ...), custom_call_target="tpu_custom_call" | custom-call | flops 1024 | bytes 1024 | tf_op jit(solution)/shard_map/rhs_2/pallas_call | solution.py:152
  45.3 6.5 %all-to-all-start = ((f32[4,6,64,256]{3,2,1,0:T(8,128)}), f32[4,6,64,256]{3,2,1,0:T(8,128)S(1)}, u32[]{:S(2)}, u32[]{:S(2)}) async-start(f32[4,6,64,256]{3,2,1,0:T(8,128)} %rhs_2.1), calls=%async_computation | async-start | bytes 3145728 | tf_op jit(solution)/shard_map/all_to_all | solution.py:353
  51.8 14.9 %rhs_4.1 = f32[4,6,64,256]{3,2,1,0:T(8,128)} custom-call(f32[8]{0:T(128)} %inv_dx.4, f32[64,1]{1,0:T(8,128)} %copy.11.inv_dr, f32[64,1]{1,0:T(8,128)} %copy.12.inv_rt, f32[3,8,64,1024]{3,2,1,0:T(8,128)} %velocity.9, f32[8,64,1024]{2,1,0:T(8,128)} %viscosity.9, f32[8,8,1024]{2,1,0:T(8,128)} %copy-done.6, f32[8,8,1024]{2,1,0:T(8,128)} %copy-done.7, ...), custom_call_target="tpu_custom_call" | custom-call | flops 1024 | bytes 1024 | tf_op jit(solution)/shard_map/rhs_4/pallas_call | solution.py:152
  66.7 2.9 %half.1 = (bf16[256,512]{1,0:T(8,128)(2,1)}, bf16[256,512]{1,0:T(8,128)(2,1)}) custom-call(s32[1]{0:T(128)} %bitcast.side_ref, f32[512,512]{1,0:T(8,128)} %x_ref.3), custom_call_target="tpu_custom_call" | custom-call | bytes 209715200 | tf_op jit(solution)/shard_map/half/pallas_call | solution.py:194
  69.6 3.4 %all-to-all-done.own_ref = f32[4,6,64,256]{3,2,1,0:T(8,128)S(1)} async-done(((f32[4,6,64,256]{3,2,1,0:T(8,128)}), f32[4,6,64,256]{3,2,1,0:T(8,128)S(1)}, u32[]{:S(2)}, u32[]{:S(2)}) %all-to-all-start) | async-done | bytes 1572896 | tf_op jit(solution)/shard_map/all_to_all | solution.py:353
  73.0 4.4 %all-to-all-start.1 = ((f32[4,6,64,256]{3,2,1,0:T(8,128)}), f32[4,6,64,256]{3,2,1,0:T(8,128)}, u32[]{:S(2)}, u32[]{:S(2)}) async-start(f32[4,6,64,256]{3,2,1,0:T(8,128)} %rhs_4.1), calls=%async_computation.1 | async-start | bytes 3145728 | tf_op jit(solution)/shard_map/all_to_all | solution.py:353
  77.4 1.4 collective-permute-start.4
  78.8 15.8 %rhs_0.1 = f32[4,6,64,256]{3,2,1,0:T(8,128)} custom-call(f32[8]{0:T(128)} %inv_dx.4, f32[64,1]{1,0:T(8,128)} %copy.11.inv_dr, f32[64,1]{1,0:T(8,128)} %copy.12.inv_rt, f32[3,8,64,1024]{3,2,1,0:T(8,128)} %velocity.9, f32[8,64,1024]{2,1,0:T(8,128)} %viscosity.9, f32[8,8,1024]{2,1,0:T(8,128)} %copy-done.6, f32[8,8,1024]{2,1,0:T(8,128)} %copy-done.7, ...), custom_call_target="tpu_custom_call" | custom-call | flops 1024 | bytes 1024 | tf_op jit(solution)/shard_map/rhs_0/pallas_call | solution.py:152
  94.6 4.8 %all-to-all-done.1.own_ref = f32[4,6,64,256]{3,2,1,0:T(8,128)} async-done(((f32[4,6,64,256]{3,2,1,0:T(8,128)}), f32[4,6,64,256]{3,2,1,0:T(8,128)}, u32[]{:S(2)}, u32[]{:S(2)}) %all-to-all-start.1) | async-done | bytes 1572896 | tf_op jit(solution)/shard_map/all_to_all | solution.py:353
  99.4 4.3 %all-to-all-start.2 = ((f32[4,6,64,256]{3,2,1,0:T(8,128)}), f32[4,6,64,256]{3,2,1,0:T(8,128)}, u32[]{:S(2)}, u32[]{:S(2)}) async-start(f32[4,6,64,256]{3,2,1,0:T(8,128)} %rhs_0.1), calls=%async_computation.2 | async-start | bytes 3145728 | tf_op jit(solution)/shard_map/all_to_all | solution.py:353
  103.7 12.3 %collective-permute-done.4.other_ref = f32[4,6,64,256]{3,2,1,0:T(8,128)S(1)} collective-permute-done((f32[4,6,64,256]{3,2,1,0:T(8,128)S(1)}, f32[4,6,64,256]{3,2,1,0:T(8,128)S(1)}, u32[]{:S(2)}, u32[]{:S(2)}) %collective-permute-start.4) | collective-permute-done | bytes 1572896 | tf_op jit(solution)/shard_map/ppermute | solution.py:358
  116.1 16.3 %rhs_6.1 = f32[4,6,64,256]{3,2,1,0:T(8,128)} custom-call(f32[8]{0:T(128)} %inv_dx.4, f32[64,1]{1,0:T(8,128)} %copy.11.inv_dr, f32[64,1]{1,0:T(8,128)} %copy.12.inv_rt, f32[3,8,64,1024]{3,2,1,0:T(8,128)} %velocity.9, f32[8,64,1024]{2,1,0:T(8,128)} %viscosity.9, f32[8,8,1024]{2,1,0:T(8,128)} %copy-done.6, f32[8,8,1024]{2,1,0:T(8,128)} %copy-done.7, ...), custom_call_target="tpu_custom_call" | custom-call | flops 1024 | bytes 1024 | tf_op jit(solution)/shard_map/rhs_6/pallas_call | solution.py:152
  132.4 4.4 %all-to-all-start.3 = ((f32[4,6,64,256]{3,2,1,0:T(8,128)}), f32[4,6,64,256]{3,2,1,0:T(8,128)}, u32[]{:S(2)}, u32[]{:S(2)}) async-start(f32[4,6,64,256]{3,2,1,0:T(8,128)} %rhs_6.1), calls=%async_computation.3 | async-start | bytes 3145728 | tf_op jit(solution)/shard_map/all_to_all | solution.py:353
  136.8 1.7 collective-permute-start.5
  138.5 4.0 %radial.7 = f32[4,6,64,256]{3,2,1,0:T(8,128)} custom-call(bf16[256,512]{1,0:T(8,128)(2,1)} %get-tuple-element.46.r_hi, bf16[256,512]{1,0:T(8,128)(2,1)} %get-tuple-element.47.r_lo, f32[4,6,64,256]{3,2,1,0:T(8,128)} %copy-done.4, f32[4,6,64,256]{3,2,1,0:T(8,128)} %copy-done.8), custom_call_target="tpu_custom_call" | custom-call | flops 1207959552 | bytes 4718592 | tf_op jit(solution)/shard_map/radial/pallas_call | solution.py:228
  142.5 15.4 %all-to-all-done.3.own_ref = f32[4,6,64,256]{3,2,1,0:T(8,128)} async-done(((f32[4,6,64,256]{3,2,1,0:T(8,128)}), f32[4,6,64,256]{3,2,1,0:T(8,128)}, u32[]{:S(2)}, u32[]{:S(2)}) %all-to-all-start.3) | async-done | bytes 1572896 | tf_op jit(solution)/shard_map/all_to_all | solution.py:353
  157.9 3.6 %all-to-all-start.4 = ((f32[4,6,64,256]{3,2,1,0:T(8,128)}), f32[4,6,64,256]{3,2,1,0:T(8,128)S(1)}, u32[]{:S(2)}, u32[]{:S(2)}) async-start(f32[4,6,64,256]{3,2,1,0:T(8,128)} %radial.7), calls=%async_computation.4 | async-start | bytes 3145728 | tf_op jit(solution)/shard_map/all_to_all | solution.py:353
  161.5 1.9 collective-permute-start.7
  163.4 12.6 %collective-permute-done.5.other_ref = f32[4,6,64,256]{3,2,1,0:T(8,128)} collective-permute-done((f32[4,6,64,256]{3,2,1,0:T(8,128)}, f32[4,6,64,256]{3,2,1,0:T(8,128)}, u32[]{:S(2)}, u32[]{:S(2)}) %collective-permute-start.5) | collective-permute-done | bytes 1572896 | tf_op jit(solution)/shard_map/ppermute | solution.py:358
  176.0 4.0 %radial.6 = f32[4,6,64,256]{3,2,1,0:T(8,128)} custom-call(bf16[256,512]{1,0:T(8,128)(2,1)} %get-tuple-element.46.r_hi, bf16[256,512]{1,0:T(8,128)(2,1)} %get-tuple-element.47.r_lo, f32[4,6,64,256]{3,2,1,0:T(8,128)} %all-to-all-done.1.own_ref, f32[4,6,64,256]{3,2,1,0:T(8,128)} %collective-permute-done.5.other_ref), custom_call_target="tpu_custom_call" | custom-call | flops 1207959552 | bytes 4718592 | tf_op jit(solution)/shard_map/radial/pallas_call | solution.py:228
  180.0 1.6 all-to-all-done.4.x_ref
  181.6 1.1 copy-done.5
  182.7 3.6 %all-to-all-start.5 = ((f32[4,6,64,256]{3,2,1,0:T(8,128)}), f32[4,6,64,256]{3,2,1,0:T(8,128)S(1)}, u32[]{:S(2)}, u32[]{:S(2)}) async-start(f32[4,6,64,256]{3,2,1,0:T(8,128)} %radial.6), calls=%async_computation.5 | async-start | bytes 3145728 | tf_op jit(solution)/shard_map/all_to_all | solution.py:353
  186.3 2.1 collective-permute-start.6
  188.4 21.2 %collective-permute-done.7.other_ref = f32[4,6,64,256]{3,2,1,0:T(8,128)S(1)} collective-permute-done((f32[4,6,64,256]{3,2,1,0:T(8,128)}, f32[4,6,64,256]{3,2,1,0:T(8,128)S(1)}, u32[]{:S(2)}, u32[]{:S(2)}) %collective-permute-start.7) | collective-permute-done | bytes 1572896 | tf_op jit(solution)/shard_map/ppermute | solution.py:358
  209.6 1.1 copy-done.9
  210.7 4.0 %radial.5 = f32[4,6,64,256]{3,2,1,0:T(8,128)} custom-call(bf16[256,512]{1,0:T(8,128)(2,1)} %get-tuple-element.46.r_hi, bf16[256,512]{1,0:T(8,128)(2,1)} %get-tuple-element.47.r_lo, f32[4,6,64,256]{3,2,1,0:T(8,128)} %all-to-all-done.2.own_ref, f32[4,6,64,256]{3,2,1,0:T(8,128)} %copy-done.9), custom_call_target="tpu_custom_call" | custom-call | flops 1207959552 | bytes 4718592 | tf_op jit(solution)/shard_map/radial/pallas_call | solution.py:228
  214.7 1.2 copy-done.1
  215.9 4.8 %all-to-all-start.6 = ((f32[4,6,64,256]{3,2,1,0:T(8,128)}), f32[4,6,64,256]{3,2,1,0:T(8,128)S(1)}, u32[]{:S(2)}, u32[]{:S(2)}) async-start(f32[4,6,64,256]{3,2,1,0:T(8,128)} %radial.5), calls=%async_computation.6 | async-start | bytes 3145728 | tf_op jit(solution)/shard_map/all_to_all | solution.py:353
  220.7 21.6 %collective-permute-done.6.other_ref = f32[4,6,64,256]{3,2,1,0:T(8,128)} collective-permute-done((f32[4,6,64,256]{3,2,1,0:T(8,128)}, f32[4,6,64,256]{3,2,1,0:T(8,128)}, u32[]{:S(2)}, u32[]{:S(2)}) %collective-permute-start.6) | collective-permute-done | bytes 1572896 | tf_op jit(solution)/shard_map/ppermute | solution.py:358
  242.3 4.0 %radial.4 = f32[4,6,64,256]{3,2,1,0:T(8,128)} custom-call(bf16[256,512]{1,0:T(8,128)(2,1)} %get-tuple-element.46.r_hi, bf16[256,512]{1,0:T(8,128)(2,1)} %get-tuple-element.47.r_lo, f32[4,6,64,256]{3,2,1,0:T(8,128)} %all-to-all-done.3.own_ref, f32[4,6,64,256]{3,2,1,0:T(8,128)} %collective-permute-done.6.other_ref), custom_call_target="tpu_custom_call" | custom-call | flops 1207959552 | bytes 4718592 | tf_op jit(solution)/shard_map/radial/pallas_call | solution.py:228
  246.3 1.2 copy-done.2
  247.5 4.4 %all-to-all-start.7 = ((f32[4,6,64,256]{3,2,1,0:T(8,128)}), f32[4,6,64,256]{3,2,1,0:T(8,128)S(1)}, u32[]{:S(2)}, u32[]{:S(2)}) async-start(f32[4,6,64,256]{3,2,1,0:T(8,128)} %radial.4), calls=%async_computation.7 | async-start | bytes 3145728 | tf_op jit(solution)/shard_map/all_to_all | solution.py:353
  251.9 2.3 place.4.rest_0_
  254.2 2.3 place.5.rest_0_
  256.6 2.3 place.6.rest_0_
  258.9 12.6 %all-to-all-done.7.x_ref = f32[4,6,64,256]{3,2,1,0:T(8,128)S(1)} async-done(((f32[4,6,64,256]{3,2,1,0:T(8,128)}), f32[4,6,64,256]{3,2,1,0:T(8,128)S(1)}, u32[]{:S(2)}, u32[]{:S(2)}) %all-to-all-start.7) | async-done | bytes 1572896 | tf_op jit(solution)/shard_map/all_to_all | solution.py:353
  271.4 1.2 copy-done.3
  272.6 2.3 place.7
  (25 shorter events, 0.1 us)
Async XLA Ops:
  0.0 24.2 %copy-start.10 = (f32[64]{0:T(128)S(1)}, f32[64]{0:T(128)}, u32[]{:S(2)}) copy-start(f32[64]{0:T(128)} %param.10) | copy-start | bytes 772
  0.0 24.9 %copy-start.11 = (f32[64]{0:T(128)S(1)}, f32[64]{0:T(128)}, u32[]{:S(2)}) copy-start(f32[64]{0:T(128)} %param.11) | copy-start | bytes 772
  4.8 16.7 %collective-permute-start = (f32[8,8,1024]{2,1,0:T(8,128)}, f32[8,8,1024]{2,1,0:T(8,128)S(1)}, u32[]{:S(2)}, u32[]{:S(2)}) collective-permute-start(f32[8,8,1024]{2,1,0:T(8,128)} %get-tuple-element.36), channel_id=1, source_target_pairs={{0,1},{1,2},{2,3},{3,4},{4,5},{5,6},{6,7},{8,9},{9,10},{10,11},{11... | collective-permute-start | bytes 786440 | tf_op jit(solution)/shard_map/ppermute | solution.py:340
  10.0 11.5 %collective-permute-start.1 = (f32[8,8,1024]{2,1,0:T(8,128)}, f32[8,8,1024]{2,1,0:T(8,128)S(1)}, u32[]{:S(2)}, u32[]{:S(2)}) collective-permute-start(f32[8,8,1024]{2,1,0:T(8,128)} %get-tuple-element.37), channel_id=1, source_target_pairs={{1,0},{2,1},{3,2},{4,3},{5,4},{6,5},{7,6},{9,8},{10,9},{11,10},{12... | collective-permute-start | bytes 786440 | tf_op jit(solution)/shard_map/ppermute | solution.py:341
  21.5 8.9 %copy-start.6 = (f32[8,8,1024]{2,1,0:T(8,128)}, f32[8,8,1024]{2,1,0:T(8,128)S(1)}, u32[]{:S(2)}) copy-start(f32[8,8,1024]{2,1,0:T(8,128)S(1)} %collective-permute-done.rad_lo) | copy-start | bytes 786436
  21.5 8.9 %copy-start.7 = (f32[8,8,1024]{2,1,0:T(8,128)}, f32[8,8,1024]{2,1,0:T(8,128)S(1)}, u32[]{:S(2)}) copy-start(f32[8,8,1024]{2,1,0:T(8,128)S(1)} %collective-permute-done.1.rad_hi) | copy-start | bytes 786436
  21.5 45.2 %collective-permute-start.2 = (f32[7,64,1024]{2,1,0:T(8,128)}, f32[7,64,1024]{2,1,0:T(8,128)S(1)}, u32[]{:S(2)}, u32[]{:S(2)}) collective-permute-start(f32[7,64,1024]{2,1,0:T(8,128)} %get-tuple-element.38), channel_id=1, source_target_pairs={{0,8},{8,16},{16,24},{24,32},{32,40},{40,48},{48,56},{56,64},{64,7... | collective-permute-start | bytes 5505032 | tf_op jit(solution)/shard_map/ppermute | solution.py:346
  22.9 43.8 %collective-permute-start.3 = (f32[7,64,1024]{2,1,0:T(8,128)}, f32[7,64,1024]{2,1,0:T(8,128)}, u32[]{:S(2)}, u32[]{:S(2)}) collective-permute-start(f32[7,64,1024]{2,1,0:T(8,128)} %get-tuple-element.39), channel_id=1, source_target_pairs={{8,0},{16,8},{24,16},{32,24},{40,32},{48,40},{56,48},{64,56},{72,6... | collective-permute-start | bytes 5505032 | tf_op jit(solution)/shard_map/ppermute | solution.py:347
  45.3 27.7 %all-to-all-start = ((f32[4,6,64,256]{3,2,1,0:T(8,128)}), f32[4,6,64,256]{3,2,1,0:T(8,128)S(1)}, u32[]{:S(2)}, u32[]{:S(2)}) async-start(f32[4,6,64,256]{3,2,1,0:T(8,128)} %rhs_2.1), calls=%async_computation | async-start | bytes 3145728 | tf_op jit(solution)/shard_map/all_to_all | solution.py:353
  66.7 6.3 %copy-start = (f32[7,64,1024]{2,1,0:T(8,128)}, f32[7,64,1024]{2,1,0:T(8,128)S(1)}, u32[]{:S(2)}) copy-start(f32[7,64,1024]{2,1,0:T(8,128)S(1)} %collective-permute-done.2.rest_0_) | copy-start | bytes 5505028
  73.0 4.4 %copy-start.4 = (f32[4,6,64,256]{3,2,1,0:T(8,128)}, f32[4,6,64,256]{3,2,1,0:T(8,128)S(1)}, u32[]{:S(2)}) copy-start(f32[4,6,64,256]{3,2,1,0:T(8,128)S(1)} %all-to-all-done.own_ref) | copy-start | bytes 4718596
  73.0 26.3 %all-to-all-start.1 = ((f32[4,6,64,256]{3,2,1,0:T(8,128)}), f32[4,6,64,256]{3,2,1,0:T(8,128)}, u32[]{:S(2)}, u32[]{:S(2)}) async-start(f32[4,6,64,256]{3,2,1,0:T(8,128)} %rhs_4.1), calls=%async_computation.1 | async-start | bytes 3145728 | tf_op jit(solution)/shard_map/all_to_all | solution.py:353
  77.4 38.6 %collective-permute-start.4 = (f32[4,6,64,256]{3,2,1,0:T(8,128)S(1)}, f32[4,6,64,256]{3,2,1,0:T(8,128)S(1)}, u32[]{:S(2)}, u32[]{:S(2)}) collective-permute-start(f32[4,6,64,256]{3,2,1,0:T(8,128)S(1)} %all-to-all-done.own_ref), channel_id=1, source_target_pairs={{0,1},{1,0},{2,3},{3,2},{4,5},{5,4},{6,7},{7,6},{8,9},{9,8},{10,11... | collective-permute-start | bytes 4718600 | tf_op jit(solution)/shard_map/ppermute | solution.py:358
  99.4 33.0 %all-to-all-start.2 = ((f32[4,6,64,256]{3,2,1,0:T(8,128)}), f32[4,6,64,256]{3,2,1,0:T(8,128)}, u32[]{:S(2)}, u32[]{:S(2)}) async-start(f32[4,6,64,256]{3,2,1,0:T(8,128)} %rhs_0.1), calls=%async_computation.2 | async-start | bytes 3145728 | tf_op jit(solution)/shard_map/all_to_all | solution.py:353
  116.0 16.3 %copy-start.8 = (f32[4,6,64,256]{3,2,1,0:T(8,128)}, f32[4,6,64,256]{3,2,1,0:T(8,128)S(1)}, u32[]{:S(2)}) copy-start(f32[4,6,64,256]{3,2,1,0:T(8,128)S(1)} %collective-permute-done.4.other_ref) | copy-start | bytes 4718596
  132.4 25.5 %all-to-all-start.3 = ((f32[4,6,64,256]{3,2,1,0:T(8,128)}), f32[4,6,64,256]{3,2,1,0:T(8,128)}, u32[]{:S(2)}, u32[]{:S(2)}) async-start(f32[4,6,64,256]{3,2,1,0:T(8,128)} %rhs_6.1), calls=%async_computation.3 | async-start | bytes 3145728 | tf_op jit(solution)/shard_map/all_to_all | solution.py:353
  136.8 39.2 %collective-permute-start.5 = (f32[4,6,64,256]{3,2,1,0:T(8,128)}, f32[4,6,64,256]{3,2,1,0:T(8,128)}, u32[]{:S(2)}, u32[]{:S(2)}) collective-permute-start(f32[4,6,64,256]{3,2,1,0:T(8,128)} %all-to-all-done.1.own_ref), channel_id=1, source_target_pairs={{0,1},{1,0},{2,3},{3,2},{4,5},{5,4},{6,7},{7,6},{8,9},{9,8},{10,11... | collective-permute-start | bytes 4718600 | tf_op jit(solution)/shard_map/ppermute | solution.py:358
  157.9 23.7 %all-to-all-start.4 = ((f32[4,6,64,256]{3,2,1,0:T(8,128)}), f32[4,6,64,256]{3,2,1,0:T(8,128)S(1)}, u32[]{:S(2)}, u32[]{:S(2)}) async-start(f32[4,6,64,256]{3,2,1,0:T(8,128)} %radial.7), calls=%async_computation.4 | async-start | bytes 3145728 | tf_op jit(solution)/shard_map/all_to_all | solution.py:353
  161.5 48.1 %collective-permute-start.7 = (f32[4,6,64,256]{3,2,1,0:T(8,128)}, f32[4,6,64,256]{3,2,1,0:T(8,128)S(1)}, u32[]{:S(2)}, u32[]{:S(2)}) collective-permute-start(f32[4,6,64,256]{3,2,1,0:T(8,128)} %all-to-all-done.2.own_ref), channel_id=1, source_target_pairs={{0,1},{1,0},{2,3},{3,2},{4,5},{5,4},{6,7},{7,6},{8,9},{9,8},{10,11... | collective-permute-start | bytes 4718600 | tf_op jit(solution)/shard_map/ppermute | solution.py:358
  181.6 1.2 copy-start.5
  182.7 32.0 %all-to-all-start.5 = ((f32[4,6,64,256]{3,2,1,0:T(8,128)}), f32[4,6,64,256]{3,2,1,0:T(8,128)S(1)}, u32[]{:S(2)}, u32[]{:S(2)}) async-start(f32[4,6,64,256]{3,2,1,0:T(8,128)} %radial.6), calls=%async_computation.5 | async-start | bytes 3145728 | tf_op jit(solution)/shard_map/all_to_all | solution.py:353
  186.3 56.0 %collective-permute-start.6 = (f32[4,6,64,256]{3,2,1,0:T(8,128)}, f32[4,6,64,256]{3,2,1,0:T(8,128)}, u32[]{:S(2)}, u32[]{:S(2)}) collective-permute-start(f32[4,6,64,256]{3,2,1,0:T(8,128)} %all-to-all-done.3.own_ref), channel_id=1, source_target_pairs={{0,1},{1,0},{2,3},{3,2},{4,5},{5,4},{6,7},{7,6},{8,9},{9,8},{10,11... | collective-permute-start | bytes 4718600 | tf_op jit(solution)/shard_map/ppermute | solution.py:358
  209.6 1.1 copy-start.9
  214.7 1.2 copy-start.1
  215.9 30.4 %all-to-all-start.6 = ((f32[4,6,64,256]{3,2,1,0:T(8,128)}), f32[4,6,64,256]{3,2,1,0:T(8,128)S(1)}, u32[]{:S(2)}, u32[]{:S(2)}) async-start(f32[4,6,64,256]{3,2,1,0:T(8,128)} %radial.5), calls=%async_computation.6 | async-start | bytes 3145728 | tf_op jit(solution)/shard_map/all_to_all | solution.py:353
  246.3 1.2 copy-start.2
  247.5 23.9 %all-to-all-start.7 = ((f32[4,6,64,256]{3,2,1,0:T(8,128)}), f32[4,6,64,256]{3,2,1,0:T(8,128)S(1)}, u32[]{:S(2)}, u32[]{:S(2)}) async-start(f32[4,6,64,256]{3,2,1,0:T(8,128)} %radial.4), calls=%async_computation.7 | async-start | bytes 3145728 | tf_op jit(solution)/shard_map/all_to_all | solution.py:353
  271.4 1.2 copy-start.3

commit v2 on v1

v2 whole, which is shorter than its diff:
```python
import functools

import jax
import jax.numpy as jnp
from jax import lax
from jax.experimental import pallas as pl
from jax.experimental.pallas import tpu as pltpu
from jax.sharding import PartitionSpec as P

COEF = 0.25
F32 = jnp.float32
BF16 = jnp.bfloat16
CHUNKS = ((2, 3), (4, 5), (0, 1), (6, 7))
RADIAL_BYTES = (8 * 1024 * 1024, 1024, 1024, 1024)
HALF_BYTES = 200 * 1024 * 1024
COLUMNS = 256
VMEM_LIMIT = 56 * 1024 * 1024


def split(x):
    hi = x.astype(BF16)
    return hi, (x - hi.astype(F32)).astype(BF16)


def dot3(a_hi, a_lo, b_hi, b_lo, dims):
    dot = functools.partial(
        lax.dot_general, dimension_numbers=(dims, ((), ())), preferred_element_type=F32
    )
    return dot(a_hi, b_hi) + (dot(a_hi, b_lo) + dot(a_lo, b_hi))


def split_kernel(x_ref, hi_ref, lo_ref):
    hi_ref[...], lo_ref[...] = split(x_ref[...].T)


def split_call(x):
    rows, cols = x.shape
    spec = pl.BlockSpec((256, cols), lambda i: (i, 0))
    return pl.pallas_call(
        split_kernel,
        name=f"split_{rows}",
        grid=(rows // 256,),
        in_specs=[spec],
        out_specs=[pl.BlockSpec((cols, 256), lambda i: (0, i))] * 2,
        out_shape=[jax.ShapeDtypeStruct((cols, rows), BF16)] * 2,
    )(x)


def rhs_kernel(
    groups, edge, inv_dx, inv_dr, inv_rt, velocity, viscosity, rad_lo, rad_hi, *rest
):
    if edge:
        ax_lo, ax_hi, az_hi, az_lo, *outs = rest
    else:
        az_hi, az_lo, *outs = rest
    *outs, vbuf, nbuf, rhs, hi, lo, sems = outs
    planes, rows, nt = viscosity.shape
    width = outs[0].shape[3]
    copies = []

    def bring(source, target):
        copy = pltpu.make_async_copy(source, target, sems.at[len(copies)])
        copy.start()
        copies.append(copy)

    chosen = [p for group in groups for p in group]
    first, last = max(min(chosen) - 2, 0), min(max(chosen) + 3, planes)
    inner, mine = pl.ds(8, rows), pl.ds(first, last - first)
    held = pl.ds(first + 2, last - first)
    for c in range(3):
        bring(velocity.at[c, mine], vbuf.at[c, held, inner])
    bring(viscosity.at[mine], nbuf.at[held, inner])
    if edge:
        for halo, at, thin in ((ax_lo, 0, 1), (ax_hi, planes + 2, planes + 2)):
            for c in range(3):
                bring(halo.at[pl.ds(2 * c, 2)], vbuf.at[c, pl.ds(at, 2), inner])
            bring(halo.at[6], nbuf.at[thin, inner])
    for copy in copies:
        copy.wait()

    def stencil(place, p):
        at = p + 2
        low, high = rad_lo[p], rad_hi[p]
        for c in range(3):
            vbuf[c, at, 0:8, :] = pltpu.roll(low, 6 - 2 * c, 0)
            vbuf[c, at, rows + 8 : rows + 16, :] = pltpu.roll(high, (8 - 2 * c) % 8, 0)
        nbuf[at, 0:8, :] = pltpu.roll(low, 1, 0)
        nbuf[at, rows + 8 : rows + 16, :] = pltpu.roll(high, 2, 0)
        gx = inv_dx[p]

        def strip(i, carry):
            r0 = pl.multiple_of(i * 8, 8)
            mid = pl.ds(pl.multiple_of(r0 + 8, 8), 8)
            wide = pl.ds(r0, 24)
            metrics = (gx, inv_rt[pl.ds(r0, 8), :], inv_dr[pl.ds(r0, 8), :])
            metrics = tuple(
                (g, (0.5 * COEF) * g * g, (COEF / 12.0) * g) for g in metrics
            )
            for l0 in range(0, nt, COLUMNS):
                cols = pl.ds(l0, COLUMNS)
                before, behind = pl.ds((l0 - 128) % nt, 128), pl.ds((l0 + COLUMNS) % nt, 128)

                def turned(ref, *shifts):
                    ext = jnp.concatenate(
                        [ref[mid, before], ref[mid, cols], ref[mid, behind]], axis=1
                    )
                    size = COLUMNS + 256
                    return [
                        pltpu.roll(ext, shift % size, 1)[:, 128 : 128 + COLUMNS]
                        for shift in shifts
                    ]

                nu24 = nbuf[at, wide, cols]
                nu = nu24[8:16]
                nus = (
                    (nbuf[at + 1, mid, cols], nbuf[at - 1, mid, cols]),
                    turned(nbuf.at[at], -1, 1),
                    (nu24[9:17], nu24[7:15]),
                )
                coefs = []
                centre = None
                for d, ((up, down), (_, gg, g12)) in enumerate(zip(nus, metrics)):
                    a_up = gg * (nu + up)
                    a_down = gg * (nu + down)
                    b = g12 * vbuf[d, at, mid, cols]
                    b8 = 8.0 * b
                    total = a_up + a_down
                    centre = total if centre is None else centre + total
                    coefs.append((a_up - b8, a_down + b8, b))
                centre = 1.0 - centre
                for c in range(3):
                    q24 = vbuf[c, at, wide, cols]
                    near = (
                        [vbuf[c, at + k, mid, cols] for k in (1, -1, 2, -2)],
                        turned(vbuf.at[c, at], -1, 1, -2, 2),
                        [q24[8 + k : 16 + k] for k in (1, -1, 2, -2)],
                    )
                    total = centre * q24[8:16]
                    for (up, down, up2, down2), (c_up, c_down, b) in zip(near, coefs):
                        total = total + (c_up * up + c_down * down + b * (up2 - down2))
                    rhs[c, place, pl.ds(r0, 8), cols] = total
            return carry

        lax.fori_loop(0, rows // 8, strip, 0)

    for group, out in zip(groups, outs):
        size = len(group)

        def plane(j, carry):
            stencil(j, group[0] + j)
            return carry

        lax.fori_loop(0, size, plane, 0)
        lines = size * rows
        for c in range(3):
            part = pl.ds(c * lines, lines)
            hi[part, :], lo[part, :] = split(rhs[c, 0:size].reshape(lines, nt))
        for d in range(nt // width):
            cols = pl.ds(d * width, width)
            solved = dot3(
                hi[0 : 3 * lines, :], lo[0 : 3 * lines, :], az_hi[:, cols], az_lo[:, cols],
                ((1,), (0,)),
            )
            out[d] = solved.reshape(3 * size, rows, width)


def rhs_call(groups, parts, inv_dx, inv_dr, inv_rt, velocity, viscosity, rad_lo, rad_hi, ax, az):
    rows, nt = velocity.shape[2], velocity.shape[3]
    anywhere = pl.BlockSpec(memory_space=pl.ANY)
    vmem = pl.BlockSpec(memory_space=pltpu.VMEM)
    most = max(len(group) for group in groups)
    return pl.pallas_call(
        functools.partial(rhs_kernel, groups, bool(ax)),
        name=f"rhs_{groups[0][0]}",
        in_specs=[pl.BlockSpec(memory_space=pltpu.SMEM), vmem, vmem, anywhere, anywhere, vmem, vmem]
        + [anywhere] * len(ax)
        + [vmem, vmem],
        out_specs=[vmem] * len(groups),
        out_shape=[
            jax.ShapeDtypeStruct((parts, 3 * len(group), rows, nt // parts), F32)
            for group in groups
        ],
        scratch_shapes=[
            pltpu.VMEM((3, 12, rows + 16, nt), F32),
            pltpu.VMEM((12, rows + 16, nt), F32),
            pltpu.VMEM((3, most, rows, nt), F32),
            pltpu.VMEM((3 * most * rows, nt), BF16),
            pltpu.VMEM((3 * most * rows, nt), BF16),
            pltpu.SemaphoreType.DMA((12,)),
        ],
        compiler_params=pltpu.CompilerParams(vmem_limit_bytes=VMEM_LIMIT),
        cost_estimate=pl.CostEstimate(flops=1024, bytes_accessed=1024, transcendentals=0),
    )(inv_dx, inv_dr[:, None], inv_rt[:, None], velocity, viscosity, rad_lo, rad_hi, *ax, *az)


def half_kernel(side_ref, x_ref, hi_ref, lo_ref):
    rows = x_ref.shape[0] // 8
    side = side_ref[0]
    for part in range(4):
        x = x_ref[pl.ds(pl.multiple_of(part * 2 * rows + side * rows, rows), rows), :]
        swapped = jnp.concatenate(
            [
                pltpu.roll(x[:, at : at + 2 * rows], rows, 1)
                for at in range(0, x.shape[1], 2 * rows)
            ],
            axis=1,
        )
        at = slice(part * rows, (part + 1) * rows)
        hi_ref[at, :], lo_ref[at, :] = split(jnp.where(side == 0, x, swapped))


def half_call(side, x):
    rows, cols = x.shape
    vmem = pl.BlockSpec(memory_space=pltpu.VMEM)
    return pl.pallas_call(
        half_kernel,
        name="half",
        in_specs=[pl.BlockSpec(memory_space=pltpu.SMEM), vmem],
        out_specs=[vmem, vmem],
        out_shape=[jax.ShapeDtypeStruct((rows // 2, cols), BF16)] * 2,
        cost_estimate=pl.CostEstimate(
            flops=0, bytes_accessed=HALF_BYTES, transcendentals=0
        ),
    )(side, x)


def radial_kernel(r_hi, r_lo, own_ref, other_ref, out_ref):
    parts, slabs, rows, width = own_ref.shape
    x = jnp.concatenate(
        [
            jnp.concatenate(
                [ref[part, s] for part in range(parts) for ref in (own_ref, other_ref)], axis=0
            )
            for s in range(slabs)
        ],
        axis=1,
    )
    hi, lo = split(x)
    y = dot3(r_hi[...], r_lo[...], hi, lo, ((1,), (0,)))
    for s in range(slabs):
        out_ref[:, s] = y[:, s * width : (s + 1) * width].reshape(parts, rows, width)


def radial_call(rad, own, other, moved):
    parts, slabs, rows, width = own.shape
    step = 3
    block = pl.BlockSpec((parts, step, rows, width), lambda i: (0, i, 0, 0))
    full = pl.BlockSpec(rad[0].shape, lambda i: (0, 0))
    return pl.pallas_call(
        radial_kernel,
        name="radial",
        grid=(slabs // step,),
        in_specs=[full, full, block, block],
        out_specs=block,
        out_shape=jax.ShapeDtypeStruct(own.shape, F32),
        compiler_params=pltpu.CompilerParams(vmem_limit_bytes=VMEM_LIMIT),
        cost_estimate=pl.CostEstimate(
            flops=1024,
            bytes_accessed=moved,
            transcendentals=0,
        ),
    )(*rad, own, other)


def place_kernel(x_ref, *rest):
    out_ref = rest[-1]
    parts, width = x_ref.shape[0], x_ref.shape[4]
    for d in range(parts):
        for c in range(3):
            out_ref[c, 0, :, d * width : (d + 1) * width] = x_ref[d, c, 0]


def place_call(planes, x, whole, shape):
    parts, slabs, rows, width = x.shape
    first = planes[0]
    aliased = () if whole is None else (whole,)
    return pl.pallas_call(
        place_kernel,
        name="place",
        grid=(len(planes),),
        in_specs=[pl.BlockSpec((parts, 3, 1, rows, width), lambda j: (0, 0, j, 0, 0))]
        + [pl.BlockSpec(memory_space=pl.ANY)] * len(aliased),
        out_specs=pl.BlockSpec((3, 1, rows, parts * width), lambda j: (0, first + j, 0, 0)),
        out_shape=jax.ShapeDtypeStruct(shape, F32),
        input_output_aliases={1: 0} if aliased else {},
        cost_estimate=pl.CostEstimate(flops=0, bytes_accessed=8 * x.size, transcendentals=0),
    )(x.reshape(parts, 3, slabs // 3, rows, width), *aliased)


def line_kernel(velocity, viscosity, top, bottom, edges, sems):
    planes, rows = viscosity.shape[0], viscosity.shape[1]
    copies = []
    for side, at in enumerate((rows - 8, 0)):
        for f in range(4):
            source = velocity.at[f, :, pl.ds(at, 8)] if f < 3 else viscosity.at[:, pl.ds(at, 8)]
            copies.append(
                pltpu.make_async_copy(source, edges.at[side, f], sems.at[len(copies)])
            )
    for copy in copies:
        copy.start()
    for copy in copies:
        copy.wait()
    row = lax.broadcasted_iota(jnp.int32, edges.shape[3:], 0)
    for p in range(planes):
        for side, out, turns in ((0, top, (2, 4, 6, 7)), (1, bottom, (0, 2, 4, 6))):
            strips = [
                pltpu.roll(edges[side, f, p], turn, 0) if turn else edges[side, f, p]
                for f, turn in enumerate(turns)
            ]
            out[p] = jnp.where(
                row < 4,
                jnp.where(row < 2, strips[0], strips[1]),
                jnp.where(row < 6, strips[2], strips[3]),
            )


def line_call(velocity, viscosity):
    planes, _, nt = viscosity.shape
    anywhere = pl.BlockSpec(memory_space=pl.ANY)
    vmem = pl.BlockSpec(memory_space=pltpu.VMEM)
    return pl.pallas_call(
        line_kernel,
        name="lines",
        in_specs=[anywhere, anywhere],
        out_specs=[vmem, vmem],
        out_shape=[jax.ShapeDtypeStruct((planes, 8, nt), F32)] * 2,
        scratch_shapes=[pltpu.VMEM((2, 4, planes, 8, nt), F32), pltpu.SemaphoreType.DMA((8,))],
        compiler_params=pltpu.CompilerParams(vmem_limit_bytes=VMEM_LIMIT),
    )(velocity, viscosity)


def face_kernel(velocity, viscosity, top, bottom, sems):
    planes = viscosity.shape[0]
    copies = []
    for out, at, thin in ((top, planes - 2, planes - 1), (bottom, 0, 0)):
        for f in range(4):
            source = velocity.at[f, pl.ds(at, 2)] if f < 3 else viscosity.at[pl.ds(thin, 1)]
            target = out.at[pl.ds(2 * f, 2 if f < 3 else 1)]
            copies.append(pltpu.make_async_copy(source, target, sems.at[len(copies)]))
    for copy in copies:
        copy.start()
    for copy in copies:
        copy.wait()


def face_call(velocity, viscosity):
    _, rows, nt = viscosity.shape
    anywhere = pl.BlockSpec(memory_space=pl.ANY)
    vmem = pl.BlockSpec(memory_space=pltpu.VMEM)
    return pl.pallas_call(
        face_kernel,
        name="faces",
        in_specs=[anywhere, anywhere],
        out_specs=[vmem, vmem],
        out_shape=[jax.ShapeDtypeStruct((7, rows, nt), F32)] * 2,
        scratch_shapes=[pltpu.SemaphoreType.DMA((8,))],
        compiler_params=pltpu.CompilerParams(vmem_limit_bytes=VMEM_LIMIT),
    )(velocity, viscosity)


def after(x, *events):
    return lax.optimization_barrier((x, *events))[0]


def local(velocity, viscosity, inv_dx, inv_dr, inv_rt, az_inverse, rad_inverse):
    planes = velocity.shape[1]
    lines = lax.axis_size("rad")
    parts = lines // 2
    side = (lax.axis_index("rad") % 2).astype(jnp.int32).reshape(1)

    def shifts(axis):
        count = lax.axis_size(axis)
        forward = [(i, i + 1) for i in range(count - 1)]
        return forward, [(b, a) for a, b in forward]

    rad_top, rad_bottom = line_call(velocity, viscosity)
    forward, backward = shifts("rad")
    rad_lo = lax.ppermute(rad_top, "rad", forward)
    rad_hi = lax.ppermute(rad_bottom, "rad", backward)
    ax_top, ax_bottom = face_call(velocity, after(viscosity, rad_top))
    az = split_call(after(az_inverse, ax_top))
    rad = half_call(after(side, az[0]), rad_inverse)
    forward, backward = shifts("ax")
    ax_top, ax_bottom, rad_lo, rad_hi, *_ = lax.optimization_barrier(
        (ax_top, ax_bottom, rad_lo, rad_hi, az[0], rad[0])
    )
    ax_lo = lax.ppermute(ax_top, "ax", forward)
    ax_hi = lax.ppermute(ax_bottom, "ax", backward)
    groups = [list(range(0, lines, 2)), list(range(1, lines, 2))]

    def exchange(x):
        return lax.all_to_all(
            x, "rad", split_axis=0, concat_axis=0, tiled=True, axis_index_groups=groups
        )

    def partner(x):
        return lax.ppermute(x, "rad", [(i, i ^ 1) for i in range(lines)])

    common = (inv_dr, inv_rt, velocity, viscosity, rad_lo, rad_hi)
    (first,) = rhs_call(CHUNKS[:1], parts, inv_dx, *common, (), az)
    (second,) = rhs_call(CHUNKS[1:2], parts, after(inv_dx, first), *common, (), az)
    second, ax_lo, ax_hi = lax.optimization_barrier((second, ax_lo, ax_hi))
    own = [exchange(first)]
    other = [partner(after(own[0], ax_lo))]
    own.append(exchange(after(second, own[0])))
    edges = rhs_call(CHUNKS[2:], parts, after(inv_dx, own[0]), *common, (ax_lo, ax_hi), az)
    other.append(partner(after(own[1], edges[0])))
    solved = [radial_call(rad, own[k], other[k], RADIAL_BYTES[k]) for k in range(2)]
    own.append(exchange(after(edges[0], own[1])))
    own.append(exchange(after(edges[1], own[2], solved[0])))
    back = [exchange(after(solved[0], own[3], other[1]))]
    for k in range(2, len(CHUNKS)):
        other.append(partner(after(own[k], other[k - 2])))
        solved.append(radial_call(rad, own[k], other[k], RADIAL_BYTES[k]))
    whole = place_call(CHUNKS[0], back[0], None, velocity.shape)
    for k in range(1, len(CHUNKS)):
        back.append(exchange(after(solved[k], back[-1])))
        whole = place_call(CHUNKS[k], back[k], whole, velocity.shape)
    return whole


def solution(mesh):
    placed = (
        P(None, "ax", "rad", None),
        P("ax", "rad", None),
        P("ax"),
        P("rad"),
        P("rad"),
        P(),
        P(),
    )
    return jax.shard_map(
        local, mesh=mesh, in_specs=placed, out_specs=P(None, "ax", "rad", None), check_vma=False
    )
```

time: 276 us -> 254 us (0.920)
  Pallas kernels: 99.7 us -> 87.5 us
  waiting for transfers between devices: 116 us -> 110 us
    all_to_all x8, waiting for transfers between devices: 37.8 us -> 50 us  [exchange(): lax.all_to_all(x, 'rad', split_axis=0, concat_axis=0, tiled=True, axis_in...]
    pallas_call x5, Pallas kernels: 66.7 us -> 54.6 us  [the longest x3 48.2 us: rhs_call(): pl.pallas_call(functools.partial(rhs_kernel, groups, bool(ax)), name=f'rh...]
    ppermute x1, waiting for transfers between devices: 10.2 us -> 0.01 us  [local(): rad_lo = lax.ppermute(rad_top, 'rad', forward)]
    ppermute x4, waiting for transfers between devices: 67.7 us -> 60.1 us  [partner(): return lax.ppermute(x, 'rad', [(i, i ^ 1) for i in range(lines)])]
    all_to_all x8, starting transfers between devices: 35.9 us -> 31.9 us  [exchange(): lax.all_to_all(x, 'rad', split_axis=0, concat_axis=0, tiled=True, axis_in...]
    unnamed x24 -> x20, local copies, waits for them, and re-layouts: 5.91 us -> 3.59 us
  transfers between devices with their start and end apart: 16 -> 16, of which waited for: 10 -> 10; matrix products, arithmetic and copies ran while one was open for 1% -> 1% of each run, Pallas kernels for 34% -> 33%
where the time goes in v2:
time: 254 us; the launch traced here: 252 us
  waiting for transfers between devices  110 us (43%)
  Pallas kernels  87.5 us (34%)
  starting transfers between devices  49.5 us (19%)
  local copies, waits for them, and re-layouts  4.99 us (2%)
    ppermute x4, waiting for transfers between devices, partner(): return lax.ppermute(x, 'rad', [(i, i ^ 1) for i in range(lines)])  60.1 us
    all_to_all x8, waiting for transfers between devices, exchange(): lax.all_to_all(x, 'rad', split_axis=0, concat_axis=0, tiled=True, axis_in...  50 us
    pallas_call x3, Pallas kernels, rhs_call(): pl.pallas_call(functools.partial(rhs_kernel, groups, bool(ax)), name=f'rh...  48.2 us
    all_to_all x8, starting transfers between devices, exchange(): lax.all_to_all(x, 'rad', split_axis=0, concat_axis=0, tiled=True, axis_in...  31.9 us
    pallas_call x4, Pallas kernels, radial_call(): pl.pallas_call(radial_kernel, name='radial', grid=(slabs // step,), in_sp...  16.1 us
    pallas_call x4, Pallas kernels, place_call(): pl.pallas_call(place_kernel, name='place', grid=(len(planes),), in_specs=...  9.3 us
    ppermute x4, starting transfers between devices, partner(): return lax.ppermute(x, 'rad', [(i, i ^ 1) for i in range(lines)])  6.43 us
    ppermute x1, starting transfers between devices, local(): rad_lo = lax.ppermute(rad_top, 'rad', forward)  6.07 us
  transfers between devices with their start and end apart: 16, of which 10 were waited for; matrix products, arithmetic and copies ran while one was open for 1% of the time, Pallas kernels for 33%

profile of v2, /device:TPU:0, one launch (start us, length us, event | category | flops | bytes accessed | tf_op | source)
XLA Modules:
  0.0 252.4 jit_solution(8156814081339019786)
XLA Ops:
  0.0 2.5 lines.1
  2.5 1.3 collective-permute-start.1
  3.8 6.1 %collective-permute-start = (f32[8,8,1024]{2,1,0:T(8,128)}, f32[8,8,1024]{2,1,0:T(8,128)S(1)}, u32[]{:S(2)}, u32[]{:S(2)}) collective-permute-start(f32[8,8,1024]{2,1,0:T(8,128)} %get-tuple-element.38), channel_id=1, source_target_pairs={{0,1},{1,2},{2,3},{3,4},{4,5},{5,6},{6,7},{8,9},{9,10},{10,11},{11... | collective-permute-start | bytes 786440 | tf_op jit(solution)/shard_map/ppermute | solution.py:378
  9.9 3.9 %faces.1 = (f32[7,64,1024]{2,1,0:T(8,128)}, f32[7,64,1024]{2,1,0:T(8,128)}) custom-call(f32[3,8,64,1024]{3,2,1,0:T(8,128)} %velocity.9, f32[8,64,1024]{2,1,0:T(8,128)} %viscosity.8), custom_call_target="tpu_custom_call" | custom-call | tf_op jit(solution)/shard_map/faces/pallas_call | solution.py:350
  13.8 0.0 copy-start.8
  13.8 0.0 copy-start.9
  13.8 5.3 %split_1024.1 = (bf16[1024,1024]{1,0:T(8,128)(2,1)}, bf16[1024,1024]{1,0:T(8,128)(2,1)}) custom-call(f32[1024,1024]{1,0:T(8,128)} %x_ref.1), custom_call_target="tpu_custom_call" | custom-call | tf_op jit(solution)/shard_map/split_1024/pallas_call | solution.py:39
  19.2 2.2 half.1
  21.4 0.0 collective-permute-done.1.rad_hi
  21.4 2.6 %collective-permute-start.2 = (f32[7,64,1024]{2,1,0:T(8,128)}, f32[7,64,1024]{2,1,0:T(8,128)}, u32[]{:S(2)}, u32[]{:S(2)}) collective-permute-start(f32[7,64,1024]{2,1,0:T(8,128)} %get-tuple-element.53), channel_id=1, source_target_pairs={{0,8},{8,16},{16,24},{24,32},{32,40},{40,48},{48,56},{56,64},{64,7... | collective-permute-start | bytes 5505032 | tf_op jit(solution)/shard_map/ppermute | solution.py:387
  24.0 1.3 collective-permute-start.3
  25.3 0.7 copy.11.inv_dr
  26.0 0.7 copy.12.inv_rt
  26.7 13.3 %rhs_2.1 = f32[4,6,64,256]{3,2,1,0:T(8,128)} custom-call(f32[8]{0:T(128)} %inv_dx.3, f32[64,1]{1,0:T(8,128)} %copy.11.inv_dr, f32[64,1]{1,0:T(8,128)} %copy.12.inv_rt, f32[3,8,64,1024]{3,2,1,0:T(8,128)} %velocity.9, f32[8,64,1024]{2,1,0:T(8,128)} %viscosity.8, f32[8,8,1024]{2,1,0:T(8,128)} %copy-done.7, f32[8,8,1024]{2,1,0:T(8,128)} %copy-done.6, ...), custom_call_target="tpu_custom_call" | custom-call | flops 1024 | bytes 1024 | tf_op jit(solution)/shard_map/rhs_2/pallas_call | solution.py:172
  40.0 4.4 %all-to-all-start = ((f32[4,6,64,256]{3,2,1,0:T(8,128)}), f32[4,6,64,256]{3,2,1,0:T(8,128)}, u32[]{:S(2)}, u32[]{:S(2)}) async-start(f32[4,6,64,256]{3,2,1,0:T(8,128)} %rhs_2.1), calls=%async_computation | async-start | bytes 3145728 | tf_op jit(solution)/shard_map/all_to_all | solution.py:392
  44.4 13.3 %rhs_4.1 = f32[4,6,64,256]{3,2,1,0:T(8,128)} custom-call(f32[8]{0:T(128)} %inv_dx.3, f32[64,1]{1,0:T(8,128)} %copy.11.inv_dr, f32[64,1]{1,0:T(8,128)} %copy.12.inv_rt, f32[3,8,64,1024]{3,2,1,0:T(8,128)} %velocity.9, f32[8,64,1024]{2,1,0:T(8,128)} %viscosity.8, f32[8,8,1024]{2,1,0:T(8,128)} %copy-done.7, f32[8,8,1024]{2,1,0:T(8,128)} %copy-done.6, ...), custom_call_target="tpu_custom_call" | custom-call | flops 1024 | bytes 1024 | tf_op jit(solution)/shard_map/rhs_4/pallas_call | solution.py:172
  57.7 8.2 %all-to-all-done.own_ref = f32[4,6,64,256]{3,2,1,0:T(8,128)} async-done(((f32[4,6,64,256]{3,2,1,0:T(8,128)}), f32[4,6,64,256]{3,2,1,0:T(8,128)}, u32[]{:S(2)}, u32[]{:S(2)}) %all-to-all-start) | async-done | bytes 1572896 | tf_op jit(solution)/shard_map/all_to_all | solution.py:392
  65.9 3.6 %all-to-all-start.1 = ((f32[4,6,64,256]{3,2,1,0:T(8,128)}), f32[4,6,64,256]{3,2,1,0:T(8,128)S(1)}, u32[]{:S(2)}, u32[]{:S(2)}) async-start(f32[4,6,64,256]{3,2,1,0:T(8,128)} %rhs_4.1), calls=%async_computation.1 | async-start | bytes 3145728 | tf_op jit(solution)/shard_map/all_to_all | solution.py:392
  69.5 4.6 %collective-permute-start.4 = (f32[4,6,64,256]{3,2,1,0:T(8,128)}, f32[4,6,64,256]{3,2,1,0:T(8,128)}, u32[]{:S(2)}, u32[]{:S(2)}) collective-permute-start(f32[4,6,64,256]{3,2,1,0:T(8,128)} %all-to-all-done.own_ref), channel_id=1, source_target_pairs={{0,1},{1,0},{2,3},{3,2},{4,5},{5,4},{6,7},{7,6},{8,9},{9,8},{10,11... | collective-permute-start | bytes 4718600 | tf_op jit(solution)/shard_map/ppermute | solution.py:397
  74.0 21.6 %rhs_0.1 = (f32[4,6,64,256]{3,2,1,0:T(8,128)}, f32[4,6,64,256]{3,2,1,0:T(8,128)}) custom-call(f32[8]{0:T(128)} %inv_dx.3, f32[64,1]{1,0:T(8,128)} %copy.11.inv_dr, f32[64,1]{1,0:T(8,128)} %copy.12.inv_rt, f32[3,8,64,1024]{3,2,1,0:T(8,128)} %velocity.9, f32[8,64,1024]{2,1,0:T(8,128)} %viscosity.8, f32[8,8,1024]{2,1,0:T(8,128)} %copy-done.7, ...), custom_call_target="tpu_custom_call" | custom-call | flops 1024 | bytes 1024 | tf_op jit(solution)/shard_map/rhs_0/pallas_call | solution.py:172
  95.7 4.7 %all-to-all-start.2 = ((f32[4,6,64,256]{3,2,1,0:T(8,128)}), f32[4,6,64,256]{3,2,1,0:T(8,128)S(1)}, u32[]{:S(2)}, u32[]{:S(2)}) async-start(f32[4,6,64,256]{3,2,1,0:T(8,128)} %get-tuple-element.61), calls=%async_computation.2 | async-start | bytes 3145728 | tf_op jit(solution)/shard_map/all_to_all | solution.py:392
  100.4 8.7 %collective-permute-done.4.other_ref = f32[4,6,64,256]{3,2,1,0:T(8,128)} collective-permute-done((f32[4,6,64,256]{3,2,1,0:T(8,128)}, f32[4,6,64,256]{3,2,1,0:T(8,128)}, u32[]{:S(2)}, u32[]{:S(2)}) %collective-permute-start.4) | collective-permute-done | bytes 1572896 | tf_op jit(solution)/shard_map/ppermute | solution.py:397
  109.1 4.0 %radial.4 = f32[4,6,64,256]{3,2,1,0:T(8,128)} custom-call(bf16[256,512]{1,0:T(8,128)(2,1)} %get-tuple-element.44.r_hi, bf16[256,512]{1,0:T(8,128)(2,1)} %get-tuple-element.45.r_lo, f32[4,6,64,256]{3,2,1,0:T(8,128)} %all-to-all-done.own_ref, f32[4,6,64,256]{3,2,1,0:T(8,128)} %collective-permute-done.4.other_ref), custom_call_target="tpu_custom_call" | custom-call | flops 1024 | bytes 8388608 | tf_op jit(solution)/shard_map/radial/pallas_call | solution.py:249
  113.1 9.0 %all-to-all-done.2.own_ref = f32[4,6,64,256]{3,2,1,0:T(8,128)S(1)} async-done(((f32[4,6,64,256]{3,2,1,0:T(8,128)}), f32[4,6,64,256]{3,2,1,0:T(8,128)S(1)}, u32[]{:S(2)}, u32[]{:S(2)}) %all-to-all-start.2) | async-done | bytes 1572896 | tf_op jit(solution)/shard_map/all_to_all | solution.py:392
  122.1 4.4 %all-to-all-start.3 = ((f32[4,6,64,256]{3,2,1,0:T(8,128)}), f32[4,6,64,256]{3,2,1,0:T(8,128)}, u32[]{:S(2)}, u32[]{:S(2)}) async-start(f32[4,6,64,256]{3,2,1,0:T(8,128)} %get-tuple-element.63), calls=%async_computation.3 | async-start | bytes 3145728 | tf_op jit(solution)/shard_map/all_to_all | solution.py:392
  126.4 16.3 %collective-permute-done.5.other_ref = f32[4,6,64,256]{3,2,1,0:T(8,128)} collective-permute-done((f32[4,6,64,256]{3,2,1,0:T(8,128)S(1)}, f32[4,6,64,256]{3,2,1,0:T(8,128)}, u32[]{:S(2)}, u32[]{:S(2)}) %collective-permute-start.5) | collective-permute-done | bytes 1572896 | tf_op jit(solution)/shard_map/ppermute | solution.py:397
  142.8 4.8 %all-to-all-done.3.own_ref = f32[4,6,64,256]{3,2,1,0:T(8,128)} async-done(((f32[4,6,64,256]{3,2,1,0:T(8,128)}), f32[4,6,64,256]{3,2,1,0:T(8,128)}, u32[]{:S(2)}, u32[]{:S(2)}) %all-to-all-start.3) | async-done | bytes 1572896 | tf_op jit(solution)/shard_map/all_to_all | solution.py:392
  147.5 3.6 %all-to-all-start.4 = ((f32[4,6,64,256]{3,2,1,0:T(8,128)}), f32[4,6,64,256]{3,2,1,0:T(8,128)S(1)}, u32[]{:S(2)}, u32[]{:S(2)}) async-start(f32[4,6,64,256]{3,2,1,0:T(8,128)} %radial.4), calls=%async_computation.4 | async-start | bytes 3145728 | tf_op jit(solution)/shard_map/all_to_all | solution.py:392
  151.1 0.6 collective-permute-start.7
  151.7 4.0 %radial.7 = f32[4,6,64,256]{3,2,1,0:T(8,128)} custom-call(bf16[256,512]{1,0:T(8,128)(2,1)} %get-tuple-element.44.r_hi, bf16[256,512]{1,0:T(8,128)(2,1)} %get-tuple-element.45.r_lo, f32[4,6,64,256]{3,2,1,0:T(8,128)} %copy-done.3, f32[4,6,64,256]{3,2,1,0:T(8,128)} %collective-permute-done.5.other_ref), custom_call_target="tpu_custom_call" | custom-call | flops 1024 | bytes 1024 | tf_op jit(solution)/shard_map/radial/pallas_call | solution.py:249
  155.8 15.5 %all-to-all-done.4 = f32[4,6,64,256]{3,2,1,0:T(8,128)S(1)} async-done(((f32[4,6,64,256]{3,2,1,0:T(8,128)}), f32[4,6,64,256]{3,2,1,0:T(8,128)S(1)}, u32[]{:S(2)}, u32[]{:S(2)}) %all-to-all-start.4) | async-done | bytes 1572896 | tf_op jit(solution)/shard_map/all_to_all | solution.py:392
  171.2 1.1 copy-done.5
  172.4 3.6 %all-to-all-start.5 = ((f32[4,6,64,256]{3,2,1,0:T(8,128)}), f32[4,6,64,256]{3,2,1,0:T(8,128)S(1)}, u32[]{:S(2)}, u32[]{:S(2)}) async-start(f32[4,6,64,256]{3,2,1,0:T(8,128)} %radial.7), calls=%async_computation.5 | async-start | bytes 3145728 | tf_op jit(solution)/shard_map/all_to_all | solution.py:392
  175.9 1.2 collective-permute-start.6
  177.2 13.1 %collective-permute-done.7.other_ref = f32[4,6,64,256]{3,2,1,0:T(8,128)} collective-permute-done((f32[4,6,64,256]{3,2,1,0:T(8,128)S(1)}, f32[4,6,64,256]{3,2,1,0:T(8,128)}, u32[]{:S(2)}, u32[]{:S(2)}) %collective-permute-start.7) | collective-permute-done | bytes 1572896 | tf_op jit(solution)/shard_map/ppermute | solution.py:397
  190.3 4.0 %radial.6 = f32[4,6,64,256]{3,2,1,0:T(8,128)} custom-call(bf16[256,512]{1,0:T(8,128)(2,1)} %get-tuple-element.44.r_hi, bf16[256,512]{1,0:T(8,128)(2,1)} %get-tuple-element.45.r_lo, f32[4,6,64,256]{3,2,1,0:T(8,128)} %copy-done.4, f32[4,6,64,256]{3,2,1,0:T(8,128)} %collective-permute-done.7.other_ref), custom_call_target="tpu_custom_call" | custom-call | flops 1024 | bytes 1024 | tf_op jit(solution)/shard_map/radial/pallas_call | solution.py:249
  194.3 0.9 all-to-all-done.5
  195.3 1.2 copy-done
  196.5 3.6 %all-to-all-start.6 = ((f32[4,6,64,256]{3,2,1,0:T(8,128)}), f32[4,6,64,256]{3,2,1,0:T(8,128)S(1)}, u32[]{:S(2)}, u32[]{:S(2)}) async-start(f32[4,6,64,256]{3,2,1,0:T(8,128)} %radial.6), calls=%async_computation.6 | async-start | bytes 3145728 | tf_op jit(solution)/shard_map/all_to_all | solution.py:392
  200.0 21.9 %collective-permute-done.6.other_ref = f32[4,6,64,256]{3,2,1,0:T(8,128)} collective-permute-done((f32[4,6,64,256]{3,2,1,0:T(8,128)}, f32[4,6,64,256]{3,2,1,0:T(8,128)}, u32[]{:S(2)}, u32[]{:S(2)}) %collective-permute-start.6) | collective-permute-done | bytes 1572896 | tf_op jit(solution)/shard_map/ppermute | solution.py:397
  222.0 4.0 %radial.5 = f32[4,6,64,256]{3,2,1,0:T(8,128)} custom-call(bf16[256,512]{1,0:T(8,128)(2,1)} %get-tuple-element.44.r_hi, bf16[256,512]{1,0:T(8,128)(2,1)} %get-tuple-element.45.r_lo, f32[4,6,64,256]{3,2,1,0:T(8,128)} %all-to-all-done.3.own_ref, f32[4,6,64,256]{3,2,1,0:T(8,128)} %collective-permute-done.6.other_ref), custom_call_target="tpu_custom_call" | custom-call | flops 1024 | bytes 1024 | tf_op jit(solution)/shard_map/radial/pallas_call | solution.py:249
  226.0 4.2 %all-to-all-start.7 = ((f32[4,6,64,256]{3,2,1,0:T(8,128)}), f32[4,6,64,256]{3,2,1,0:T(8,128)S(1)}, u32[]{:S(2)}, u32[]{:S(2)}) async-start(f32[4,6,64,256]{3,2,1,0:T(8,128)} %radial.5), calls=%async_computation.7 | async-start | bytes 3145728 | tf_op jit(solution)/shard_map/all_to_all | solution.py:392
  230.2 2.3 place.4.rest_0_
  232.6 2.3 place.5.rest_0_
  234.9 2.3 place.6.rest_0_
  237.2 11.7 %all-to-all-done.7 = f32[4,6,64,256]{3,2,1,0:T(8,128)S(1)} async-done(((f32[4,6,64,256]{3,2,1,0:T(8,128)}), f32[4,6,64,256]{3,2,1,0:T(8,128)S(1)}, u32[]{:S(2)}, u32[]{:S(2)}) %all-to-all-start.7) | async-done | bytes 1572896 | tf_op jit(solution)/shard_map/all_to_all | solution.py:392
  248.9 1.2 copy-done.2
  250.1 2.3 place.7
  (21 shorter events, 0.0 us)
Async XLA Ops:
  2.5 18.9 %collective-permute-start.1 = (f32[8,8,1024]{2,1,0:T(8,128)}, f32[8,8,1024]{2,1,0:T(8,128)S(1)}, u32[]{:S(2)}, u32[]{:S(2)}) collective-permute-start(f32[8,8,1024]{2,1,0:T(8,128)} %get-tuple-element.47), channel_id=1, source_target_pairs={{1,0},{2,1},{3,2},{4,3},{5,4},{6,5},{7,6},{9,8},{10,9},{11,10},{12... | collective-permute-start | bytes 786440 | tf_op jit(solution)/shard_map/ppermute | solution.py:379
  3.8 17.6 %collective-permute-start = (f32[8,8,1024]{2,1,0:T(8,128)}, f32[8,8,1024]{2,1,0:T(8,128)S(1)}, u32[]{:S(2)}, u32[]{:S(2)}) collective-permute-start(f32[8,8,1024]{2,1,0:T(8,128)} %get-tuple-element.38), channel_id=1, source_target_pairs={{0,1},{1,2},{2,3},{3,4},{4,5},{5,6},{6,7},{8,9},{9,10},{10,11},{11... | collective-permute-start | bytes 786440 | tf_op jit(solution)/shard_map/ppermute | solution.py:378
  13.8 11.4 %copy-start.8 = (f32[64]{0:T(128)S(1)}, f32[64]{0:T(128)}, u32[]{:S(2)}) copy-start(f32[64]{0:T(128)} %param.10) | copy-start | bytes 772
  13.8 12.1 %copy-start.9 = (f32[64]{0:T(128)S(1)}, f32[64]{0:T(128)}, u32[]{:S(2)}) copy-start(f32[64]{0:T(128)} %param.11) | copy-start | bytes 772
  21.4 5.3 %copy-start.6 = (f32[8,8,1024]{2,1,0:T(8,128)}, f32[8,8,1024]{2,1,0:T(8,128)S(1)}, u32[]{:S(2)}) copy-start(f32[8,8,1024]{2,1,0:T(8,128)S(1)} %collective-permute-done.1.rad_hi) | copy-start | bytes 786436
  21.4 5.3 %copy-start.7 = (f32[8,8,1024]{2,1,0:T(8,128)}, f32[8,8,1024]{2,1,0:T(8,128)S(1)}, u32[]{:S(2)}) copy-start(f32[8,8,1024]{2,1,0:T(8,128)S(1)} %collective-permute-done.rad_lo) | copy-start | bytes 786436
  21.4 36.2 %collective-permute-start.2 = (f32[7,64,1024]{2,1,0:T(8,128)}, f32[7,64,1024]{2,1,0:T(8,128)}, u32[]{:S(2)}, u32[]{:S(2)}) collective-permute-start(f32[7,64,1024]{2,1,0:T(8,128)} %get-tuple-element.53), channel_id=1, source_target_pairs={{0,8},{8,16},{16,24},{24,32},{32,40},{40,48},{48,56},{56,64},{64,7... | collective-permute-start | bytes 5505032 | tf_op jit(solution)/shard_map/ppermute | solution.py:387
  24.0 33.7 %collective-permute-start.3 = (f32[7,64,1024]{2,1,0:T(8,128)}, f32[7,64,1024]{2,1,0:T(8,128)}, u32[]{:S(2)}, u32[]{:S(2)}) collective-permute-start(f32[7,64,1024]{2,1,0:T(8,128)} %get-tuple-element.54), channel_id=1, source_target_pairs={{8,0},{16,8},{24,16},{32,24},{40,32},{48,40},{56,48},{64,56},{72,6... | collective-permute-start | bytes 5505032 | tf_op jit(solution)/shard_map/ppermute | solution.py:388
  40.0 25.9 %all-to-all-start = ((f32[4,6,64,256]{3,2,1,0:T(8,128)}), f32[4,6,64,256]{3,2,1,0:T(8,128)}, u32[]{:S(2)}, u32[]{:S(2)}) async-start(f32[4,6,64,256]{3,2,1,0:T(8,128)} %rhs_2.1), calls=%async_computation | async-start | bytes 3145728 | tf_op jit(solution)/shard_map/all_to_all | solution.py:392
  65.9 29.8 %all-to-all-start.1 = ((f32[4,6,64,256]{3,2,1,0:T(8,128)}), f32[4,6,64,256]{3,2,1,0:T(8,128)S(1)}, u32[]{:S(2)}, u32[]{:S(2)}) async-start(f32[4,6,64,256]{3,2,1,0:T(8,128)} %rhs_4.1), calls=%async_computation.1 | async-start | bytes 3145728 | tf_op jit(solution)/shard_map/all_to_all | solution.py:392
  69.5 39.6 %collective-permute-start.4 = (f32[4,6,64,256]{3,2,1,0:T(8,128)}, f32[4,6,64,256]{3,2,1,0:T(8,128)}, u32[]{:S(2)}, u32[]{:S(2)}) collective-permute-start(f32[4,6,64,256]{3,2,1,0:T(8,128)} %all-to-all-done.own_ref), channel_id=1, source_target_pairs={{0,1},{1,0},{2,3},{3,2},{4,5},{5,4},{6,7},{7,6},{8,9},{9,8},{10,11... | collective-permute-start | bytes 4718600 | tf_op jit(solution)/shard_map/ppermute | solution.py:397
  95.7 4.7 %copy-start.3 = (f32[4,6,64,256]{3,2,1,0:T(8,128)}, f32[4,6,64,256]{3,2,1,0:T(8,128)S(1)}, u32[]{:S(2)}) copy-start(f32[4,6,64,256]{3,2,1,0:T(8,128)S(1)} %all-to-all-done.1.own_ref) | copy-start | bytes 4718596
  95.7 26.4 %all-to-all-start.2 = ((f32[4,6,64,256]{3,2,1,0:T(8,128)}), f32[4,6,64,256]{3,2,1,0:T(8,128)S(1)}, u32[]{:S(2)}, u32[]{:S(2)}) async-start(f32[4,6,64,256]{3,2,1,0:T(8,128)} %get-tuple-element.61), calls=%async_computation.2 | async-start | bytes 3145728 | tf_op jit(solution)/shard_map/all_to_all | solution.py:392
  100.4 42.4 %collective-permute-start.5 = (f32[4,6,64,256]{3,2,1,0:T(8,128)S(1)}, f32[4,6,64,256]{3,2,1,0:T(8,128)}, u32[]{:S(2)}, u32[]{:S(2)}) collective-permute-start(f32[4,6,64,256]{3,2,1,0:T(8,128)S(1)} %all-to-all-done.1.own_ref), channel_id=1, source_target_pairs={{0,1},{1,0},{2,3},{3,2},{4,5},{5,4},{6,7},{7,6},{8,9},{9,8},{10,11... | collective-permute-start | bytes 4718600 | tf_op jit(solution)/shard_map/ppermute | solution.py:397
  122.1 29.0 %copy-start.4 = (f32[4,6,64,256]{3,2,1,0:T(8,128)}, f32[4,6,64,256]{3,2,1,0:T(8,128)S(1)}, u32[]{:S(2)}) copy-start(f32[4,6,64,256]{3,2,1,0:T(8,128)S(1)} %all-to-all-done.2.own_ref) | copy-start | bytes 4718596
  122.1 25.5 %all-to-all-start.3 = ((f32[4,6,64,256]{3,2,1,0:T(8,128)}), f32[4,6,64,256]{3,2,1,0:T(8,128)}, u32[]{:S(2)}, u32[]{:S(2)}) async-start(f32[4,6,64,256]{3,2,1,0:T(8,128)} %get-tuple-element.63), calls=%async_computation.3 | async-start | bytes 3145728 | tf_op jit(solution)/shard_map/all_to_all | solution.py:392
  147.5 23.7 %all-to-all-start.4 = ((f32[4,6,64,256]{3,2,1,0:T(8,128)}), f32[4,6,64,256]{3,2,1,0:T(8,128)S(1)}, u32[]{:S(2)}, u32[]{:S(2)}) async-start(f32[4,6,64,256]{3,2,1,0:T(8,128)} %radial.4), calls=%async_computation.4 | async-start | bytes 3145728 | tf_op jit(solution)/shard_map/all_to_all | solution.py:392
  151.1 39.2 %collective-permute-start.7 = (f32[4,6,64,256]{3,2,1,0:T(8,128)S(1)}, f32[4,6,64,256]{3,2,1,0:T(8,128)}, u32[]{:S(2)}, u32[]{:S(2)}) collective-permute-start(f32[4,6,64,256]{3,2,1,0:T(8,128)S(1)} %all-to-all-done.2.own_ref), channel_id=1, source_target_pairs={{0,1},{1,0},{2,3},{3,2},{4,5},{5,4},{6,7},{7,6},{8,9},{9,8},{10,11... | collective-permute-start | bytes 4718600 | tf_op jit(solution)/shard_map/ppermute | solution.py:397
  171.2 1.2 copy-start.5
  172.4 22.9 %all-to-all-start.5 = ((f32[4,6,64,256]{3,2,1,0:T(8,128)}), f32[4,6,64,256]{3,2,1,0:T(8,128)S(1)}, u32[]{:S(2)}, u32[]{:S(2)}) async-start(f32[4,6,64,256]{3,2,1,0:T(8,128)} %radial.7), calls=%async_computation.5 | async-start | bytes 3145728 | tf_op jit(solution)/shard_map/all_to_all | solution.py:392
  175.9 46.0 %collective-permute-start.6 = (f32[4,6,64,256]{3,2,1,0:T(8,128)}, f32[4,6,64,256]{3,2,1,0:T(8,128)}, u32[]{:S(2)}, u32[]{:S(2)}) collective-permute-start(f32[4,6,64,256]{3,2,1,0:T(8,128)} %all-to-all-done.3.own_ref), channel_id=1, source_target_pairs={{0,1},{1,0},{2,3},{3,2},{4,5},{5,4},{6,7},{7,6},{8,9},{9,8},{10,11... | collective-permute-start | bytes 4718600 | tf_op jit(solution)/shard_map/ppermute | solution.py:397
  195.3 1.2 copy-start
  196.5 29.5 %all-to-all-start.6 = ((f32[4,6,64,256]{3,2,1,0:T(8,128)}), f32[4,6,64,256]{3,2,1,0:T(8,128)S(1)}, u32[]{:S(2)}, u32[]{:S(2)}) async-start(f32[4,6,64,256]{3,2,1,0:T(8,128)} %radial.6), calls=%async_computation.6 | async-start | bytes 3145728 | tf_op jit(solution)/shard_map/all_to_all | solution.py:392
  226.0 4.2 %copy-start.1 = (f32[4,6,64,256]{3,2,1,0:T(8,128)}, f32[4,6,64,256]{3,2,1,0:T(8,128)S(1)}, u32[]{:S(2)}) copy-start(f32[4,6,64,256]{3,2,1,0:T(8,128)S(1)} %all-to-all-done.6) | copy-start | bytes 4718596
  226.0 22.9 %all-to-all-start.7 = ((f32[4,6,64,256]{3,2,1,0:T(8,128)}), f32[4,6,64,256]{3,2,1,0:T(8,128)S(1)}, u32[]{:S(2)}, u32[]{:S(2)}) async-start(f32[4,6,64,256]{3,2,1,0:T(8,128)} %radial.5), calls=%async_computation.7 | async-start | bytes 3145728 | tf_op jit(solution)/shard_map/all_to_all | solution.py:392
  248.9 1.2 copy-start.2

commit v3 on v2

--- a/solution.py
+++ b/solution.py
@@ -10,8 +10,8 @@
 COEF = 0.25
 F32 = jnp.float32
 BF16 = jnp.bfloat16
-CHUNKS = ((2, 3), (4, 5), (0, 1), (6, 7))
-RADIAL_BYTES = (8 * 1024 * 1024, 1024, 1024, 1024)
+INNER = ((2, 3), (4, 5))
+OUTER = ((0, 1), (6, 7))
 HALF_BYTES = 200 * 1024 * 1024
 COLUMNS = 256
 VMEM_LIMIT = 56 * 1024 * 1024
@@ -138,7 +138,7 @@
                     total = centre * q24[8:16]
                     for (up, down, up2, down2), (c_up, c_down, b) in zip(near, coefs):
                         total = total + (c_up * up + c_down * down + b * (up2 - down2))
-                    rhs[c, place, pl.ds(r0, 8), cols] = total
+                    rhs[place, c, pl.ds(r0, 8), cols] = total
             return carry
 
         lax.fori_loop(0, rows // 8, strip, 0)
@@ -146,15 +146,16 @@
     for group, out in zip(groups, outs):
         size = len(group)
 
+        low = sum(p < group[0] + len(group) for p in group)
+        jump = group[-1] - group[0] - size + 1
+
         def plane(j, carry):
-            stencil(j, group[0] + j)
+            stencil(j, group[0] + j + jnp.where(j >= low, jump, 0))
             return carry
 
         lax.fori_loop(0, size, plane, 0)
         lines = size * rows
-        for c in range(3):
-            part = pl.ds(c * lines, lines)
-            hi[part, :], lo[part, :] = split(rhs[c, 0:size].reshape(lines, nt))
+        hi[0 : 3 * lines, :], lo[0 : 3 * lines, :] = split(rhs[0:size].reshape(3 * lines, nt))
         for d in range(nt // width):
             cols = pl.ds(d * width, width)
             solved = dot3(
@@ -183,7 +184,7 @@
         scratch_shapes=[
             pltpu.VMEM((3, 12, rows + 16, nt), F32),
             pltpu.VMEM((12, rows + 16, nt), F32),
-            pltpu.VMEM((3, most, rows, nt), F32),
+            pltpu.VMEM((most, 3, rows, nt), F32),
             pltpu.VMEM((3 * most * rows, nt), BF16),
             pltpu.VMEM((3 * most * rows, nt), BF16),
             pltpu.SemaphoreType.DMA((12,)),
@@ -193,20 +194,21 @@
     )(inv_dx, inv_dr[:, None], inv_rt[:, None], velocity, viscosity, rad_lo, rad_hi, *ax, *az)
 
 
-def half_kernel(side_ref, x_ref, hi_ref, lo_ref):
+def half_kernel(side_ref, x_ref, hi_ref, lo_ref, hi_far_ref, lo_far_ref):
     rows = x_ref.shape[0] // 8
     side = side_ref[0]
     for part in range(4):
-        x = x_ref[pl.ds(pl.multiple_of(part * 2 * rows + side * rows, rows), rows), :]
-        swapped = jnp.concatenate(
-            [
-                pltpu.roll(x[:, at : at + 2 * rows], rows, 1)
-                for at in range(0, x.shape[1], 2 * rows)
-            ],
-            axis=1,
-        )
         at = slice(part * rows, (part + 1) * rows)
-        hi_ref[at, :], lo_ref[at, :] = split(jnp.where(side == 0, x, swapped))
+        for one, hi, lo in ((side, hi_ref, lo_ref), (1 - side, hi_far_ref, lo_far_ref)):
+            x = x_ref[pl.ds(pl.multiple_of(part * 2 * rows + one * rows, rows), rows), :]
+            swapped = jnp.concatenate(
+                [
+                    pltpu.roll(x[:, low : low + 2 * rows], rows, 1)
+                    for low in range(0, x.shape[1], 2 * rows)
+                ],
+                axis=1,
+            )
+            hi[at, :], lo[at, :] = split(jnp.where(side == 0, x, swapped))
 
 
 def half_call(side, x):
@@ -216,20 +218,24 @@
         half_kernel,
         name="half",
         in_specs=[pl.BlockSpec(memory_space=pltpu.SMEM), vmem],
-        out_specs=[vmem, vmem],
-        out_shape=[jax.ShapeDtypeStruct((rows // 2, cols), BF16)] * 2,
-        cost_estimate=pl.CostEstimate(
-            flops=0, bytes_accessed=HALF_BYTES, transcendentals=0
-        ),
+        out_specs=[vmem] * 4,
+        out_shape=[jax.ShapeDtypeStruct((rows // 2, cols), BF16)] * 4,
     )(side, x)
 
 
-def radial_kernel(r_hi, r_lo, own_ref, other_ref, out_ref):
+def radial_kernel(r_hi, r_lo, own_ref, *rest):
+    *others, out_ref = rest
     parts, slabs, rows, width = own_ref.shape
+    theirs = [(ref, part) for ref in others for part in range(ref.shape[0])]
     x = jnp.concatenate(
         [
             jnp.concatenate(
-                [ref[part, s] for part in range(parts) for ref in (own_ref, other_ref)], axis=0
+                [
+                    ref[at, s]
+                    for part in range(parts)
+                    for ref, at in ((own_ref, part), theirs[part])
+                ],
+                axis=0,
             )
             for s in range(slabs)
         ],
@@ -241,50 +247,122 @@
         out_ref[:, s] = y[:, s * width : (s + 1) * width].reshape(parts, rows, width)
 
 
-def radial_call(rad, own, other, moved):
+def radial_call(rad, own, others):
     parts, slabs, rows, width = own.shape
-    step = 3
-    block = pl.BlockSpec((parts, step, rows, width), lambda i: (0, i, 0, 0))
+
+    def block(x):
+        return pl.BlockSpec((x.shape[0], 3, rows, width), lambda i: (0, i, 0, 0))
+
     full = pl.BlockSpec(rad[0].shape, lambda i: (0, 0))
     return pl.pallas_call(
         radial_kernel,
         name="radial",
-        grid=(slabs // step,),
-        in_specs=[full, full, block, block],
-        out_specs=block,
+        grid=(slabs // 3,),
+        in_specs=[full, full, block(own)] + [block(x) for x in others],
+        out_specs=block(own),
         out_shape=jax.ShapeDtypeStruct(own.shape, F32),
         compiler_params=pltpu.CompilerParams(vmem_limit_bytes=VMEM_LIMIT),
-        cost_estimate=pl.CostEstimate(
-            flops=1024,
-            bytes_accessed=moved,
-            transcendentals=0,
-        ),
-    )(*rad, own, other)
+        cost_estimate=pl.CostEstimate(flops=1024, bytes_accessed=1024, transcendentals=0),
+    )(*rad, own, *others)
+
+
+def both_kernel(side_ref, r_hi, r_lo, f_hi, f_lo, own_ref, other_ref, out_ref):
+    parts, slabs, rows, width = other_ref.shape
+    mine = pl.ds(pl.multiple_of(side_ref[0] * width, width), width)
+    x = jnp.concatenate(
+        [
+            jnp.concatenate(
+                [
+                    piece
+                    for part in range(parts)
+                    for piece in (own_ref[part, s, :, mine], other_ref[part, s])
+                ],
+                axis=0,
+            )
+            for s in range(slabs)
+        ],
+        axis=1,
+    )
+    hi, lo = split(x)
+    for way, (a_hi, a_lo) in enumerate(((r_hi, r_lo), (f_hi, f_lo))):
+        y = dot3(a_hi[...], a_lo[...], hi, lo, ((1,), (0,)))
+        for s in range(slabs):
+            out_ref[:, way, s] = y[:, s * width : (s + 1) * width].reshape(parts, rows, width)
+
+
+def both_call(side, rad, own, other):
+    parts, slabs, rows, width = other.shape
+    full = pl.BlockSpec(rad[0].shape, lambda i: (0, 0))
+    return pl.pallas_call(
+        both_kernel,
+        name="radial_both",
+        grid=(slabs // 3,),
+        in_specs=[pl.BlockSpec(memory_space=pltpu.SMEM)]
+        + [full] * 4
+        + [
+            pl.BlockSpec((parts, 3, rows, 2 * width), lambda i: (0, i, 0, 0)),
+            pl.BlockSpec((parts, 3, rows, width), lambda i: (0, i, 0, 0)),
+        ],
+        out_specs=pl.BlockSpec((parts, 2, 3, rows, width), lambda i: (0, 0, i, 0, 0)),
+        out_shape=jax.ShapeDtypeStruct((parts, 2, slabs, rows, width), F32),
+        compiler_params=pltpu.CompilerParams(vmem_limit_bytes=VMEM_LIMIT),
+        cost_estimate=pl.CostEstimate(flops=1024, bytes_accessed=1024, transcendentals=0),
+    )(side, *rad, own, other)
+
+
+def weave_kernel(side_ref, near_ref, far_ref, _, out_ref):
+    parts, _, _, _, width = near_ref.shape
+    side = side_ref[0]
+    for d in range(parts):
+        for c in range(3):
+            for at, value in ((side, near_ref[d, 0, c]), (1 - side, far_ref[d, c])):
+                cols = pl.ds(pl.multiple_of((2 * d + at) * width, width), width)
+                out_ref[c, 0, :, cols] = value
+
+
+def weave_call(side, planes, near, far, whole):
+    parts, _, rows, width = far.shape
+    first = planes[0]
+    return pl.pallas_call(
+        weave_kernel,
+        name="weave",
+        grid=(len(planes),),
+        in_specs=[
+            pl.BlockSpec(memory_space=pltpu.SMEM),
+            pl.BlockSpec((parts, 1, 3, rows, width), lambda j: (0, 0, j, 0, 0)),
+            pl.BlockSpec((parts, 3, rows, width), lambda j: (0, j, 0, 0)),
+            pl.BlockSpec(memory_space=pl.ANY),
+        ],
+        out_specs=pl.BlockSpec((3, 1, rows, 2 * parts * width), lambda j: (0, first + j, 0, 0)),
+        out_shape=jax.ShapeDtypeStruct(whole.shape, F32),
+        input_output_aliases={3: 0},
+        cost_estimate=pl.CostEstimate(flops=0, bytes_accessed=16 * far.size, transcendentals=0),
+    )(side, near, far, whole)
 
 
 def place_kernel(x_ref, *rest):
     out_ref = rest[-1]
-    parts, width = x_ref.shape[0], x_ref.shape[4]
+    parts, width = x_ref.shape[0], x_ref.shape[3]
     for d in range(parts):
         for c in range(3):
-            out_ref[c, 0, :, d * width : (d + 1) * width] = x_ref[d, c, 0]
+            out_ref[c, 0, :, d * width : (d + 1) * width] = x_ref[d, c]
 
 
 def place_call(planes, x, whole, shape):
-    parts, slabs, rows, width = x.shape
+    parts, _, rows, width = x.shape
     first = planes[0]
     aliased = () if whole is None else (whole,)
     return pl.pallas_call(
         place_kernel,
         name="place",
         grid=(len(planes),),
-        in_specs=[pl.BlockSpec((parts, 3, 1, rows, width), lambda j: (0, 0, j, 0, 0))]
+        in_specs=[pl.BlockSpec((parts, 3, rows, width), lambda j: (0, j, 0, 0))]
         + [pl.BlockSpec(memory_space=pl.ANY)] * len(aliased),
         out_specs=pl.BlockSpec((3, 1, rows, parts * width), lambda j: (0, first + j, 0, 0)),
         out_shape=jax.ShapeDtypeStruct(shape, F32),
         input_output_aliases={1: 0} if aliased else {},
         cost_estimate=pl.CostEstimate(flops=0, bytes_accessed=8 * x.size, transcendentals=0),
-    )(x.reshape(parts, 3, slabs // 3, rows, width), *aliased)
+    )(x, *aliased)
 
 
 def line_kernel(velocity, viscosity, top, bottom, edges, sems):
@@ -379,10 +457,9 @@
     rad_hi = lax.ppermute(rad_bottom, "rad", backward)
     ax_top, ax_bottom = face_call(velocity, after(viscosity, rad_top))
     az = split_call(after(az_inverse, ax_top))
-    rad = half_call(after(side, az[0]), rad_inverse)
     forward, backward = shifts("ax")
     ax_top, ax_bottom, rad_lo, rad_hi, *_ = lax.optimization_barrier(
-        (ax_top, ax_bottom, rad_lo, rad_hi, az[0], rad[0])
+        (ax_top, ax_bottom, rad_lo, rad_hi, az[0])
     )
     ax_lo = lax.ppermute(ax_top, "ax", forward)
     ax_hi = lax.ppermute(ax_bottom, "ax", backward)
@@ -397,25 +474,31 @@
         return lax.ppermute(x, "rad", [(i, i ^ 1) for i in range(lines)])
 
     common = (inv_dr, inv_rt, velocity, viscosity, rad_lo, rad_hi)
-    (first,) = rhs_call(CHUNKS[:1], parts, inv_dx, *common, (), az)
-    (second,) = rhs_call(CHUNKS[1:2], parts, after(inv_dx, first), *common, (), az)
+    (first,) = rhs_call(INNER[:1], parts, inv_dx, *common, (), az)
+    rad = half_call(after(side, first), rad_inverse)
+    (second,) = rhs_call(INNER[1:], parts, after(inv_dx, first, rad[0]), *common, (), az)
     second, ax_lo, ax_hi = lax.optimization_barrier((second, ax_lo, ax_hi))
     own = [exchange(first)]
-    other = [partner(after(own[0], ax_lo))]
+    other = [(partner(after(own[0], ax_lo)),)]
     own.append(exchange(after(second, own[0])))
-    edges = rhs_call(CHUNKS[2:], parts, after(inv_dx, own[0]), *common, (ax_lo, ax_hi), az)
-    other.append(partner(after(own[1], edges[0])))
-    solved = [radial_call(rad, own[k], other[k], RADIAL_BYTES[k]) for k in range(2)]
+    edges = rhs_call(OUTER, parts, after(inv_dx, own[0]), *common, (ax_lo, ax_hi), az)
     own.append(exchange(after(edges[0], own[1])))
+    other.append((partner(after(own[1], edges[0])),))
+    solved = [radial_call(rad[:2], own[k], other[k]) for k in range(2)]
     own.append(exchange(after(edges[1], own[2], solved[0])))
-    back = [exchange(after(solved[0], own[3], other[1]))]
-    for k in range(2, len(CHUNKS)):
-        other.append(partner(after(own[k], other[k - 2])))
-        solved.append(radial_call(rad, own[k], other[k], RADIAL_BYTES[k]))
-    whole = place_call(CHUNKS[0], back[0], None, velocity.shape)
-    for k in range(1, len(CHUNKS)):
-        back.append(exchange(after(solved[k], back[-1])))
-        whole = place_call(CHUNKS[k], back[k], whole, velocity.shape)
+    width = own[2].shape[3] // 2
+    sent = lax.dynamic_slice_in_dim(own[2], (1 - side[0]) * width, width, axis=3)
+    sent = partner(after(sent, other[0][0]))
+    other.append((partner(after(own[3], other[1][0])),))
+    backs = [exchange(after(solved[0], own[3], other[1][0]))]
+    backs.append(exchange(after(solved[1], backs[0], sent)))
+    near = exchange(after(both_call(side, rad, own[2], sent), backs[1]))
+    far = partner(near[:, 1])
+    backs.append(exchange(after(radial_call(rad[:2], own[3], other[2]), near)))
+    whole = None
+    for planes_of, back in zip((*INNER, OUTER[1]), backs):
+        whole = place_call(planes_of, back, whole, velocity.shape)
+    whole = weave_call(side, OUTER[0], near, far, whole)
     return whole
 
 

time: 254 us -> 243 us (0.957)
  waiting for transfers between devices: 110 us -> 92 us
  local copies, waits for them, and re-layouts: 4.99 us -> 8.05 us
  starting transfers between devices: 49.5 us -> 52.5 us
    all_to_all x8, waiting for transfers between devices: 50 us -> 40.4 us  [exchange(): lax.all_to_all(x, 'rad', split_axis=0, concat_axis=0, tiled=True, axis_in...]
    ppermute x4 -> x5, waiting for transfers between devices: 60.1 us -> 50.7 us  [partner(): return lax.ppermute(x, 'rad', [(i, i ^ 1) for i in range(lines)])]
    pallas_call x4 -> x5, Pallas kernels: 16.1 us -> 18.8 us  [the longest x3 12 us: radial_call(): pl.pallas_call(radial_kernel, name='radial', grid=(slabs // 3,), in_specs...]
    pallas_call x4 -> x3, Pallas kernels: 9.3 us -> 6.98 us  [place_call(): pl.pallas_call(place_kernel, name='place', grid=(len(planes),), in_specs=...]
    unnamed x20 -> x26, local copies, waits for them, and re-layouts: 3.59 us -> 5.64 us
    ppermute x4 -> x5, starting transfers between devices: 6.43 us -> 8.45 us  [partner(): return lax.ppermute(x, 'rad', [(i, i ^ 1) for i in range(lines)])]
  transfers between devices with their start and end apart: 16 -> 17, of which waited for: 10 -> 11; matrix products, arithmetic and copies ran while one was open for 1% -> 1% of each run, Pallas kernels for 33% -> 35%
where the time goes in v3:
time: 243 us; the launch traced here: 241 us
  waiting for transfers between devices  92 us (38%)
  Pallas kernels  88.2 us (36%)
  starting transfers between devices  52.5 us (22%)
  local copies, waits for them, and re-layouts  8.05 us (3%)
    ppermute x5, waiting for transfers between devices, partner(): return lax.ppermute(x, 'rad', [(i, i ^ 1) for i in range(lines)])  50.7 us
    pallas_call x3, Pallas kernels, rhs_call(): pl.pallas_call(functools.partial(rhs_kernel, groups, bool(ax)), name=f'rh...  48.2 us
    all_to_all x8, waiting for transfers between devices, exchange(): lax.all_to_all(x, 'rad', split_axis=0, concat_axis=0, tiled=True, axis_in...  40.4 us
    all_to_all x8, starting transfers between devices, exchange(): lax.all_to_all(x, 'rad', split_axis=0, concat_axis=0, tiled=True, axis_in...  32.3 us
    pallas_call x3, Pallas kernels, radial_call(): pl.pallas_call(radial_kernel, name='radial', grid=(slabs // 3,), in_specs...  12 us
    ppermute x5, starting transfers between devices, partner(): return lax.ppermute(x, 'rad', [(i, i ^ 1) for i in range(lines)])  8.45 us
    pallas_call x3, Pallas kernels, place_call(): pl.pallas_call(place_kernel, name='place', grid=(len(planes),), in_specs=...  6.98 us
    ppermute x1, starting transfers between devices, local(): rad_lo = lax.ppermute(rad_top, 'rad', forward)  6.07 us
  transfers between devices with their start and end apart: 17, of which 11 were waited for; matrix products, arithmetic and copies ran while one was open for 1% of the time, Pallas kernels for 35%

profile of v3, /device:TPU:0, one launch (start us, length us, event | category | flops | bytes accessed | tf_op | source)
XLA Modules:
  0.0 241.1 jit_solution(7600800684523888412)
XLA Ops:
  0.0 2.5 %lines.1 = (f32[8,8,1024]{2,1,0:T(8,128)}, f32[8,8,1024]{2,1,0:T(8,128)}) custom-call(f32[3,8,64,1024]{3,2,1,0:T(8,128)} %velocity.9, f32[8,64,1024]{2,1,0:T(8,128)} %viscosity.8), custom_call_target="tpu_custom_call" | custom-call | tf_op jit(solution)/shard_map/lines/pallas_call | solution.py:399
  2.5 1.3 collective-permute-start.1
  3.8 6.1 %collective-permute-start = (f32[8,8,1024]{2,1,0:T(8,128)}, f32[8,8,1024]{2,1,0:T(8,128)S(1)}, u32[]{:S(2)}, u32[]{:S(2)}) collective-permute-start(f32[8,8,1024]{2,1,0:T(8,128)} %get-tuple-element.40), channel_id=1, source_target_pairs={{0,1},{1,2},{2,3},{3,4},{4,5},{5,6},{6,7},{8,9},{9,10},{10,11},{11... | collective-permute-start | bytes 786440 | tf_op jit(solution)/shard_map/ppermute | solution.py:456
  9.9 3.9 %faces.1 = (f32[7,64,1024]{2,1,0:T(8,128)}, f32[7,64,1024]{2,1,0:T(8,128)}) custom-call(f32[3,8,64,1024]{3,2,1,0:T(8,128)} %velocity.9, f32[8,64,1024]{2,1,0:T(8,128)} %viscosity.8), custom_call_target="tpu_custom_call" | custom-call | tf_op jit(solution)/shard_map/faces/pallas_call | solution.py:428
  13.8 5.3 %split_1024.1 = (bf16[1024,1024]{1,0:T(8,128)(2,1)}, bf16[1024,1024]{1,0:T(8,128)(2,1)}) custom-call(f32[1024,1024]{1,0:T(8,128)} %x_ref.1), custom_call_target="tpu_custom_call" | custom-call | tf_op jit(solution)/shard_map/split_1024/pallas_call | solution.py:39
  19.1 1.0 collective-permute-done.rad_lo
  20.1 3.1 %collective-permute-start.2 = (f32[7,64,1024]{2,1,0:T(8,128)}, f32[7,64,1024]{2,1,0:T(8,128)}, u32[]{:S(2)}, u32[]{:S(2)}) collective-permute-start(f32[7,64,1024]{2,1,0:T(8,128)} %get-tuple-element.57), channel_id=1, source_target_pairs={{0,8},{8,16},{16,24},{24,32},{32,40},{40,48},{48,56},{56,64},{64,7... | collective-permute-start | bytes 5505032 | tf_op jit(solution)/shard_map/ppermute | solution.py:464
  23.2 1.3 collective-permute-start.3
  25.2 0.7 copy.20.inv_rt
  25.9 13.3 %rhs_2.1 = f32[4,6,64,256]{3,2,1,0:T(8,128)} custom-call(f32[8]{0:T(128)} %inv_dx.3, f32[64,1]{1,0:T(8,128)} %copy.19.inv_dr, f32[64,1]{1,0:T(8,128)} %copy.20.inv_rt, f32[3,8,64,1024]{3,2,1,0:T(8,128)} %velocity.9, f32[8,64,1024]{2,1,0:T(8,128)} %viscosity.8, f32[8,8,1024]{2,1,0:T(8,128)} %copy-done.8, f32[8,8,1024]{2,1,0:T(8,128)} %copy-done.7, ...), custom_call_target="tpu_custom_call" | custom-call | flops 1024 | bytes 1024 | tf_op jit(solution)/shard_map/rhs_2/pallas_call | solution.py:173
  39.3 4.3 %all-to-all-start = ((f32[4,6,64,256]{3,2,1,0:T(8,128)}), f32[4,6,64,256]{3,2,1,0:T(8,128)S(1)}, u32[]{:S(2)}, u32[]{:S(2)}) async-start(f32[4,6,64,256]{3,2,1,0:T(8,128)} %rhs_2.1), calls=%async_computation | async-start | bytes 3145728 | tf_op jit(solution)/shard_map/all_to_all | solution.py:469
  43.6 2.5 %half.1 = (bf16[256,512]{1,0:T(8,128)(2,1)}, bf16[256,512]{1,0:T(8,128)(2,1)}, bf16[256,512]{1,0:T(8,128)(2,1)}, bf16[256,512]{1,0:T(8,128)(2,1)}) custom-call(s32[1]{0:T(128)} %bitcast.side_ref, f32[512,512]{1,0:T(8,128)} %x_ref.2), custom_call_target="tpu_custom_call" | custom-call | tf_op jit(solution)/shard_map/half/pallas_call | solution.py:217
  46.1 13.3 %rhs_4.1 = f32[4,6,64,256]{3,2,1,0:T(8,128)} custom-call(f32[8]{0:T(128)} %inv_dx.3, f32[64,1]{1,0:T(8,128)} %copy.19.inv_dr, f32[64,1]{1,0:T(8,128)} %copy.20.inv_rt, f32[3,8,64,1024]{3,2,1,0:T(8,128)} %velocity.9, f32[8,64,1024]{2,1,0:T(8,128)} %viscosity.8, f32[8,8,1024]{2,1,0:T(8,128)} %copy-done.8, f32[8,8,1024]{2,1,0:T(8,128)} %copy-done.7, ...), custom_call_target="tpu_custom_call" | custom-call | flops 1024 | bytes 1024 | tf_op jit(solution)/shard_map/rhs_4/pallas_call | solution.py:173
  59.4 6.2 %all-to-all-done.own_ref = f32[4,6,64,256]{3,2,1,0:T(8,128)S(1)} async-done(((f32[4,6,64,256]{3,2,1,0:T(8,128)}), f32[4,6,64,256]{3,2,1,0:T(8,128)S(1)}, u32[]{:S(2)}, u32[]{:S(2)}) %all-to-all-start) | async-done | bytes 1572896 | tf_op jit(solution)/shard_map/all_to_all | solution.py:469
  65.6 3.6 %all-to-all-start.1 = ((f32[4,6,64,256]{3,2,1,0:T(8,128)}), f32[4,6,64,256]{3,2,1,0:T(8,128)S(1)}, u32[]{:S(2)}, u32[]{:S(2)}) async-start(f32[4,6,64,256]{3,2,1,0:T(8,128)} %rhs_4.1), calls=%async_computation.1 | async-start | bytes 3145728 | tf_op jit(solution)/shard_map/all_to_all | solution.py:469
  69.2 4.0 %collective-permute-start.4 = (f32[4,6,64,256]{3,2,1,0:T(8,128)S(1)}, f32[4,6,64,256]{3,2,1,0:T(8,128)}, u32[]{:S(2)}, u32[]{:S(2)}) collective-permute-start(f32[4,6,64,256]{3,2,1,0:T(8,128)S(1)} %all-to-all-done.own_ref), channel_id=1, source_target_pairs={{0,1},{1,0},{2,3},{3,2},{4,5},{5,4},{6,7},{7,6},{8,9},{9,8},{10,11... | collective-permute-start | bytes 4718600 | tf_op jit(solution)/shard_map/ppermute | solution.py:474
  73.1 21.6 %rhs_0.1 = (f32[4,6,64,256]{3,2,1,0:T(8,128)}, f32[4,6,64,256]{3,2,1,0:T(8,128)}) custom-call(f32[8]{0:T(128)} %inv_dx.3, f32[64,1]{1,0:T(8,128)} %copy.19.inv_dr, f32[64,1]{1,0:T(8,128)} %copy.20.inv_rt, f32[3,8,64,1024]{3,2,1,0:T(8,128)} %velocity.9, f32[8,64,1024]{2,1,0:T(8,128)} %viscosity.8, f32[8,8,1024]{2,1,0:T(8,128)} %copy-done.8, ...), custom_call_target="tpu_custom_call" | custom-call | flops 1024 | bytes 1024 | tf_op jit(solution)/shard_map/rhs_0/pallas_call | solution.py:173
  94.8 1.2 copy-done.5
  95.9 4.7 %all-to-all-start.2 = ((f32[4,6,64,256]{3,2,1,0:T(8,128)}), f32[4,6,64,256]{3,2,1,0:T(8,128)S(1)}, u32[]{:S(2)}, u32[]{:S(2)}) async-start(f32[4,6,64,256]{3,2,1,0:T(8,128)} %get-tuple-element.64), calls=%async_computation.2 | async-start | bytes 3145728 | tf_op jit(solution)/shard_map/all_to_all | solution.py:469
  100.6 7.9 %collective-permute-done.4.rest_0_ = f32[4,6,64,256]{3,2,1,0:T(8,128)} collective-permute-done((f32[4,6,64,256]{3,2,1,0:T(8,128)S(1)}, f32[4,6,64,256]{3,2,1,0:T(8,128)}, u32[]{:S(2)}, u32[]{:S(2)}) %collective-permute-start.4) | collective-permute-done | bytes 1572896 | tf_op jit(solution)/shard_map/ppermute | solution.py:474
  108.5 4.0 %radial.4 = f32[4,6,64,256]{3,2,1,0:T(8,128)} custom-call(bf16[256,512]{1,0:T(8,128)(2,1)} %get-tuple-element.51.r_hi, bf16[256,512]{1,0:T(8,128)(2,1)} %get-tuple-element.52.r_lo, f32[4,6,64,256]{3,2,1,0:T(8,128)} %copy-done.4, f32[4,6,64,256]{3,2,1,0:T(8,128)} %collective-permute-done.4.rest_0_), custom_call_target="tpu_custom_call" | custom-call | flops 1024 | bytes 1024 | tf_op jit(solution)/shard_map/radial/pallas_call | solution.py:257
  112.5 9.1 %all-to-all-done.2.own_ref = f32[4,6,64,256]{3,2,1,0:T(8,128)S(1)} async-done(((f32[4,6,64,256]{3,2,1,0:T(8,128)}), f32[4,6,64,256]{3,2,1,0:T(8,128)S(1)}, u32[]{:S(2)}, u32[]{:S(2)}) %all-to-all-start.2) | async-done | bytes 1572896 | tf_op jit(solution)/shard_map/all_to_all | solution.py:469
  121.6 4.3 %all-to-all-start.3 = ((f32[4,6,64,256]{3,2,1,0:T(8,128)}), f32[4,6,64,256]{3,2,1,0:T(8,128)}, u32[]{:S(2)}, u32[]{:S(2)}) async-start(f32[4,6,64,256]{3,2,1,0:T(8,128)} %get-tuple-element.69), calls=%async_computation.3 | async-start | bytes 3145728 | tf_op jit(solution)/shard_map/all_to_all | solution.py:469
  125.9 16.1 %collective-permute-done.6.rest_0_ = f32[4,6,64,256]{3,2,1,0:T(8,128)} collective-permute-done((f32[4,6,64,256]{3,2,1,0:T(8,128)}, f32[4,6,64,256]{3,2,1,0:T(8,128)}, u32[]{:S(2)}, u32[]{:S(2)}) %collective-permute-start.6) | collective-permute-done | bytes 1572896 | tf_op jit(solution)/shard_map/ppermute | solution.py:474
  142.0 4.1 %all-to-all-done.3.own_ref = f32[4,6,64,256]{3,2,1,0:T(8,128)} async-done(((f32[4,6,64,256]{3,2,1,0:T(8,128)}), f32[4,6,64,256]{3,2,1,0:T(8,128)}, u32[]{:S(2)}, u32[]{:S(2)}) %all-to-all-start.3) | async-done | bytes 1572896 | tf_op jit(solution)/shard_map/all_to_all | solution.py:469
  146.1 3.6 %all-to-all-start.4 = ((f32[4,6,64,256]{3,2,1,0:T(8,128)}), f32[4,6,64,256]{3,2,1,0:T(8,128)S(1)}, u32[]{:S(2)}, u32[]{:S(2)}) async-start(f32[4,6,64,256]{3,2,1,0:T(8,128)} %radial.4), calls=%async_computation.4 | async-start | bytes 3145728 | tf_op jit(solution)/shard_map/all_to_all | solution.py:469
  149.8 0.8 collective-permute-start.5
  150.6 4.0 %radial.3 = f32[4,6,64,256]{3,2,1,0:T(8,128)} custom-call(bf16[256,512]{1,0:T(8,128)(2,1)} %get-tuple-element.51.r_hi, bf16[256,512]{1,0:T(8,128)(2,1)} %get-tuple-element.52.r_lo, f32[4,6,64,256]{3,2,1,0:T(8,128)} %copy-done.5, f32[4,6,64,256]{3,2,1,0:T(8,128)} %collective-permute-done.6.rest_0_), custom_call_target="tpu_custom_call" | custom-call | flops 1024 | bytes 1024 | tf_op jit(solution)/shard_map/radial/pallas_call | solution.py:257
  154.6 14.5 %collective-permute-done.5.other_ref = f32[4,6,64,128]{3,2,1,0:T(8,128)S(1)} collective-permute-done((f32[4,6,64,128]{3,2,1,0:T(8,128)S(1)}, f32[4,6,64,128]{3,2,1,0:T(8,128)S(1)}, u32[]{:S(2)}, u32[]{:S(2)}) %collective-permute-start.5) | collective-permute-done | bytes 786464 | tf_op jit(solution)/shard_map/ppermute | solution.py:474
  169.1 1.2 copy-done.6
  170.3 4.5 %all-to-all-start.5 = ((f32[4,6,64,256]{3,2,1,0:T(8,128)}), f32[4,6,64,256]{3,2,1,0:T(8,128)S(1)}, u32[]{:S(2)}, u32[]{:S(2)}) async-start(f32[4,6,64,256]{3,2,1,0:T(8,128)} %radial.3), calls=%async_computation.5 | async-start | bytes 3145728 | tf_op jit(solution)/shard_map/all_to_all | solution.py:469
  174.8 1.3 collective-permute-start.8
  176.1 4.4 %radial_both.1 = f32[4,2,6,64,128]{4,3,2,1,0:T(8,128)} custom-call(s32[1]{0:T(128)} %bitcast.side_ref, bf16[256,512]{1,0:T(8,128)(2,1)} %get-tuple-element.51.r_hi, bf16[256,512]{1,0:T(8,128)(2,1)} %get-tuple-element.52.r_lo, bf16[256,512]{1,0:T(8,128)(2,1)} %get-tuple-element.53.f_hi, bf16[256,512]{1,0:T(8,128)(2,1)} %get-tuple-element.54.f_lo, ...), custom_call_target="tpu_custom_call" | custom-call | flops 1024 | bytes 1024 | tf_op jit(solution)/shard_map/radial_both/pallas_call | solution.py:296
  180.5 12.0 %all-to-all-done.5.x_ref = f32[4,6,64,256]{3,2,1,0:T(8,128)S(1)} async-done(((f32[4,6,64,256]{3,2,1,0:T(8,128)}), f32[4,6,64,256]{3,2,1,0:T(8,128)S(1)}, u32[]{:S(2)}, u32[]{:S(2)}) %all-to-all-start.5) | async-done | bytes 1572896 | tf_op jit(solution)/shard_map/all_to_all | solution.py:469
  192.5 1.2 copy-done.2
  193.7 3.6 %all-to-all-start.6 = ((f32[4,2,6,64,128]{4,3,2,1,0:T(8,128)}), f32[4,2,6,64,128]{4,3,2,1,0:T(8,128)S(1)}, u32[]{:S(2)}, u32[]{:S(2)}) async-start(f32[4,2,6,64,128]{4,3,2,1,0:T(8,128)} %radial_both.1), calls=%async_computation.6 | async-start | bytes 3145728 | tf_op jit(solution)/shard_map/all_to_all | solution.py:469
  197.3 12.2 %collective-permute-done.8.rest_0_ = f32[4,6,64,256]{3,2,1,0:T(8,128)} collective-permute-done((f32[4,6,64,256]{3,2,1,0:T(8,128)}, f32[4,6,64,256]{3,2,1,0:T(8,128)}, u32[]{:S(2)}, u32[]{:S(2)}) %collective-permute-start.8) | collective-permute-done | bytes 1572896 | tf_op jit(solution)/shard_map/ppermute | solution.py:474
  209.5 4.0 %radial.5 = f32[4,6,64,256]{3,2,1,0:T(8,128)} custom-call(bf16[256,512]{1,0:T(8,128)(2,1)} %get-tuple-element.51.r_hi, bf16[256,512]{1,0:T(8,128)(2,1)} %get-tuple-element.52.r_lo, f32[4,6,64,256]{3,2,1,0:T(8,128)} %all-to-all-done.3.own_ref, f32[4,6,64,256]{3,2,1,0:T(8,128)} %collective-permute-done.8.rest_0_), custom_call_target="tpu_custom_call" | custom-call | flops 1024 | bytes 1024 | tf_op jit(solution)/shard_map/radial/pallas_call | solution.py:257
  214.2 3.8 %all-to-all-start.7 = ((f32[4,6,64,256]{3,2,1,0:T(8,128)}), f32[4,6,64,256]{3,2,1,0:T(8,128)S(1)}, u32[]{:S(2)}, u32[]{:S(2)}) async-start(f32[4,6,64,256]{3,2,1,0:T(8,128)} %radial.5), calls=%async_computation.7 | async-start | bytes 3145728 | tf_op jit(solution)/shard_map/all_to_all | solution.py:469
  218.1 0.9 slice_bitcast_fusion
  219.0 2.4 %collective-permute-start.7 = (f32[4,6,64,128]{3,2,1,0:T(8,128)}, f32[4,6,64,128]{3,2,1,0:T(8,128)S(1)}, u32[]{:S(2)}, u32[]{:S(2)}) collective-permute-start(f32[4,6,64,128]{3,2,1,0:T(8,128)} %slice_bitcast_fusion), channel_id=1, source_target_pairs={{0,1},{1,0},{2,3},{3,2},{4,5},{5,4},{6,7},{7,6},{8,9},{9,8},{10,11... | collective-permute-start | bytes 2359304 | tf_op jit(solution)/shard_map/ppermute | solution.py:474
  221.4 2.3 place.3.rest_0_
  223.8 2.3 place.4.rest_0_
  226.1 8.3 %all-to-all-done.7.x_ref = f32[4,6,64,256]{3,2,1,0:T(8,128)S(1)} async-done(((f32[4,6,64,256]{3,2,1,0:T(8,128)}), f32[4,6,64,256]{3,2,1,0:T(8,128)S(1)}, u32[]{:S(2)}, u32[]{:S(2)}) %all-to-all-start.7) | async-done | bytes 1572896 | tf_op jit(solution)/shard_map/all_to_all | solution.py:469
  234.4 1.2 copy-done.3
  235.5 2.3 place.5._
  237.9 0.9 copy-done.9
  238.7 2.3 weave.1
  (31 shorter events, 1.5 us)
Async XLA Ops:
  2.5 16.6 %collective-permute-start.1 = (f32[8,8,1024]{2,1,0:T(8,128)}, f32[8,8,1024]{2,1,0:T(8,128)S(1)}, u32[]{:S(2)}, u32[]{:S(2)}) collective-permute-start(f32[8,8,1024]{2,1,0:T(8,128)} %get-tuple-element.44), channel_id=1, source_target_pairs={{1,0},{2,1},{3,2},{4,3},{5,4},{6,5},{7,6},{9,8},{10,9},{11,10},{12... | collective-permute-start | bytes 786440 | tf_op jit(solution)/shard_map/ppermute | solution.py:457
  3.8 16.3 %collective-permute-start = (f32[8,8,1024]{2,1,0:T(8,128)}, f32[8,8,1024]{2,1,0:T(8,128)S(1)}, u32[]{:S(2)}, u32[]{:S(2)}) collective-permute-start(f32[8,8,1024]{2,1,0:T(8,128)} %get-tuple-element.40), channel_id=1, source_target_pairs={{0,1},{1,2},{2,3},{3,4},{4,5},{5,6},{6,7},{8,9},{9,10},{10,11},{11... | collective-permute-start | bytes 786440 | tf_op jit(solution)/shard_map/ppermute | solution.py:456
  13.8 10.7 %copy-start.11 = (f32[64]{0:T(128)S(1)}, f32[64]{0:T(128)}, u32[]{:S(2)}) copy-start(f32[64]{0:T(128)} %param.10) | copy-start | bytes 772
  13.8 11.4 %copy-start.12 = (f32[64]{0:T(128)S(1)}, f32[64]{0:T(128)}, u32[]{:S(2)}) copy-start(f32[64]{0:T(128)} %param.11) | copy-start | bytes 772
  19.1 6.8 %copy-start.7 = (f32[8,8,1024]{2,1,0:T(8,128)}, f32[8,8,1024]{2,1,0:T(8,128)S(1)}, u32[]{:S(2)}) copy-start(f32[8,8,1024]{2,1,0:T(8,128)S(1)} %collective-permute-done.1.rad_hi) | copy-start | bytes 786436
  20.1 5.9 %copy-start.8 = (f32[8,8,1024]{2,1,0:T(8,128)}, f32[8,8,1024]{2,1,0:T(8,128)S(1)}, u32[]{:S(2)}) copy-start(f32[8,8,1024]{2,1,0:T(8,128)S(1)} %collective-permute-done.rad_lo) | copy-start | bytes 786436
  20.1 39.3 %collective-permute-start.2 = (f32[7,64,1024]{2,1,0:T(8,128)}, f32[7,64,1024]{2,1,0:T(8,128)}, u32[]{:S(2)}, u32[]{:S(2)}) collective-permute-start(f32[7,64,1024]{2,1,0:T(8,128)} %get-tuple-element.57), channel_id=1, source_target_pairs={{0,8},{8,16},{16,24},{24,32},{32,40},{40,48},{48,56},{56,64},{64,7... | collective-permute-start | bytes 5505032 | tf_op jit(solution)/shard_map/ppermute | solution.py:464
  23.2 36.2 %collective-permute-start.3 = (f32[7,64,1024]{2,1,0:T(8,128)}, f32[7,64,1024]{2,1,0:T(8,128)}, u32[]{:S(2)}, u32[]{:S(2)}) collective-permute-start(f32[7,64,1024]{2,1,0:T(8,128)} %get-tuple-element.58), channel_id=1, source_target_pairs={{8,0},{16,8},{24,16},{32,24},{40,32},{48,40},{56,48},{64,56},{72,6... | collective-permute-start | bytes 5505032 | tf_op jit(solution)/shard_map/ppermute | solution.py:465
  39.3 26.3 %all-to-all-start = ((f32[4,6,64,256]{3,2,1,0:T(8,128)}), f32[4,6,64,256]{3,2,1,0:T(8,128)S(1)}, u32[]{:S(2)}, u32[]{:S(2)}) async-start(f32[4,6,64,256]{3,2,1,0:T(8,128)} %rhs_2.1), calls=%async_computation | async-start | bytes 3145728 | tf_op jit(solution)/shard_map/all_to_all | solution.py:469
  65.6 3.6 %copy-start.4 = (f32[4,6,64,256]{3,2,1,0:T(8,128)}, f32[4,6,64,256]{3,2,1,0:T(8,128)S(1)}, u32[]{:S(2)}) copy-start(f32[4,6,64,256]{3,2,1,0:T(8,128)S(1)} %all-to-all-done.own_ref) | copy-start | bytes 4718596
  65.6 29.2 %all-to-all-start.1 = ((f32[4,6,64,256]{3,2,1,0:T(8,128)}), f32[4,6,64,256]{3,2,1,0:T(8,128)S(1)}, u32[]{:S(2)}, u32[]{:S(2)}) async-start(f32[4,6,64,256]{3,2,1,0:T(8,128)} %rhs_4.1), calls=%async_computation.1 | async-start | bytes 3145728 | tf_op jit(solution)/shard_map/all_to_all | solution.py:469
  69.2 39.3 %collective-permute-start.4 = (f32[4,6,64,256]{3,2,1,0:T(8,128)S(1)}, f32[4,6,64,256]{3,2,1,0:T(8,128)}, u32[]{:S(2)}, u32[]{:S(2)}) collective-permute-start(f32[4,6,64,256]{3,2,1,0:T(8,128)S(1)} %all-to-all-done.own_ref), channel_id=1, source_target_pairs={{0,1},{1,0},{2,3},{3,2},{4,5},{5,4},{6,7},{7,6},{8,9},{9,8},{10,11... | collective-permute-start | bytes 4718600 | tf_op jit(solution)/shard_map/ppermute | solution.py:474
  94.8 1.2 copy-start.5
  95.9 25.6 %all-to-all-start.2 = ((f32[4,6,64,256]{3,2,1,0:T(8,128)}), f32[4,6,64,256]{3,2,1,0:T(8,128)S(1)}, u32[]{:S(2)}, u32[]{:S(2)}) async-start(f32[4,6,64,256]{3,2,1,0:T(8,128)} %get-tuple-element.64), calls=%async_computation.2 | async-start | bytes 3145728 | tf_op jit(solution)/shard_map/all_to_all | solution.py:469
  100.6 41.4 %collective-permute-start.6 = (f32[4,6,64,256]{3,2,1,0:T(8,128)}, f32[4,6,64,256]{3,2,1,0:T(8,128)}, u32[]{:S(2)}, u32[]{:S(2)}) collective-permute-start(f32[4,6,64,256]{3,2,1,0:T(8,128)} %copy-done.5), channel_id=1, source_target_pairs={{0,1},{1,0},{2,3},{3,2},{4,5},{5,4},{6,7},{7,6},{8,9},{9,8},{10,11... | collective-permute-start | bytes 4718600 | tf_op jit(solution)/shard_map/ppermute | solution.py:474
  121.6 28.2 %copy-start = (f32[4,6,64,256]{3,2,1,0:T(8,128)}, f32[4,6,64,256]{3,2,1,0:T(8,128)S(1)}, u32[]{:S(2)}) copy-start(f32[4,6,64,256]{3,2,1,0:T(8,128)S(1)} %all-to-all-done.2.own_ref) | copy-start | bytes 4718596
  121.6 24.6 %all-to-all-start.3 = ((f32[4,6,64,256]{3,2,1,0:T(8,128)}), f32[4,6,64,256]{3,2,1,0:T(8,128)}, u32[]{:S(2)}, u32[]{:S(2)}) async-start(f32[4,6,64,256]{3,2,1,0:T(8,128)} %get-tuple-element.69), calls=%async_computation.3 | async-start | bytes 3145728 | tf_op jit(solution)/shard_map/all_to_all | solution.py:469
  146.1 23.0 %all-to-all-start.4 = ((f32[4,6,64,256]{3,2,1,0:T(8,128)}), f32[4,6,64,256]{3,2,1,0:T(8,128)S(1)}, u32[]{:S(2)}, u32[]{:S(2)}) async-start(f32[4,6,64,256]{3,2,1,0:T(8,128)} %radial.4), calls=%async_computation.4 | async-start | bytes 3145728 | tf_op jit(solution)/shard_map/all_to_all | solution.py:469
  149.8 19.3 %collective-permute-start.5 = (f32[4,6,64,128]{3,2,1,0:T(8,128)S(1)}, f32[4,6,64,128]{3,2,1,0:T(8,128)S(1)}, u32[]{:S(2)}, u32[]{:S(2)}) collective-permute-start(f32[4,6,64,128]{3,2,1,0:T(8,128)S(1)} %constant_dynamic-slice_fusion), channel_id=1, source_target_pairs={{0,1},{1,0},{2,3},{3,2},{4,5},{5,4},{6,7},{7,6},{8,9},{9,8},{10,11... | collective-permute-start | bytes 2359304 | tf_op jit(solution)/shard_map/ppermute | solution.py:474
  169.1 6.9 %copy-start.10 = (f32[4,6,64,128]{3,2,1,0:T(8,128)}, f32[4,6,64,128]{3,2,1,0:T(8,128)S(1)}, u32[]{:S(2)}) copy-start(f32[4,6,64,128]{3,2,1,0:T(8,128)S(1)} %collective-permute-done.5.other_ref) | copy-start | bytes 2359300
  169.1 1.2 copy-start.6
  170.3 22.2 %all-to-all-start.5 = ((f32[4,6,64,256]{3,2,1,0:T(8,128)}), f32[4,6,64,256]{3,2,1,0:T(8,128)S(1)}, u32[]{:S(2)}, u32[]{:S(2)}) async-start(f32[4,6,64,256]{3,2,1,0:T(8,128)} %radial.3), calls=%async_computation.5 | async-start | bytes 3145728 | tf_op jit(solution)/shard_map/all_to_all | solution.py:469
  174.8 34.7 %collective-permute-start.8 = (f32[4,6,64,256]{3,2,1,0:T(8,128)}, f32[4,6,64,256]{3,2,1,0:T(8,128)}, u32[]{:S(2)}, u32[]{:S(2)}) collective-permute-start(f32[4,6,64,256]{3,2,1,0:T(8,128)} %all-to-all-done.3.own_ref), channel_id=1, source_target_pairs={{0,1},{1,0},{2,3},{3,2},{4,5},{5,4},{6,7},{7,6},{8,9},{9,8},{10,11... | collective-permute-start | bytes 4718600 | tf_op jit(solution)/shard_map/ppermute | solution.py:474
  192.5 1.2 copy-start.2
  193.7 20.5 %all-to-all-start.6 = ((f32[4,2,6,64,128]{4,3,2,1,0:T(8,128)}), f32[4,2,6,64,128]{4,3,2,1,0:T(8,128)S(1)}, u32[]{:S(2)}, u32[]{:S(2)}) async-start(f32[4,2,6,64,128]{4,3,2,1,0:T(8,128)} %radial_both.1), calls=%async_computation.6 | async-start | bytes 3145728 | tf_op jit(solution)/shard_map/all_to_all | solution.py:469
  214.2 3.8 %copy-start.1 = (f32[4,2,6,64,128]{4,3,2,1,0:T(8,128)}, f32[4,2,6,64,128]{4,3,2,1,0:T(8,128)S(1)}, u32[]{:S(2)}) copy-start(f32[4,2,6,64,128]{4,3,2,1,0:T(8,128)S(1)} %all-to-all-done.6.near_ref) | copy-start | bytes 4718596
  214.2 20.1 %all-to-all-start.7 = ((f32[4,6,64,256]{3,2,1,0:T(8,128)}), f32[4,6,64,256]{3,2,1,0:T(8,128)S(1)}, u32[]{:S(2)}, u32[]{:S(2)}) async-start(f32[4,6,64,256]{3,2,1,0:T(8,128)} %radial.5), calls=%async_computation.7 | async-start | bytes 3145728 | tf_op jit(solution)/shard_map/all_to_all | solution.py:469
  219.0 18.9 %collective-permute-start.7 = (f32[4,6,64,128]{3,2,1,0:T(8,128)}, f32[4,6,64,128]{3,2,1,0:T(8,128)S(1)}, u32[]{:S(2)}, u32[]{:S(2)}) collective-permute-start(f32[4,6,64,128]{3,2,1,0:T(8,128)} %slice_bitcast_fusion), channel_id=1, source_target_pairs={{0,1},{1,0},{2,3},{3,2},{4,5},{5,4},{6,7},{7,6},{8,9},{9,8},{10,11... | collective-permute-start | bytes 2359304 | tf_op jit(solution)/shard_map/ppermute | solution.py:474
  234.4 1.2 copy-start.3
  237.9 0.9 copy-start.9

commit v4 on v3

--- a/solution.py
+++ b/solution.py
@@ -13,7 +13,7 @@
 INNER = ((2, 3), (4, 5))
 OUTER = ((0, 1), (6, 7))
 HALF_BYTES = 200 * 1024 * 1024
-COLUMNS = 256
+COLUMNS = 512
 VMEM_LIMIT = 56 * 1024 * 1024
 
 
@@ -458,8 +458,8 @@
     ax_top, ax_bottom = face_call(velocity, after(viscosity, rad_top))
     az = split_call(after(az_inverse, ax_top))
     forward, backward = shifts("ax")
-    ax_top, ax_bottom, rad_lo, rad_hi, *_ = lax.optimization_barrier(
-        (ax_top, ax_bottom, rad_lo, rad_hi, az[0])
+    ax_top, ax_bottom, rad_lo, rad_hi = lax.optimization_barrier(
+        (ax_top, ax_bottom, rad_lo, rad_hi)
     )
     ax_lo = lax.ppermute(ax_top, "ax", forward)
     ax_hi = lax.ppermute(ax_bottom, "ax", backward)

time: 243 us -> 245 us (level)
  starting transfers between devices: 52.5 us -> 56.4 us
    all_to_all x8, waiting for transfers between devices: 40.4 us -> 34.1 us  [exchange(): lax.all_to_all(x, 'rad', split_axis=0, concat_axis=0, tiled=True, axis_in...]
    ppermute x1, waiting for transfers between devices: 0.96 us -> 5.87 us  [local(): rad_lo = lax.ppermute(rad_top, 'rad', forward)]
    ppermute x5, starting transfers between devices: 8.45 us -> 11.6 us  [partner(): return lax.ppermute(x, 'rad', [(i, i ^ 1) for i in range(lines)])]
  transfers between devices with their start and end apart: 17 -> 17, of which waited for: 11 -> 11; matrix products, arithmetic and copies ran while one was open for 1% -> 1% of each run, Pallas kernels for 35% -> 34%
where the time goes in v4:
time: 245 us; the launch traced here: 243 us
  waiting for transfers between devices  91.5 us (37%)
  Pallas kernels  86.8 us (35%)
  starting transfers between devices  56.4 us (23%)
  local copies, waits for them, and re-layouts  8.05 us (3%)
    ppermute x5, waiting for transfers between devices, partner(): return lax.ppermute(x, 'rad', [(i, i ^ 1) for i in range(lines)])  51.1 us
    pallas_call x3, Pallas kernels, rhs_call(): pl.pallas_call(functools.partial(rhs_kernel, groups, bool(ax)), name=f'rh...  46.8 us
    all_to_all x8, waiting for transfers between devices, exchange(): lax.all_to_all(x, 'rad', split_axis=0, concat_axis=0, tiled=True, axis_in...  34.1 us
    all_to_all x8, starting transfers between devices, exchange(): lax.all_to_all(x, 'rad', split_axis=0, concat_axis=0, tiled=True, axis_in...  33 us
    pallas_call x3, Pallas kernels, radial_call(): pl.pallas_call(radial_kernel, name='radial', grid=(slabs // 3,), in_specs...  12.1 us
    ppermute x5, starting transfers between devices, partner(): return lax.ppermute(x, 'rad', [(i, i ^ 1) for i in range(lines)])  11.6 us
    pallas_call x3, Pallas kernels, place_call(): pl.pallas_call(place_kernel, name='place', grid=(len(planes),), in_specs=...  6.98 us
    ppermute x1, starting transfers between devices, local(): rad_lo = lax.ppermute(rad_top, 'rad', forward)  6.07 us
  transfers between devices with their start and end apart: 17, of which 11 were waited for; matrix products, arithmetic and copies ran while one was open for 1% of the time, Pallas kernels for 34%

profile of v4, /device:TPU:0, one launch (start us, length us, event | category | flops | bytes accessed | tf_op | source)
XLA Modules:
  0.0 242.9 jit_solution(6650492217499229471)
XLA Ops:
  0.0 2.5 %lines.1 = (f32[8,8,1024]{2,1,0:T(8,128)}, f32[8,8,1024]{2,1,0:T(8,128)}) custom-call(f32[3,8,64,1024]{3,2,1,0:T(8,128)} %velocity.9, f32[8,64,1024]{2,1,0:T(8,128)} %viscosity.8), custom_call_target="tpu_custom_call" | custom-call | tf_op jit(solution)/shard_map/lines/pallas_call | solution.py:399
  2.5 1.3 collective-permute-start.1
  3.8 6.1 %collective-permute-start = (f32[8,8,1024]{2,1,0:T(8,128)}, f32[8,8,1024]{2,1,0:T(8,128)S(1)}, u32[]{:S(2)}, u32[]{:S(2)}) collective-permute-start(f32[8,8,1024]{2,1,0:T(8,128)} %get-tuple-element.40), channel_id=1, source_target_pairs={{0,1},{1,2},{2,3},{3,4},{4,5},{5,6},{6,7},{8,9},{9,10},{10,11},{11... | collective-permute-start | bytes 786440 | tf_op jit(solution)/shard_map/ppermute | solution.py:456
  9.9 3.9 %faces.1 = (f32[7,64,1024]{2,1,0:T(8,128)}, f32[7,64,1024]{2,1,0:T(8,128)}) custom-call(f32[3,8,64,1024]{3,2,1,0:T(8,128)} %velocity.9, f32[8,64,1024]{2,1,0:T(8,128)} %viscosity.8), custom_call_target="tpu_custom_call" | custom-call | tf_op jit(solution)/shard_map/faces/pallas_call | solution.py:428
  14.2 5.9 %collective-permute-done.rad_lo = f32[8,8,1024]{2,1,0:T(8,128)S(1)} collective-permute-done((f32[8,8,1024]{2,1,0:T(8,128)}, f32[8,8,1024]{2,1,0:T(8,128)S(1)}, u32[]{:S(2)}, u32[]{:S(2)}) %collective-permute-start) | collective-permute-done | bytes 262176 | tf_op jit(solution)/shard_map/ppermute | solution.py:456
  20.0 3.1 %collective-permute-start.2 = (f32[7,64,1024]{2,1,0:T(8,128)}, f32[7,64,1024]{2,1,0:T(8,128)}, u32[]{:S(2)}, u32[]{:S(2)}) collective-permute-start(f32[7,64,1024]{2,1,0:T(8,128)} %get-tuple-element.57), channel_id=1, source_target_pairs={{0,8},{8,16},{16,24},{24,32},{32,40},{40,48},{48,56},{56,64},{64,7... | collective-permute-start | bytes 5505032 | tf_op jit(solution)/shard_map/ppermute | solution.py:464
  23.2 1.3 collective-permute-start.3
  25.2 0.7 copy.20.inv_rt
  25.9 5.3 %split_1024.1 = (bf16[1024,1024]{1,0:T(8,128)(2,1)}, bf16[1024,1024]{1,0:T(8,128)(2,1)}) custom-call(f32[1024,1024]{1,0:T(8,128)} %x_ref.1), custom_call_target="tpu_custom_call" | custom-call | tf_op jit(solution)/shard_map/split_1024/pallas_call | solution.py:39
  31.2 13.0 %rhs_2.1 = f32[4,6,64,256]{3,2,1,0:T(8,128)} custom-call(f32[8]{0:T(128)} %inv_dx.3, f32[64,1]{1,0:T(8,128)} %copy.19.inv_dr, f32[64,1]{1,0:T(8,128)} %copy.20.inv_rt, f32[3,8,64,1024]{3,2,1,0:T(8,128)} %velocity.9, f32[8,64,1024]{2,1,0:T(8,128)} %viscosity.8, f32[8,8,1024]{2,1,0:T(8,128)} %copy-done.8, f32[8,8,1024]{2,1,0:T(8,128)} %copy-done.7, ...), custom_call_target="tpu_custom_call" | custom-call | flops 1024 | bytes 1024 | tf_op jit(solution)/shard_map/rhs_2/pallas_call | solution.py:173
  44.2 4.3 %all-to-all-start = ((f32[4,6,64,256]{3,2,1,0:T(8,128)}), f32[4,6,64,256]{3,2,1,0:T(8,128)S(1)}, u32[]{:S(2)}, u32[]{:S(2)}) async-start(f32[4,6,64,256]{3,2,1,0:T(8,128)} %rhs_2.1), calls=%async_computation | async-start | bytes 3145728 | tf_op jit(solution)/shard_map/all_to_all | solution.py:469
  48.5 2.5 %half.1 = (bf16[256,512]{1,0:T(8,128)(2,1)}, bf16[256,512]{1,0:T(8,128)(2,1)}, bf16[256,512]{1,0:T(8,128)(2,1)}, bf16[256,512]{1,0:T(8,128)(2,1)}) custom-call(s32[1]{0:T(128)} %bitcast.side_ref, f32[512,512]{1,0:T(8,128)} %x_ref.2), custom_call_target="tpu_custom_call" | custom-call | tf_op jit(solution)/shard_map/half/pallas_call | solution.py:217
  51.0 12.9 %rhs_4.1 = f32[4,6,64,256]{3,2,1,0:T(8,128)} custom-call(f32[8]{0:T(128)} %inv_dx.3, f32[64,1]{1,0:T(8,128)} %copy.19.inv_dr, f32[64,1]{1,0:T(8,128)} %copy.20.inv_rt, f32[3,8,64,1024]{3,2,1,0:T(8,128)} %velocity.9, f32[8,64,1024]{2,1,0:T(8,128)} %viscosity.8, f32[8,8,1024]{2,1,0:T(8,128)} %copy-done.8, f32[8,8,1024]{2,1,0:T(8,128)} %copy-done.7, ...), custom_call_target="tpu_custom_call" | custom-call | flops 1024 | bytes 1024 | tf_op jit(solution)/shard_map/rhs_4/pallas_call | solution.py:173
  64.0 6.5 %all-to-all-done.own_ref = f32[4,6,64,256]{3,2,1,0:T(8,128)S(1)} async-done(((f32[4,6,64,256]{3,2,1,0:T(8,128)}), f32[4,6,64,256]{3,2,1,0:T(8,128)S(1)}, u32[]{:S(2)}, u32[]{:S(2)}) %all-to-all-start) | async-done | bytes 1572896 | tf_op jit(solution)/shard_map/all_to_all | solution.py:469
  70.5 3.6 %all-to-all-start.1 = ((f32[4,6,64,256]{3,2,1,0:T(8,128)}), f32[4,6,64,256]{3,2,1,0:T(8,128)S(1)}, u32[]{:S(2)}, u32[]{:S(2)}) async-start(f32[4,6,64,256]{3,2,1,0:T(8,128)} %rhs_4.1), calls=%async_computation.1 | async-start | bytes 3145728 | tf_op jit(solution)/shard_map/all_to_all | solution.py:469
  74.1 4.0 %collective-permute-start.4 = (f32[4,6,64,256]{3,2,1,0:T(8,128)S(1)}, f32[4,6,64,256]{3,2,1,0:T(8,128)}, u32[]{:S(2)}, u32[]{:S(2)}) collective-permute-start(f32[4,6,64,256]{3,2,1,0:T(8,128)S(1)} %all-to-all-done.own_ref), channel_id=1, source_target_pairs={{0,1},{1,0},{2,3},{3,2},{4,5},{5,4},{6,7},{7,6},{8,9},{9,8},{10,11... | collective-permute-start | bytes 4718600 | tf_op jit(solution)/shard_map/ppermute | solution.py:474
  78.1 20.9 %rhs_0.1 = (f32[4,6,64,256]{3,2,1,0:T(8,128)}, f32[4,6,64,256]{3,2,1,0:T(8,128)}) custom-call(f32[8]{0:T(128)} %inv_dx.3, f32[64,1]{1,0:T(8,128)} %copy.19.inv_dr, f32[64,1]{1,0:T(8,128)} %copy.20.inv_rt, f32[3,8,64,1024]{3,2,1,0:T(8,128)} %velocity.9, f32[8,64,1024]{2,1,0:T(8,128)} %viscosity.8, f32[8,8,1024]{2,1,0:T(8,128)} %copy-done.8, ...), custom_call_target="tpu_custom_call" | custom-call | flops 1024 | bytes 1024 | tf_op jit(solution)/shard_map/rhs_0/pallas_call | solution.py:173
  99.0 1.2 copy-done.5
  100.1 4.7 %all-to-all-start.2 = ((f32[4,6,64,256]{3,2,1,0:T(8,128)}), f32[4,6,64,256]{3,2,1,0:T(8,128)S(1)}, u32[]{:S(2)}, u32[]{:S(2)}) async-start(f32[4,6,64,256]{3,2,1,0:T(8,128)} %get-tuple-element.64), calls=%async_computation.2 | async-start | bytes 3145728 | tf_op jit(solution)/shard_map/all_to_all | solution.py:469
  104.8 8.5 %collective-permute-done.4.rest_0_ = f32[4,6,64,256]{3,2,1,0:T(8,128)} collective-permute-done((f32[4,6,64,256]{3,2,1,0:T(8,128)S(1)}, f32[4,6,64,256]{3,2,1,0:T(8,128)}, u32[]{:S(2)}, u32[]{:S(2)}) %collective-permute-start.4) | collective-permute-done | bytes 1572896 | tf_op jit(solution)/shard_map/ppermute | solution.py:474
  113.4 4.0 %radial.4 = f32[4,6,64,256]{3,2,1,0:T(8,128)} custom-call(bf16[256,512]{1,0:T(8,128)(2,1)} %get-tuple-element.51.r_hi, bf16[256,512]{1,0:T(8,128)(2,1)} %get-tuple-element.52.r_lo, f32[4,6,64,256]{3,2,1,0:T(8,128)} %copy-done.4, f32[4,6,64,256]{3,2,1,0:T(8,128)} %collective-permute-done.4.rest_0_), custom_call_target="tpu_custom_call" | custom-call | flops 1024 | bytes 1024 | tf_op jit(solution)/shard_map/radial/pallas_call | solution.py:257
  117.4 7.7 %all-to-all-done.2.own_ref = f32[4,6,64,256]{3,2,1,0:T(8,128)S(1)} async-done(((f32[4,6,64,256]{3,2,1,0:T(8,128)}), f32[4,6,64,256]{3,2,1,0:T(8,128)S(1)}, u32[]{:S(2)}, u32[]{:S(2)}) %all-to-all-start.2) | async-done | bytes 1572896 | tf_op jit(solution)/shard_map/all_to_all | solution.py:469
  125.1 4.3 %all-to-all-start.3 = ((f32[4,6,64,256]{3,2,1,0:T(8,128)}), f32[4,6,64,256]{3,2,1,0:T(8,128)}, u32[]{:S(2)}, u32[]{:S(2)}) async-start(f32[4,6,64,256]{3,2,1,0:T(8,128)} %get-tuple-element.69), calls=%async_computation.3 | async-start | bytes 3145728 | tf_op jit(solution)/shard_map/all_to_all | solution.py:469
  129.5 16.9 %collective-permute-done.6.rest_0_ = f32[4,6,64,256]{3,2,1,0:T(8,128)} collective-permute-done((f32[4,6,64,256]{3,2,1,0:T(8,128)}, f32[4,6,64,256]{3,2,1,0:T(8,128)}, u32[]{:S(2)}, u32[]{:S(2)}) %collective-permute-start.6) | collective-permute-done | bytes 1572896 | tf_op jit(solution)/shard_map/ppermute | solution.py:474
  146.4 2.6 %all-to-all-done.3.own_ref = f32[4,6,64,256]{3,2,1,0:T(8,128)} async-done(((f32[4,6,64,256]{3,2,1,0:T(8,128)}), f32[4,6,64,256]{3,2,1,0:T(8,128)}, u32[]{:S(2)}, u32[]{:S(2)}) %all-to-all-start.3) | async-done | bytes 1572896 | tf_op jit(solution)/shard_map/all_to_all | solution.py:469
  149.0 3.6 %all-to-all-start.4 = ((f32[4,6,64,256]{3,2,1,0:T(8,128)}), f32[4,6,64,256]{3,2,1,0:T(8,128)S(1)}, u32[]{:S(2)}, u32[]{:S(2)}) async-start(f32[4,6,64,256]{3,2,1,0:T(8,128)} %radial.4), calls=%async_computation.4 | async-start | bytes 3145728 | tf_op jit(solution)/shard_map/all_to_all | solution.py:469
  152.7 1.7 collective-permute-start.5
  154.4 4.0 %radial.3 = f32[4,6,64,256]{3,2,1,0:T(8,128)} custom-call(bf16[256,512]{1,0:T(8,128)(2,1)} %get-tuple-element.51.r_hi, bf16[256,512]{1,0:T(8,128)(2,1)} %get-tuple-element.52.r_lo, f32[4,6,64,256]{3,2,1,0:T(8,128)} %copy-done.5, f32[4,6,64,256]{3,2,1,0:T(8,128)} %collective-permute-done.6.rest_0_), custom_call_target="tpu_custom_call" | custom-call | flops 1024 | bytes 1024 | tf_op jit(solution)/shard_map/radial/pallas_call | solution.py:257
  158.4 12.9 %collective-permute-done.5.other_ref = f32[4,6,64,128]{3,2,1,0:T(8,128)S(1)} collective-permute-done((f32[4,6,64,128]{3,2,1,0:T(8,128)S(1)}, f32[4,6,64,128]{3,2,1,0:T(8,128)S(1)}, u32[]{:S(2)}, u32[]{:S(2)}) %collective-permute-start.5) | collective-permute-done | bytes 786464 | tf_op jit(solution)/shard_map/ppermute | solution.py:474
  171.3 1.2 copy-done.6
  172.5 4.5 %all-to-all-start.5 = ((f32[4,6,64,256]{3,2,1,0:T(8,128)}), f32[4,6,64,256]{3,2,1,0:T(8,128)S(1)}, u32[]{:S(2)}, u32[]{:S(2)}) async-start(f32[4,6,64,256]{3,2,1,0:T(8,128)} %radial.3), calls=%async_computation.5 | async-start | bytes 3145728 | tf_op jit(solution)/shard_map/all_to_all | solution.py:469
  177.0 2.6 %collective-permute-start.8 = (f32[4,6,64,256]{3,2,1,0:T(8,128)}, f32[4,6,64,256]{3,2,1,0:T(8,128)}, u32[]{:S(2)}, u32[]{:S(2)}) collective-permute-start(f32[4,6,64,256]{3,2,1,0:T(8,128)} %all-to-all-done.3.own_ref), channel_id=1, source_target_pairs={{0,1},{1,0},{2,3},{3,2},{4,5},{5,4},{6,7},{7,6},{8,9},{9,8},{10,11... | collective-permute-start | bytes 4718600 | tf_op jit(solution)/shard_map/ppermute | solution.py:474
  179.6 4.4 %radial_both.1 = f32[4,2,6,64,128]{4,3,2,1,0:T(8,128)} custom-call(s32[1]{0:T(128)} %bitcast.side_ref, bf16[256,512]{1,0:T(8,128)(2,1)} %get-tuple-element.51.r_hi, bf16[256,512]{1,0:T(8,128)(2,1)} %get-tuple-element.52.r_lo, bf16[256,512]{1,0:T(8,128)(2,1)} %get-tuple-element.53.f_hi, bf16[256,512]{1,0:T(8,128)(2,1)} %get-tuple-element.54.f_lo, ...), custom_call_target="tpu_custom_call" | custom-call | flops 1024 | bytes 1024 | tf_op jit(solution)/shard_map/radial_both/pallas_call | solution.py:296
  184.1 10.0 %all-to-all-done.5.x_ref = f32[4,6,64,256]{3,2,1,0:T(8,128)S(1)} async-done(((f32[4,6,64,256]{3,2,1,0:T(8,128)}), f32[4,6,64,256]{3,2,1,0:T(8,128)S(1)}, u32[]{:S(2)}, u32[]{:S(2)}) %all-to-all-start.5) | async-done | bytes 1572896 | tf_op jit(solution)/shard_map/all_to_all | solution.py:469
  194.0 1.2 copy-done.2
  195.2 3.6 %all-to-all-start.6 = ((f32[4,2,6,64,128]{4,3,2,1,0:T(8,128)}), f32[4,2,6,64,128]{4,3,2,1,0:T(8,128)S(1)}, u32[]{:S(2)}, u32[]{:S(2)}) async-start(f32[4,2,6,64,128]{4,3,2,1,0:T(8,128)} %radial_both.1), calls=%async_computation.6 | async-start | bytes 3145728 | tf_op jit(solution)/shard_map/all_to_all | solution.py:469
  198.8 12.7 %collective-permute-done.8.rest_0_ = f32[4,6,64,256]{3,2,1,0:T(8,128)} collective-permute-done((f32[4,6,64,256]{3,2,1,0:T(8,128)}, f32[4,6,64,256]{3,2,1,0:T(8,128)}, u32[]{:S(2)}, u32[]{:S(2)}) %collective-permute-start.8) | collective-permute-done | bytes 1572896 | tf_op jit(solution)/shard_map/ppermute | solution.py:474
  211.5 4.0 %radial.5 = f32[4,6,64,256]{3,2,1,0:T(8,128)} custom-call(bf16[256,512]{1,0:T(8,128)(2,1)} %get-tuple-element.51.r_hi, bf16[256,512]{1,0:T(8,128)(2,1)} %get-tuple-element.52.r_lo, f32[4,6,64,256]{3,2,1,0:T(8,128)} %all-to-all-done.3.own_ref, f32[4,6,64,256]{3,2,1,0:T(8,128)} %collective-permute-done.8.rest_0_), custom_call_target="tpu_custom_call" | custom-call | flops 1024 | bytes 1024 | tf_op jit(solution)/shard_map/radial/pallas_call | solution.py:257
  215.6 4.5 %all-to-all-start.7 = ((f32[4,6,64,256]{3,2,1,0:T(8,128)}), f32[4,6,64,256]{3,2,1,0:T(8,128)S(1)}, u32[]{:S(2)}, u32[]{:S(2)}) async-start(f32[4,6,64,256]{3,2,1,0:T(8,128)} %radial.5), calls=%async_computation.7 | async-start | bytes 3145728 | tf_op jit(solution)/shard_map/all_to_all | solution.py:469
  220.1 0.9 slice_bitcast_fusion
  221.0 3.3 %collective-permute-start.7 = (f32[4,6,64,128]{3,2,1,0:T(8,128)}, f32[4,6,64,128]{3,2,1,0:T(8,128)S(1)}, u32[]{:S(2)}, u32[]{:S(2)}) collective-permute-start(f32[4,6,64,128]{3,2,1,0:T(8,128)} %slice_bitcast_fusion), channel_id=1, source_target_pairs={{0,1},{1,0},{2,3},{3,2},{4,5},{5,4},{6,7},{7,6},{8,9},{9,8},{10,11... | collective-permute-start | bytes 2359304 | tf_op jit(solution)/shard_map/ppermute | solution.py:474
  224.3 2.3 place.3.rest_0_
  226.7 2.3 place.4.rest_0_
  229.0 7.2 %all-to-all-done.7.x_ref = f32[4,6,64,256]{3,2,1,0:T(8,128)S(1)} async-done(((f32[4,6,64,256]{3,2,1,0:T(8,128)}), f32[4,6,64,256]{3,2,1,0:T(8,128)S(1)}, u32[]{:S(2)}, u32[]{:S(2)}) %all-to-all-start.7) | async-done | bytes 1572896 | tf_op jit(solution)/shard_map/all_to_all | solution.py:469
  236.2 1.2 copy-done.3
  237.4 2.3 place.5._
  239.7 0.9 copy-done.9
  240.6 2.3 weave.1
  (31 shorter events, 1.2 us)
Async XLA Ops:
  2.5 11.7 %collective-permute-start.1 = (f32[8,8,1024]{2,1,0:T(8,128)}, f32[8,8,1024]{2,1,0:T(8,128)S(1)}, u32[]{:S(2)}, u32[]{:S(2)}) collective-permute-start(f32[8,8,1024]{2,1,0:T(8,128)} %get-tuple-element.44), channel_id=1, source_target_pairs={{1,0},{2,1},{3,2},{4,3},{5,4},{6,5},{7,6},{9,8},{10,9},{11,10},{12... | collective-permute-start | bytes 786440 | tf_op jit(solution)/shard_map/ppermute | solution.py:457
  3.8 20.7 %copy-start.11 = (f32[64]{0:T(128)S(1)}, f32[64]{0:T(128)}, u32[]{:S(2)}) copy-start(f32[64]{0:T(128)} %param.10) | copy-start | bytes 772
  3.8 21.4 %copy-start.12 = (f32[64]{0:T(128)S(1)}, f32[64]{0:T(128)}, u32[]{:S(2)}) copy-start(f32[64]{0:T(128)} %param.11) | copy-start | bytes 772
  3.8 16.2 %collective-permute-start = (f32[8,8,1024]{2,1,0:T(8,128)}, f32[8,8,1024]{2,1,0:T(8,128)S(1)}, u32[]{:S(2)}, u32[]{:S(2)}) collective-permute-start(f32[8,8,1024]{2,1,0:T(8,128)} %get-tuple-element.40), channel_id=1, source_target_pairs={{0,1},{1,2},{2,3},{3,4},{4,5},{5,6},{6,7},{8,9},{9,10},{10,11},{11... | collective-permute-start | bytes 786440 | tf_op jit(solution)/shard_map/ppermute | solution.py:456
  14.2 17.0 %copy-start.7 = (f32[8,8,1024]{2,1,0:T(8,128)}, f32[8,8,1024]{2,1,0:T(8,128)S(1)}, u32[]{:S(2)}) copy-start(f32[8,8,1024]{2,1,0:T(8,128)S(1)} %collective-permute-done.1.rad_hi) | copy-start | bytes 786436
  20.0 11.2 %copy-start.8 = (f32[8,8,1024]{2,1,0:T(8,128)}, f32[8,8,1024]{2,1,0:T(8,128)S(1)}, u32[]{:S(2)}) copy-start(f32[8,8,1024]{2,1,0:T(8,128)S(1)} %collective-permute-done.rad_lo) | copy-start | bytes 786436
  20.0 43.9 %collective-permute-start.2 = (f32[7,64,1024]{2,1,0:T(8,128)}, f32[7,64,1024]{2,1,0:T(8,128)}, u32[]{:S(2)}, u32[]{:S(2)}) collective-permute-start(f32[7,64,1024]{2,1,0:T(8,128)} %get-tuple-element.57), channel_id=1, source_target_pairs={{0,8},{8,16},{16,24},{24,32},{32,40},{40,48},{48,56},{56,64},{64,7... | collective-permute-start | bytes 5505032 | tf_op jit(solution)/shard_map/ppermute | solution.py:464
  23.2 40.8 %collective-permute-start.3 = (f32[7,64,1024]{2,1,0:T(8,128)}, f32[7,64,1024]{2,1,0:T(8,128)}, u32[]{:S(2)}, u32[]{:S(2)}) collective-permute-start(f32[7,64,1024]{2,1,0:T(8,128)} %get-tuple-element.58), channel_id=1, source_target_pairs={{8,0},{16,8},{24,16},{32,24},{40,32},{48,40},{56,48},{64,56},{72,6... | collective-permute-start | bytes 5505032 | tf_op jit(solution)/shard_map/ppermute | solution.py:465
  44.2 26.3 %all-to-all-start = ((f32[4,6,64,256]{3,2,1,0:T(8,128)}), f32[4,6,64,256]{3,2,1,0:T(8,128)S(1)}, u32[]{:S(2)}, u32[]{:S(2)}) async-start(f32[4,6,64,256]{3,2,1,0:T(8,128)} %rhs_2.1), calls=%async_computation | async-start | bytes 3145728 | tf_op jit(solution)/shard_map/all_to_all | solution.py:469
  70.5 3.6 %copy-start.4 = (f32[4,6,64,256]{3,2,1,0:T(8,128)}, f32[4,6,64,256]{3,2,1,0:T(8,128)S(1)}, u32[]{:S(2)}) copy-start(f32[4,6,64,256]{3,2,1,0:T(8,128)S(1)} %all-to-all-done.own_ref) | copy-start | bytes 4718596
  70.5 28.4 %all-to-all-start.1 = ((f32[4,6,64,256]{3,2,1,0:T(8,128)}), f32[4,6,64,256]{3,2,1,0:T(8,128)S(1)}, u32[]{:S(2)}, u32[]{:S(2)}) async-start(f32[4,6,64,256]{3,2,1,0:T(8,128)} %rhs_4.1), calls=%async_computation.1 | async-start | bytes 3145728 | tf_op jit(solution)/shard_map/all_to_all | solution.py:469
  74.1 39.3 %collective-permute-start.4 = (f32[4,6,64,256]{3,2,1,0:T(8,128)S(1)}, f32[4,6,64,256]{3,2,1,0:T(8,128)}, u32[]{:S(2)}, u32[]{:S(2)}) collective-permute-start(f32[4,6,64,256]{3,2,1,0:T(8,128)S(1)} %all-to-all-done.own_ref), channel_id=1, source_target_pairs={{0,1},{1,0},{2,3},{3,2},{4,5},{5,4},{6,7},{7,6},{8,9},{9,8},{10,11... | collective-permute-start | bytes 4718600 | tf_op jit(solution)/shard_map/ppermute | solution.py:474
  99.0 1.2 copy-start.5
  100.1 25.0 %all-to-all-start.2 = ((f32[4,6,64,256]{3,2,1,0:T(8,128)}), f32[4,6,64,256]{3,2,1,0:T(8,128)S(1)}, u32[]{:S(2)}, u32[]{:S(2)}) async-start(f32[4,6,64,256]{3,2,1,0:T(8,128)} %get-tuple-element.64), calls=%async_computation.2 | async-start | bytes 3145728 | tf_op jit(solution)/shard_map/all_to_all | solution.py:469
  104.8 41.6 %collective-permute-start.6 = (f32[4,6,64,256]{3,2,1,0:T(8,128)}, f32[4,6,64,256]{3,2,1,0:T(8,128)}, u32[]{:S(2)}, u32[]{:S(2)}) collective-permute-start(f32[4,6,64,256]{3,2,1,0:T(8,128)} %copy-done.5), channel_id=1, source_target_pairs={{0,1},{1,0},{2,3},{3,2},{4,5},{5,4},{6,7},{7,6},{8,9},{9,8},{10,11... | collective-permute-start | bytes 4718600 | tf_op jit(solution)/shard_map/ppermute | solution.py:474
  125.1 27.5 %copy-start = (f32[4,6,64,256]{3,2,1,0:T(8,128)}, f32[4,6,64,256]{3,2,1,0:T(8,128)S(1)}, u32[]{:S(2)}) copy-start(f32[4,6,64,256]{3,2,1,0:T(8,128)S(1)} %all-to-all-done.2.own_ref) | copy-start | bytes 4718596
  125.1 23.9 %all-to-all-start.3 = ((f32[4,6,64,256]{3,2,1,0:T(8,128)}), f32[4,6,64,256]{3,2,1,0:T(8,128)}, u32[]{:S(2)}, u32[]{:S(2)}) async-start(f32[4,6,64,256]{3,2,1,0:T(8,128)} %get-tuple-element.69), calls=%async_computation.3 | async-start | bytes 3145728 | tf_op jit(solution)/shard_map/all_to_all | solution.py:469
  149.0 22.3 %all-to-all-start.4 = ((f32[4,6,64,256]{3,2,1,0:T(8,128)}), f32[4,6,64,256]{3,2,1,0:T(8,128)S(1)}, u32[]{:S(2)}, u32[]{:S(2)}) async-start(f32[4,6,64,256]{3,2,1,0:T(8,128)} %radial.4), calls=%async_computation.4 | async-start | bytes 3145728 | tf_op jit(solution)/shard_map/all_to_all | solution.py:469
  152.7 18.6 %collective-permute-start.5 = (f32[4,6,64,128]{3,2,1,0:T(8,128)S(1)}, f32[4,6,64,128]{3,2,1,0:T(8,128)S(1)}, u32[]{:S(2)}, u32[]{:S(2)}) collective-permute-start(f32[4,6,64,128]{3,2,1,0:T(8,128)S(1)} %constant_dynamic-slice_fusion), channel_id=1, source_target_pairs={{0,1},{1,0},{2,3},{3,2},{4,5},{5,4},{6,7},{7,6},{8,9},{9,8},{10,11... | collective-permute-start | bytes 2359304 | tf_op jit(solution)/shard_map/ppermute | solution.py:474
  171.3 8.3 %copy-start.10 = (f32[4,6,64,128]{3,2,1,0:T(8,128)}, f32[4,6,64,128]{3,2,1,0:T(8,128)S(1)}, u32[]{:S(2)}) copy-start(f32[4,6,64,128]{3,2,1,0:T(8,128)S(1)} %collective-permute-done.5.other_ref) | copy-start | bytes 2359300
  171.3 1.2 copy-start.6
  172.5 21.5 %all-to-all-start.5 = ((f32[4,6,64,256]{3,2,1,0:T(8,128)}), f32[4,6,64,256]{3,2,1,0:T(8,128)S(1)}, u32[]{:S(2)}, u32[]{:S(2)}) async-start(f32[4,6,64,256]{3,2,1,0:T(8,128)} %radial.3), calls=%async_computation.5 | async-start | bytes 3145728 | tf_op jit(solution)/shard_map/all_to_all | solution.py:469
  177.0 34.6 %collective-permute-start.8 = (f32[4,6,64,256]{3,2,1,0:T(8,128)}, f32[4,6,64,256]{3,2,1,0:T(8,128)}, u32[]{:S(2)}, u32[]{:S(2)}) collective-permute-start(f32[4,6,64,256]{3,2,1,0:T(8,128)} %all-to-all-done.3.own_ref), channel_id=1, source_target_pairs={{0,1},{1,0},{2,3},{3,2},{4,5},{5,4},{6,7},{7,6},{8,9},{9,8},{10,11... | collective-permute-start | bytes 4718600 | tf_op jit(solution)/shard_map/ppermute | solution.py:474
  194.0 1.2 copy-start.2
  195.2 20.3 %all-to-all-start.6 = ((f32[4,2,6,64,128]{4,3,2,1,0:T(8,128)}), f32[4,2,6,64,128]{4,3,2,1,0:T(8,128)S(1)}, u32[]{:S(2)}, u32[]{:S(2)}) async-start(f32[4,2,6,64,128]{4,3,2,1,0:T(8,128)} %radial_both.1), calls=%async_computation.6 | async-start | bytes 3145728 | tf_op jit(solution)/shard_map/all_to_all | solution.py:469
  215.5 4.5 %copy-start.1 = (f32[4,2,6,64,128]{4,3,2,1,0:T(8,128)}, f32[4,2,6,64,128]{4,3,2,1,0:T(8,128)S(1)}, u32[]{:S(2)}) copy-start(f32[4,2,6,64,128]{4,3,2,1,0:T(8,128)S(1)} %all-to-all-done.6.near_ref) | copy-start | bytes 4718596
  215.6 20.7 %all-to-all-start.7 = ((f32[4,6,64,256]{3,2,1,0:T(8,128)}), f32[4,6,64,256]{3,2,1,0:T(8,128)S(1)}, u32[]{:S(2)}, u32[]{:S(2)}) async-start(f32[4,6,64,256]{3,2,1,0:T(8,128)} %radial.5), calls=%async_computation.7 | async-start | bytes 3145728 | tf_op jit(solution)/shard_map/all_to_all | solution.py:469
  221.0 18.7 %collective-permute-start.7 = (f32[4,6,64,128]{3,2,1,0:T(8,128)}, f32[4,6,64,128]{3,2,1,0:T(8,128)S(1)}, u32[]{:S(2)}, u32[]{:S(2)}) collective-permute-start(f32[4,6,64,128]{3,2,1,0:T(8,128)} %slice_bitcast_fusion), channel_id=1, source_target_pairs={{0,1},{1,0},{2,3},{3,2},{4,5},{5,4},{6,7},{7,6},{8,9},{9,8},{10,11... | collective-permute-start | bytes 2359304 | tf_op jit(solution)/shard_map/ppermute | solution.py:474
  236.2 1.2 copy-start.3
  239.7 0.9 copy-start.9

commit v5 on v3

--- a/solution.py
+++ b/solution.py
@@ -13,7 +13,7 @@
 INNER = ((2, 3), (4, 5))
 OUTER = ((0, 1), (6, 7))
 HALF_BYTES = 200 * 1024 * 1024
-COLUMNS = 256
+COLUMNS = 512
 VMEM_LIMIT = 56 * 1024 * 1024
 
 
@@ -481,7 +481,9 @@
     own = [exchange(first)]
     other = [(partner(after(own[0], ax_lo)),)]
     own.append(exchange(after(second, own[0])))
-    edges = rhs_call(OUTER, parts, after(inv_dx, own[0]), *common, (ax_lo, ax_hi), az)
+    dx, faces = after(inv_dx, own[0]), (ax_lo, ax_hi)
+    edges = rhs_call(OUTER[:1], parts, dx, *common, faces, az)
+    edges += rhs_call(OUTER[1:], parts, after(dx, edges[0], own[1]), *common, faces, az)
     own.append(exchange(after(edges[0], own[1])))
     other.append((partner(after(own[1], edges[0])),))
     solved = [radial_call(rad[:2], own[k], other[k]) for k in range(2)]

time: 243 us -> 248 us (1.021)
  starting transfers between devices: 52.5 us -> 61.4 us
  waiting for transfers between devices: 92 us -> 85.5 us
  Pallas kernels: 88.2 us -> 92.5 us
    ppermute x5, starting transfers between devices: 8.45 us -> 18 us  [partner(): return lax.ppermute(x, 'rad', [(i, i ^ 1) for i in range(lines)])]
    pallas_call x3 -> x4, Pallas kernels: 48.2 us -> 52.5 us  [rhs_call(): pl.pallas_call(functools.partial(rhs_kernel, groups, bool(ax)), name=f'rh...]
    all_to_all x8, waiting for transfers between devices: 40.4 us -> 37.1 us  [exchange(): lax.all_to_all(x, 'rad', split_axis=0, concat_axis=0, tiled=True, axis_in...]
    ppermute x5, waiting for transfers between devices: 50.7 us -> 47.4 us  [partner(): return lax.ppermute(x, 'rad', [(i, i ^ 1) for i in range(lines)])]
    unnamed x26 -> x24, local copies, waits for them, and re-layouts: 5.64 us -> 4.37 us
  transfers between devices with their start and end apart: 17 -> 17, of which waited for: 11 -> 11; matrix products, arithmetic and copies ran while one was open for 1% -> 1% of each run, Pallas kernels for 35% -> 36%
where the time goes in v5:
time: 248 us; the launch traced here: 246 us
  Pallas kernels  92.5 us (37%)
  waiting for transfers between devices  85.5 us (34%)
  starting transfers between devices  61.4 us (25%)
  local copies, waits for them, and re-layouts  6.76 us (3%)
    pallas_call x4, Pallas kernels, rhs_call(): pl.pallas_call(functools.partial(rhs_kernel, groups, bool(ax)), name=f'rh...  52.5 us
    ppermute x5, waiting for transfers between devices, partner(): return lax.ppermute(x, 'rad', [(i, i ^ 1) for i in range(lines)])  47.4 us
    all_to_all x8, waiting for transfers between devices, exchange(): lax.all_to_all(x, 'rad', split_axis=0, concat_axis=0, tiled=True, axis_in...  37.1 us
    all_to_all x8, starting transfers between devices, exchange(): lax.all_to_all(x, 'rad', split_axis=0, concat_axis=0, tiled=True, axis_in...  32.8 us
    ppermute x5, starting transfers between devices, partner(): return lax.ppermute(x, 'rad', [(i, i ^ 1) for i in range(lines)])  18 us
    pallas_call x3, Pallas kernels, radial_call(): pl.pallas_call(radial_kernel, name='radial', grid=(slabs // 3,), in_specs...  12.1 us
    pallas_call x3, Pallas kernels, place_call(): pl.pallas_call(place_kernel, name='place', grid=(len(planes),), in_specs=...  6.98 us
    ppermute x1, starting transfers between devices, local(): rad_lo = lax.ppermute(rad_top, 'rad', forward)  6.07 us
  transfers between devices with their start and end apart: 17, of which 11 were waited for; matrix products, arithmetic and copies ran while one was open for 1% of the time, Pallas kernels for 36%

profile of v5, /device:TPU:0, one launch (start us, length us, event | category | flops | bytes accessed | tf_op | source)
XLA Modules:
  0.0 246.4 jit_solution(15509684618322936772)
XLA Ops:
  0.0 2.5 %lines.1 = (f32[8,8,1024]{2,1,0:T(8,128)}, f32[8,8,1024]{2,1,0:T(8,128)}) custom-call(f32[3,8,64,1024]{3,2,1,0:T(8,128)} %velocity.11, f32[8,64,1024]{2,1,0:T(8,128)} %viscosity.10), custom_call_target="tpu_custom_call" | custom-call | tf_op jit(solution)/shard_map/lines/pallas_call | solution.py:399
  2.5 1.3 collective-permute-start.1
  3.8 6.1 %collective-permute-start = (f32[8,8,1024]{2,1,0:T(8,128)}, f32[8,8,1024]{2,1,0:T(8,128)S(1)}, u32[]{:S(2)}, u32[]{:S(2)}) collective-permute-start(f32[8,8,1024]{2,1,0:T(8,128)} %get-tuple-element.39), channel_id=1, source_target_pairs={{0,1},{1,2},{2,3},{3,4},{4,5},{5,6},{6,7},{8,9},{9,10},{10,11},{11... | collective-permute-start | bytes 786440 | tf_op jit(solution)/shard_map/ppermute | solution.py:456
  9.9 3.8 %faces.1 = (f32[7,64,1024]{2,1,0:T(8,128)}, f32[7,64,1024]{2,1,0:T(8,128)}) custom-call(f32[3,8,64,1024]{3,2,1,0:T(8,128)} %velocity.11, f32[8,64,1024]{2,1,0:T(8,128)} %viscosity.10), custom_call_target="tpu_custom_call" | custom-call | tf_op jit(solution)/shard_map/faces/pallas_call | solution.py:428
  13.7 5.3 %split_1024.1 = (bf16[1024,1024]{1,0:T(8,128)(2,1)}, bf16[1024,1024]{1,0:T(8,128)(2,1)}) custom-call(f32[1024,1024]{1,0:T(8,128)} %x_ref.1), custom_call_target="tpu_custom_call" | custom-call | tf_op jit(solution)/shard_map/split_1024/pallas_call | solution.py:39
  19.0 1.0 collective-permute-done.rad_lo
  20.1 2.0 collective-permute-start.2
  22.1 1.3 collective-permute-start.3
  23.4 0.7 copy.21.inv_dr
  24.8 13.0 %rhs_2.1 = f32[4,6,64,256]{3,2,1,0:T(8,128)} custom-call(f32[8]{0:T(128)} %inv_dx.4, f32[64,1]{1,0:T(8,128)} %copy.21.inv_dr, f32[64,1]{1,0:T(8,128)} %copy.22.inv_rt, f32[3,8,64,1024]{3,2,1,0:T(8,128)} %velocity.11, f32[8,64,1024]{2,1,0:T(8,128)} %viscosity.10, f32[8,8,1024]{2,1,0:T(8,128)} %copy-done.8, f32[8,8,1024]{2,1,0:T(8,128)} %copy-done.7, ...), custom_call_target="tpu_custom_call" | custom-call | flops 1024 | bytes 1024 | tf_op jit(solution)/shard_map/rhs_2/pallas_call | solution.py:173
  37.8 4.3 %all-to-all-start = ((f32[4,6,64,256]{3,2,1,0:T(8,128)}), f32[4,6,64,256]{3,2,1,0:T(8,128)S(1)}, u32[]{:S(2)}, u32[]{:S(2)}) async-start(f32[4,6,64,256]{3,2,1,0:T(8,128)} %rhs_2.1), calls=%async_computation | async-start | bytes 3145728 | tf_op jit(solution)/shard_map/all_to_all | solution.py:469
  42.1 2.5 %half.1 = (bf16[256,512]{1,0:T(8,128)(2,1)}, bf16[256,512]{1,0:T(8,128)(2,1)}, bf16[256,512]{1,0:T(8,128)(2,1)}, bf16[256,512]{1,0:T(8,128)(2,1)}) custom-call(s32[1]{0:T(128)} %bitcast.side_ref, f32[512,512]{1,0:T(8,128)} %x_ref.2), custom_call_target="tpu_custom_call" | custom-call | tf_op jit(solution)/shard_map/half/pallas_call | solution.py:217
  44.6 12.9 %rhs_4.1 = f32[4,6,64,256]{3,2,1,0:T(8,128)} custom-call(f32[8]{0:T(128)} %inv_dx.4, f32[64,1]{1,0:T(8,128)} %copy.21.inv_dr, f32[64,1]{1,0:T(8,128)} %copy.22.inv_rt, f32[3,8,64,1024]{3,2,1,0:T(8,128)} %velocity.11, f32[8,64,1024]{2,1,0:T(8,128)} %viscosity.10, f32[8,8,1024]{2,1,0:T(8,128)} %copy-done.8, f32[8,8,1024]{2,1,0:T(8,128)} %copy-done.7, ...), custom_call_target="tpu_custom_call" | custom-call | flops 1024 | bytes 1024 | tf_op jit(solution)/shard_map/rhs_4/pallas_call | solution.py:173
  57.5 6.0 %all-to-all-done.own_ref = f32[4,6,64,256]{3,2,1,0:T(8,128)S(1)} async-done(((f32[4,6,64,256]{3,2,1,0:T(8,128)}), f32[4,6,64,256]{3,2,1,0:T(8,128)S(1)}, u32[]{:S(2)}, u32[]{:S(2)}) %all-to-all-start) | async-done | bytes 1572896 | tf_op jit(solution)/shard_map/all_to_all | solution.py:469
  63.5 4.4 %all-to-all-start.1 = ((f32[4,6,64,256]{3,2,1,0:T(8,128)}), f32[4,6,64,256]{3,2,1,0:T(8,128)}, u32[]{:S(2)}, u32[]{:S(2)}) async-start(f32[4,6,64,256]{3,2,1,0:T(8,128)} %rhs_4.1), calls=%async_computation.1 | async-start | bytes 3145728 | tf_op jit(solution)/shard_map/all_to_all | solution.py:469
  67.9 4.1 %collective-permute-start.4 = (f32[4,6,64,256]{3,2,1,0:T(8,128)S(1)}, f32[4,6,64,256]{3,2,1,0:T(8,128)}, u32[]{:S(2)}, u32[]{:S(2)}) collective-permute-start(f32[4,6,64,256]{3,2,1,0:T(8,128)S(1)} %all-to-all-done.own_ref), channel_id=1, source_target_pairs={{0,1},{1,0},{2,3},{3,2},{4,5},{5,4},{6,7},{7,6},{8,9},{9,8},{10,11... | collective-permute-start | bytes 4718600 | tf_op jit(solution)/shard_map/ppermute | solution.py:474
  71.9 13.3 %rhs_0.1 = f32[4,6,64,256]{3,2,1,0:T(8,128)} custom-call(f32[8]{0:T(128)} %inv_dx.4, f32[64,1]{1,0:T(8,128)} %copy.21.inv_dr, f32[64,1]{1,0:T(8,128)} %copy.22.inv_rt, f32[3,8,64,1024]{3,2,1,0:T(8,128)} %velocity.11, f32[8,64,1024]{2,1,0:T(8,128)} %viscosity.10, f32[8,8,1024]{2,1,0:T(8,128)} %copy-done.8, f32[8,8,1024]{2,1,0:T(8,128)} %copy-done.7, ...), custom_call_target="tpu_custom_call" | custom-call | flops 1024 | bytes 1024 | tf_op jit(solution)/shard_map/rhs_0/pallas_call | solution.py:173
  85.3 3.4 %all-to-all-done.1.own_ref = f32[4,6,64,256]{3,2,1,0:T(8,128)} async-done(((f32[4,6,64,256]{3,2,1,0:T(8,128)}), f32[4,6,64,256]{3,2,1,0:T(8,128)}, u32[]{:S(2)}, u32[]{:S(2)}) %all-to-all-start.1) | async-done | bytes 1572896 | tf_op jit(solution)/shard_map/all_to_all | solution.py:469
  88.7 3.6 %all-to-all-start.2 = ((f32[4,6,64,256]{3,2,1,0:T(8,128)}), f32[4,6,64,256]{3,2,1,0:T(8,128)S(1)}, u32[]{:S(2)}, u32[]{:S(2)}) async-start(f32[4,6,64,256]{3,2,1,0:T(8,128)} %rhs_0.1), calls=%async_computation.2 | async-start | bytes 3145728 | tf_op jit(solution)/shard_map/all_to_all | solution.py:469
  92.3 4.2 %collective-permute-start.6 = (f32[4,6,64,256]{3,2,1,0:T(8,128)}, f32[4,6,64,256]{3,2,1,0:T(8,128)}, u32[]{:S(2)}, u32[]{:S(2)}) collective-permute-start(f32[4,6,64,256]{3,2,1,0:T(8,128)} %all-to-all-done.1.own_ref), channel_id=1, source_target_pairs={{0,1},{1,0},{2,3},{3,2},{4,5},{5,4},{6,7},{7,6},{8,9},{9,8},{10,11... | collective-permute-start | bytes 4718600 | tf_op jit(solution)/shard_map/ppermute | solution.py:474
  96.5 13.3 %rhs_6.1 = f32[4,6,64,256]{3,2,1,0:T(8,128)} custom-call(f32[8]{0:T(128)} %inv_dx.4, f32[64,1]{1,0:T(8,128)} %copy.21.inv_dr, f32[64,1]{1,0:T(8,128)} %copy.22.inv_rt, f32[3,8,64,1024]{3,2,1,0:T(8,128)} %velocity.11, f32[8,64,1024]{2,1,0:T(8,128)} %viscosity.10, f32[8,8,1024]{2,1,0:T(8,128)} %copy-done.8, f32[8,8,1024]{2,1,0:T(8,128)} %copy-done.7, ...), custom_call_target="tpu_custom_call" | custom-call | flops 1024 | bytes 1024 | tf_op jit(solution)/shard_map/rhs_6/pallas_call | solution.py:173
  109.8 4.0 %radial.4 = f32[4,6,64,256]{3,2,1,0:T(8,128)} custom-call(bf16[256,512]{1,0:T(8,128)(2,1)} %get-tuple-element.50.r_hi, bf16[256,512]{1,0:T(8,128)(2,1)} %get-tuple-element.51.r_lo, f32[4,6,64,256]{3,2,1,0:T(8,128)} %copy-done.5, f32[4,6,64,256]{3,2,1,0:T(8,128)} %collective-permute-done.4.rest_0_), custom_call_target="tpu_custom_call" | custom-call | flops 1024 | bytes 1024 | tf_op jit(solution)/shard_map/radial/pallas_call | solution.py:257
  114.0 4.6 %all-to-all-start.3 = ((f32[4,6,64,256]{3,2,1,0:T(8,128)}), f32[4,6,64,256]{3,2,1,0:T(8,128)}, u32[]{:S(2)}, u32[]{:S(2)}) async-start(f32[4,6,64,256]{3,2,1,0:T(8,128)} %rhs_6.1), calls=%async_computation.3 | async-start | bytes 3145728 | tf_op jit(solution)/shard_map/all_to_all | solution.py:469
  118.6 20.9 %collective-permute-done.6.rest_0_ = f32[4,6,64,256]{3,2,1,0:T(8,128)} collective-permute-done((f32[4,6,64,256]{3,2,1,0:T(8,128)}, f32[4,6,64,256]{3,2,1,0:T(8,128)}, u32[]{:S(2)}, u32[]{:S(2)}) %collective-permute-start.6) | collective-permute-done | bytes 1572896 | tf_op jit(solution)/shard_map/ppermute | solution.py:474
  140.2 4.3 %all-to-all-start.4 = ((f32[4,6,64,256]{3,2,1,0:T(8,128)}), f32[4,6,64,256]{3,2,1,0:T(8,128)S(1)}, u32[]{:S(2)}, u32[]{:S(2)}) async-start(f32[4,6,64,256]{3,2,1,0:T(8,128)} %radial.4), calls=%async_computation.4 | async-start | bytes 3145728 | tf_op jit(solution)/shard_map/all_to_all | solution.py:469
  144.5 3.9 %collective-permute-start.5 = (f32[4,6,64,128]{3,2,1,0:T(8,128)S(1)}, f32[4,6,64,128]{3,2,1,0:T(8,128)}, u32[]{:S(2)}, u32[]{:S(2)}) collective-permute-start(f32[4,6,64,128]{3,2,1,0:T(8,128)S(1)} %constant_dynamic-slice_fusion), channel_id=1, source_target_pairs={{0,1},{1,0},{2,3},{3,2},{4,5},{5,4},{6,7},{7,6},{8,9},{9,8},{10,11... | collective-permute-start | bytes 2359304 | tf_op jit(solution)/shard_map/ppermute | solution.py:474
  148.5 4.0 %radial.3 = f32[4,6,64,256]{3,2,1,0:T(8,128)} custom-call(bf16[256,512]{1,0:T(8,128)(2,1)} %get-tuple-element.50.r_hi, bf16[256,512]{1,0:T(8,128)(2,1)} %get-tuple-element.51.r_lo, f32[4,6,64,256]{3,2,1,0:T(8,128)} %all-to-all-done.1.own_ref, f32[4,6,64,256]{3,2,1,0:T(8,128)} %collective-permute-done.6.rest_0_), custom_call_target="tpu_custom_call" | custom-call | flops 1024 | bytes 1024 | tf_op jit(solution)/shard_map/radial/pallas_call | solution.py:257
  152.5 14.2 %collective-permute-done.5.other_ref = f32[4,6,64,128]{3,2,1,0:T(8,128)} collective-permute-done((f32[4,6,64,128]{3,2,1,0:T(8,128)S(1)}, f32[4,6,64,128]{3,2,1,0:T(8,128)}, u32[]{:S(2)}, u32[]{:S(2)}) %collective-permute-start.5) | collective-permute-done | bytes 786464 | tf_op jit(solution)/shard_map/ppermute | solution.py:474
  166.7 1.2 copy-done.6
  167.9 4.5 %all-to-all-start.5 = ((f32[4,6,64,256]{3,2,1,0:T(8,128)}), f32[4,6,64,256]{3,2,1,0:T(8,128)S(1)}, u32[]{:S(2)}, u32[]{:S(2)}) async-start(f32[4,6,64,256]{3,2,1,0:T(8,128)} %radial.3), calls=%async_computation.5 | async-start | bytes 3145728 | tf_op jit(solution)/shard_map/all_to_all | solution.py:469
  172.4 3.2 %collective-permute-start.8 = (f32[4,6,64,256]{3,2,1,0:T(8,128)}, f32[4,6,64,256]{3,2,1,0:T(8,128)}, u32[]{:S(2)}, u32[]{:S(2)}) collective-permute-start(f32[4,6,64,256]{3,2,1,0:T(8,128)} %all-to-all-done.3.own_ref), channel_id=1, source_target_pairs={{0,1},{1,0},{2,3},{3,2},{4,5},{5,4},{6,7},{7,6},{8,9},{9,8},{10,11... | collective-permute-start | bytes 4718600 | tf_op jit(solution)/shard_map/ppermute | solution.py:474
  175.7 4.5 %radial_both.1 = f32[4,2,6,64,128]{4,3,2,1,0:T(8,128)} custom-call(s32[1]{0:T(128)} %bitcast.side_ref, bf16[256,512]{1,0:T(8,128)(2,1)} %get-tuple-element.50.r_hi, bf16[256,512]{1,0:T(8,128)(2,1)} %get-tuple-element.51.r_lo, bf16[256,512]{1,0:T(8,128)(2,1)} %get-tuple-element.52.f_hi, bf16[256,512]{1,0:T(8,128)(2,1)} %get-tuple-element.53.f_lo, ...), custom_call_target="tpu_custom_call" | custom-call | flops 1024 | bytes 1024 | tf_op jit(solution)/shard_map/radial_both/pallas_call | solution.py:296
  180.1 12.8 %all-to-all-done.5.x_ref = f32[4,6,64,256]{3,2,1,0:T(8,128)S(1)} async-done(((f32[4,6,64,256]{3,2,1,0:T(8,128)}), f32[4,6,64,256]{3,2,1,0:T(8,128)S(1)}, u32[]{:S(2)}, u32[]{:S(2)}) %all-to-all-start.5) | async-done | bytes 1572896 | tf_op jit(solution)/shard_map/all_to_all | solution.py:469
  192.9 1.2 copy-done.3
  194.1 3.6 %all-to-all-start.6 = ((f32[4,2,6,64,128]{4,3,2,1,0:T(8,128)}), f32[4,2,6,64,128]{4,3,2,1,0:T(8,128)S(1)}, u32[]{:S(2)}, u32[]{:S(2)}) async-start(f32[4,2,6,64,128]{4,3,2,1,0:T(8,128)} %radial_both.1), calls=%async_computation.6 | async-start | bytes 3145728 | tf_op jit(solution)/shard_map/all_to_all | solution.py:469
  197.7 12.2 %collective-permute-done.8.rest_0_ = f32[4,6,64,256]{3,2,1,0:T(8,128)} collective-permute-done((f32[4,6,64,256]{3,2,1,0:T(8,128)}, f32[4,6,64,256]{3,2,1,0:T(8,128)}, u32[]{:S(2)}, u32[]{:S(2)}) %collective-permute-start.8) | collective-permute-done | bytes 1572896 | tf_op jit(solution)/shard_map/ppermute | solution.py:474
  209.9 4.0 %radial.5 = f32[4,6,64,256]{3,2,1,0:T(8,128)} custom-call(bf16[256,512]{1,0:T(8,128)(2,1)} %get-tuple-element.50.r_hi, bf16[256,512]{1,0:T(8,128)(2,1)} %get-tuple-element.51.r_lo, f32[4,6,64,256]{3,2,1,0:T(8,128)} %all-to-all-done.3.own_ref, f32[4,6,64,256]{3,2,1,0:T(8,128)} %collective-permute-done.8.rest_0_), custom_call_target="tpu_custom_call" | custom-call | flops 1024 | bytes 1024 | tf_op jit(solution)/shard_map/radial/pallas_call | solution.py:257
  213.9 3.4 %all-to-all-done.6.near_ref = f32[4,2,6,64,128]{4,3,2,1,0:T(8,128)S(1)} async-done(((f32[4,2,6,64,128]{4,3,2,1,0:T(8,128)}), f32[4,2,6,64,128]{4,3,2,1,0:T(8,128)S(1)}, u32[]{:S(2)}, u32[]{:S(2)}) %all-to-all-start.6) | async-done | bytes 1572896 | tf_op jit(solution)/shard_map/all_to_all | solution.py:469
  217.4 3.6 %all-to-all-start.7 = ((f32[4,6,64,256]{3,2,1,0:T(8,128)}), f32[4,6,64,256]{3,2,1,0:T(8,128)S(1)}, u32[]{:S(2)}, u32[]{:S(2)}) async-start(f32[4,6,64,256]{3,2,1,0:T(8,128)} %radial.5), calls=%async_computation.7 | async-start | bytes 3145728 | tf_op jit(solution)/shard_map/all_to_all | solution.py:469
  220.9 0.9 slice_bitcast_fusion
  221.9 2.5 %collective-permute-start.7 = (f32[4,6,64,128]{3,2,1,0:T(8,128)}, f32[4,6,64,128]{3,2,1,0:T(8,128)S(1)}, u32[]{:S(2)}, u32[]{:S(2)}) collective-permute-start(f32[4,6,64,128]{3,2,1,0:T(8,128)} %slice_bitcast_fusion), channel_id=1, source_target_pairs={{0,1},{1,0},{2,3},{3,2},{4,5},{5,4},{6,7},{7,6},{8,9},{9,8},{10,11... | collective-permute-start | bytes 2359304 | tf_op jit(solution)/shard_map/ppermute | solution.py:474
  224.4 2.3 place.3.rest_0_
  226.7 2.3 place.4.rest_0_
  229.0 10.7 %all-to-all-done.7.x_ref = f32[4,6,64,256]{3,2,1,0:T(8,128)S(1)} async-done(((f32[4,6,64,256]{3,2,1,0:T(8,128)}), f32[4,6,64,256]{3,2,1,0:T(8,128)S(1)}, u32[]{:S(2)}, u32[]{:S(2)}) %all-to-all-start.7) | async-done | bytes 1572896 | tf_op jit(solution)/shard_map/all_to_all | solution.py:469
  239.7 1.1 copy-done.4
  240.8 2.3 place.5._
  243.2 0.9 copy-done.9
  244.0 2.3 weave.1
  (30 shorter events, 1.6 us)
Async XLA Ops:
  2.5 16.5 %collective-permute-start.1 = (f32[8,8,1024]{2,1,0:T(8,128)}, f32[8,8,1024]{2,1,0:T(8,128)S(1)}, u32[]{:S(2)}, u32[]{:S(2)}) collective-permute-start(f32[8,8,1024]{2,1,0:T(8,128)} %get-tuple-element.43), channel_id=1, source_target_pairs={{1,0},{2,1},{3,2},{4,3},{5,4},{6,5},{7,6},{9,8},{10,9},{11,10},{12... | collective-permute-start | bytes 786440 | tf_op jit(solution)/shard_map/ppermute | solution.py:457
  3.8 16.3 %collective-permute-start = (f32[8,8,1024]{2,1,0:T(8,128)}, f32[8,8,1024]{2,1,0:T(8,128)S(1)}, u32[]{:S(2)}, u32[]{:S(2)}) collective-permute-start(f32[8,8,1024]{2,1,0:T(8,128)} %get-tuple-element.39), channel_id=1, source_target_pairs={{0,1},{1,2},{2,3},{3,4},{4,5},{5,6},{6,7},{8,9},{9,10},{10,11},{11... | collective-permute-start | bytes 786440 | tf_op jit(solution)/shard_map/ppermute | solution.py:456
  13.7 9.7 %copy-start.10 = (f32[64]{0:T(128)S(1)}, f32[64]{0:T(128)}, u32[]{:S(2)}) copy-start(f32[64]{0:T(128)} %param.10) | copy-start | bytes 772
  13.7 10.4 %copy-start.11 = (f32[64]{0:T(128)S(1)}, f32[64]{0:T(128)}, u32[]{:S(2)}) copy-start(f32[64]{0:T(128)} %param.11) | copy-start | bytes 772
  19.0 5.8 %copy-start.7 = (f32[8,8,1024]{2,1,0:T(8,128)}, f32[8,8,1024]{2,1,0:T(8,128)S(1)}, u32[]{:S(2)}) copy-start(f32[8,8,1024]{2,1,0:T(8,128)S(1)} %collective-permute-done.1.rad_hi) | copy-start | bytes 786436
  20.1 4.7 %copy-start.8 = (f32[8,8,1024]{2,1,0:T(8,128)}, f32[8,8,1024]{2,1,0:T(8,128)S(1)}, u32[]{:S(2)}) copy-start(f32[8,8,1024]{2,1,0:T(8,128)S(1)} %collective-permute-done.rad_lo) | copy-start | bytes 786436
  20.1 37.4 %collective-permute-start.2 = (f32[7,64,1024]{2,1,0:T(8,128)}, f32[7,64,1024]{2,1,0:T(8,128)S(1)}, u32[]{:S(2)}, u32[]{:S(2)}) collective-permute-start(f32[7,64,1024]{2,1,0:T(8,128)} %get-tuple-element.56), channel_id=1, source_target_pairs={{0,8},{8,16},{16,24},{24,32},{32,40},{40,48},{48,56},{56,64},{64,7... | collective-permute-start | bytes 5505032 | tf_op jit(solution)/shard_map/ppermute | solution.py:464
  22.1 35.4 %collective-permute-start.3 = (f32[7,64,1024]{2,1,0:T(8,128)}, f32[7,64,1024]{2,1,0:T(8,128)}, u32[]{:S(2)}, u32[]{:S(2)}) collective-permute-start(f32[7,64,1024]{2,1,0:T(8,128)} %get-tuple-element.57), channel_id=1, source_target_pairs={{8,0},{16,8},{24,16},{32,24},{40,32},{48,40},{56,48},{64,56},{72,6... | collective-permute-start | bytes 5505032 | tf_op jit(solution)/shard_map/ppermute | solution.py:465
  37.8 25.7 %all-to-all-start = ((f32[4,6,64,256]{3,2,1,0:T(8,128)}), f32[4,6,64,256]{3,2,1,0:T(8,128)S(1)}, u32[]{:S(2)}, u32[]{:S(2)}) async-start(f32[4,6,64,256]{3,2,1,0:T(8,128)} %rhs_2.1), calls=%async_computation | async-start | bytes 3145728 | tf_op jit(solution)/shard_map/all_to_all | solution.py:469
  57.5 6.0 %copy-start.2 = (f32[7,64,1024]{2,1,0:T(8,128)}, f32[7,64,1024]{2,1,0:T(8,128)S(1)}, u32[]{:S(2)}) copy-start(f32[7,64,1024]{2,1,0:T(8,128)S(1)} %collective-permute-done.2.rest_0_) | copy-start | bytes 5505028
  63.5 21.8 %copy-start.5 = (f32[4,6,64,256]{3,2,1,0:T(8,128)}, f32[4,6,64,256]{3,2,1,0:T(8,128)S(1)}, u32[]{:S(2)}) copy-start(f32[4,6,64,256]{3,2,1,0:T(8,128)S(1)} %all-to-all-done.own_ref) | copy-start | bytes 4718596
  63.5 25.2 %all-to-all-start.1 = ((f32[4,6,64,256]{3,2,1,0:T(8,128)}), f32[4,6,64,256]{3,2,1,0:T(8,128)}, u32[]{:S(2)}, u32[]{:S(2)}) async-start(f32[4,6,64,256]{3,2,1,0:T(8,128)} %rhs_4.1), calls=%async_computation.1 | async-start | bytes 3145728 | tf_op jit(solution)/shard_map/all_to_all | solution.py:469
  67.9 41.9 %collective-permute-start.4 = (f32[4,6,64,256]{3,2,1,0:T(8,128)S(1)}, f32[4,6,64,256]{3,2,1,0:T(8,128)}, u32[]{:S(2)}, u32[]{:S(2)}) collective-permute-start(f32[4,6,64,256]{3,2,1,0:T(8,128)S(1)} %all-to-all-done.own_ref), channel_id=1, source_target_pairs={{0,1},{1,0},{2,3},{3,2},{4,5},{5,4},{6,7},{7,6},{8,9},{9,8},{10,11... | collective-permute-start | bytes 4718600 | tf_op jit(solution)/shard_map/ppermute | solution.py:474
  88.7 25.2 %all-to-all-start.2 = ((f32[4,6,64,256]{3,2,1,0:T(8,128)}), f32[4,6,64,256]{3,2,1,0:T(8,128)S(1)}, u32[]{:S(2)}, u32[]{:S(2)}) async-start(f32[4,6,64,256]{3,2,1,0:T(8,128)} %rhs_0.1), calls=%async_computation.2 | async-start | bytes 3145728 | tf_op jit(solution)/shard_map/all_to_all | solution.py:469
  92.3 47.2 %collective-permute-start.6 = (f32[4,6,64,256]{3,2,1,0:T(8,128)}, f32[4,6,64,256]{3,2,1,0:T(8,128)}, u32[]{:S(2)}, u32[]{:S(2)}) collective-permute-start(f32[4,6,64,256]{3,2,1,0:T(8,128)} %all-to-all-done.1.own_ref), channel_id=1, source_target_pairs={{0,1},{1,0},{2,3},{3,2},{4,5},{5,4},{6,7},{7,6},{8,9},{9,8},{10,11... | collective-permute-start | bytes 4718600 | tf_op jit(solution)/shard_map/ppermute | solution.py:474
  114.0 30.5 %copy-start = (f32[4,6,64,256]{3,2,1,0:T(8,128)}, f32[4,6,64,256]{3,2,1,0:T(8,128)S(1)}, u32[]{:S(2)}) copy-start(f32[4,6,64,256]{3,2,1,0:T(8,128)S(1)} %all-to-all-done.2.own_ref) | copy-start | bytes 4718596
  114.0 26.2 %all-to-all-start.3 = ((f32[4,6,64,256]{3,2,1,0:T(8,128)}), f32[4,6,64,256]{3,2,1,0:T(8,128)}, u32[]{:S(2)}, u32[]{:S(2)}) async-start(f32[4,6,64,256]{3,2,1,0:T(8,128)} %rhs_6.1), calls=%async_computation.3 | async-start | bytes 3145728 | tf_op jit(solution)/shard_map/all_to_all | solution.py:469
  140.2 26.5 %all-to-all-start.4 = ((f32[4,6,64,256]{3,2,1,0:T(8,128)}), f32[4,6,64,256]{3,2,1,0:T(8,128)S(1)}, u32[]{:S(2)}, u32[]{:S(2)}) async-start(f32[4,6,64,256]{3,2,1,0:T(8,128)} %radial.4), calls=%async_computation.4 | async-start | bytes 3145728 | tf_op jit(solution)/shard_map/all_to_all | solution.py:469
  144.5 22.2 %collective-permute-start.5 = (f32[4,6,64,128]{3,2,1,0:T(8,128)S(1)}, f32[4,6,64,128]{3,2,1,0:T(8,128)}, u32[]{:S(2)}, u32[]{:S(2)}) collective-permute-start(f32[4,6,64,128]{3,2,1,0:T(8,128)S(1)} %constant_dynamic-slice_fusion), channel_id=1, source_target_pairs={{0,1},{1,0},{2,3},{3,2},{4,5},{5,4},{6,7},{7,6},{8,9},{9,8},{10,11... | collective-permute-start | bytes 2359304 | tf_op jit(solution)/shard_map/ppermute | solution.py:474
  166.7 1.2 copy-start.6
  167.9 25.1 %all-to-all-start.5 = ((f32[4,6,64,256]{3,2,1,0:T(8,128)}), f32[4,6,64,256]{3,2,1,0:T(8,128)S(1)}, u32[]{:S(2)}, u32[]{:S(2)}) async-start(f32[4,6,64,256]{3,2,1,0:T(8,128)} %radial.3), calls=%async_computation.5 | async-start | bytes 3145728 | tf_op jit(solution)/shard_map/all_to_all | solution.py:469
  172.4 37.5 %collective-permute-start.8 = (f32[4,6,64,256]{3,2,1,0:T(8,128)}, f32[4,6,64,256]{3,2,1,0:T(8,128)}, u32[]{:S(2)}, u32[]{:S(2)}) collective-permute-start(f32[4,6,64,256]{3,2,1,0:T(8,128)} %all-to-all-done.3.own_ref), channel_id=1, source_target_pairs={{0,1},{1,0},{2,3},{3,2},{4,5},{5,4},{6,7},{7,6},{8,9},{9,8},{10,11... | collective-permute-start | bytes 4718600 | tf_op jit(solution)/shard_map/ppermute | solution.py:474
  192.9 1.2 copy-start.3
  194.1 23.3 %all-to-all-start.6 = ((f32[4,2,6,64,128]{4,3,2,1,0:T(8,128)}), f32[4,2,6,64,128]{4,3,2,1,0:T(8,128)S(1)}, u32[]{:S(2)}, u32[]{:S(2)}) async-start(f32[4,2,6,64,128]{4,3,2,1,0:T(8,128)} %radial_both.1), calls=%async_computation.6 | async-start | bytes 3145728 | tf_op jit(solution)/shard_map/all_to_all | solution.py:469
  217.4 3.6 %copy-start.1 = (f32[4,2,6,64,128]{4,3,2,1,0:T(8,128)}, f32[4,2,6,64,128]{4,3,2,1,0:T(8,128)S(1)}, u32[]{:S(2)}) copy-start(f32[4,2,6,64,128]{4,3,2,1,0:T(8,128)S(1)} %all-to-all-done.6.near_ref) | copy-start | bytes 4718596
  217.4 22.3 %all-to-all-start.7 = ((f32[4,6,64,256]{3,2,1,0:T(8,128)}), f32[4,6,64,256]{3,2,1,0:T(8,128)S(1)}, u32[]{:S(2)}, u32[]{:S(2)}) async-start(f32[4,6,64,256]{3,2,1,0:T(8,128)} %radial.5), calls=%async_computation.7 | async-start | bytes 3145728 | tf_op jit(solution)/shard_map/all_to_all | solution.py:469
  221.9 21.3 %collective-permute-start.7 = (f32[4,6,64,128]{3,2,1,0:T(8,128)}, f32[4,6,64,128]{3,2,1,0:T(8,128)S(1)}, u32[]{:S(2)}, u32[]{:S(2)}) collective-permute-start(f32[4,6,64,128]{3,2,1,0:T(8,128)} %slice_bitcast_fusion), channel_id=1, source_target_pairs={{0,1},{1,0},{2,3},{3,2},{4,5},{5,4},{6,7},{7,6},{8,9},{9,8},{10,11... | collective-permute-start | bytes 2359304 | tf_op jit(solution)/shard_map/ppermute | solution.py:474
  239.7 1.1 copy-start.4
  243.2 0.9 copy-start.9
